TPU v7x, 32 devices: a whole 2x2x4 slice. The times are simulated.
32 devices in a mesh: dp: 8 (over y, x, core), ctx: 4 (over z).
Axes of the slice: x: 2, y: 2, z: 4, core: 2. Of those that a mesh axis runs over, the one named last changes fastest.
Arguments:
- block_in: bfloat16 [8, 2048, 768], P('dp', 'ctx'), may hold values from -6 to 6
- out_grad: bfloat16 [8, 2048, 768], P('dp', 'ctx'), may hold values from -6 to 6
- lengths: int32 [8], P('dp'), may hold values from 128 to 2048, as said below
- ln1_gain: bfloat16 [768], P(('dp', 'ctx')), may hold values from 0.099609375 to 1.8984375
- ln1_bias: bfloat16 [768], P(('dp', 'ctx')), may hold values from -3 to 3
- qkv_weight: bfloat16 [768, 2304], P(('dp', 'ctx')), may hold values from -0.25 to 0.25
- qkv_bias: bfloat16 [2304], P(('dp', 'ctx')), may hold values from -3 to 3
- out_weight: bfloat16 [768, 768], P(('dp', 'ctx')), may hold values from -1.75 to 1.75
- out_bias: bfloat16 [768], P(('dp', 'ctx')), may hold values from -3 to 3
- ln2_gain: bfloat16 [768], P(('dp', 'ctx')), may hold values from 0.099609375 to 1.8984375
- ln2_bias: bfloat16 [768], P(('dp', 'ctx')), may hold values from -3 to 3
- fc1_weight: bfloat16 [768, 3072], P(('dp', 'ctx')), may hold values from -0.21875 to 0.21875
- fc1_bias: bfloat16 [3072], P(('dp', 'ctx')), may hold values from -3 to 3
- fc2_weight: bfloat16 [3072, 768], P(('dp', 'ctx')), may hold values from -0.109375 to 0.109375
- fc2_bias: bfloat16 [768], P(('dp', 'ctx')), may hold values from -3 to 3
Outputs:
- block_out: bfloat16 [8, 2048, 768], P('dp', 'ctx')
- input_grad: bfloat16 [8, 2048, 768], P('dp', 'ctx')
- ln1_gain_grad: float32 [768], P(('dp', 'ctx'))
- ln1_bias_grad: float32 [768], P(('dp', 'ctx'))
- qkv_weight_grad: float32 [768, 2304], P(('dp', 'ctx'))
- qkv_bias_grad: float32 [2304], P(('dp', 'ctx'))
- out_weight_grad: float32 [768, 768], P(('dp', 'ctx'))
- out_bias_grad: float32 [768], P(('dp', 'ctx'))
- ln2_gain_grad: float32 [768], P(('dp', 'ctx'))
- ln2_bias_grad: float32 [768], P(('dp', 'ctx'))
- fc1_weight_grad: float32 [768, 3072], P(('dp', 'ctx'))
- fc1_bias_grad: float32 [3072], P(('dp', 'ctx'))
- fc2_weight_grad: float32 [3072, 768], P(('dp', 'ctx'))
- fc2_bias_grad: float32 [768], P(('dp', 'ctx'))
- example_norms: float32 [8], P('dp')
Inputs may be any that keep to these rules, and one draw needn't show every extreme that they name: Example e holds real tokens at positions 0 to lengths[e] - 1 and padding after them; at least one example is 2048 long.
All inputs are finite; a program needn't handle non-finite values.
Results may differ from a plain program's by a relative error of at most 0.012.
The roundings to bfloat16 on the way count: a program that leaves them out, or rounds other values in their place, can miss the bound.
Values may be sent and summed in bfloat16 or wider, within the bound.
A program may use at most 96 MiB of HBM per device.

v0:
```python
import math

import jax
import jax.numpy as jnp
from jax import lax
from jax.sharding import PartitionSpec as P

D = 768
HEADS = 12
HEAD_DIM = 64
ROT = 16


eps_norm = 1e-05
neg_big = -1e30
score_block = 512
root_two = math.sqrt(2.0)
root_two_pi = math.sqrt(2.0 * math.pi)


def norm_parts(values, norm_gain, norm_shift):
    row_mean = jnp.mean(values, axis=-1, keepdims=True)
    centered = values - row_mean
    row_var = jnp.mean(centered * centered, axis=-1, keepdims=True)
    inverse = lax.rsqrt(row_var + eps_norm)
    normed = centered * inverse
    return (normed, inverse, normed * norm_gain + norm_shift)


def norm_back(grad_out, normed, inverse, norm_gain):
    scaled = grad_out * norm_gain
    return inverse * (
        scaled
        - jnp.mean(scaled, axis=-1, keepdims=True)
        - normed * jnp.mean(scaled * normed, axis=-1, keepdims=True)
    )


def rotary_tables(positions):
    freq_index = jnp.arange(ROT // 2, dtype=jnp.float32)
    inv_freqs = jnp.exp(freq_index * (-2.0 * math.log(10000.0) / ROT))
    angles = positions.astype(jnp.float32)[:, None] * inv_freqs[None, :]
    return (jnp.cos(angles)[:, None, :], jnp.sin(angles)[:, None, :])


def turn(values, cosine, sine_table):
    half_width = cosine.shape[-1]
    first_half = values[..., :half_width]
    second_half = values[..., half_width : 2 * half_width]
    return jnp.concatenate(
        [
            first_half * cosine - second_half * sine_table,
            second_half * cosine + first_half * sine_table,
            values[..., 2 * half_width :],
        ],
        axis=-1,
    )


def gelu_parts(pre_act):
    normal_cdf = 0.5 * (1.0 + lax.erf(pre_act / root_two))
    return (
        pre_act * normal_cdf,
        normal_cdf + pre_act * jnp.exp(-0.5 * pre_act * pre_act) / root_two_pi,
    )


def to_blocks(stacked, block_width):
    shaped = stacked.reshape(
        stacked.shape[0], stacked.shape[1] // block_width, block_width, HEADS, HEAD_DIM
    )
    return jnp.moveaxis(shaped, 1, 0)


def from_blocks(stacked):
    moved = jnp.moveaxis(stacked, 0, 1)
    return moved.reshape(moved.shape[0], moved.shape[1] * moved.shape[2], HEADS * HEAD_DIM)


def masked_scores(queries, key_block, block_start, query_pos, lengths, score_scale):
    raw_scores = (
        jnp.einsum("srhd,skhd->shrk", queries, key_block, preferred_element_type=jnp.float32)
        * score_scale
    )
    key_pos = block_start + jnp.arange(key_block.shape[1], dtype=jnp.int32)
    valid = (key_pos[None, None, :] <= query_pos[None, :, None]) & (
        key_pos[None, None, :] < lengths[:, None, None]
    )
    return jnp.where(valid[:, None], raw_scores, neg_big)


def attend(queries, keys_all, values_all, query_pos, lengths, score_scale):
    block_width = min(score_block, keys_all.shape[1])
    key_blocks = to_blocks(keys_all, block_width)
    value_blocks = to_blocks(values_all, block_width)
    starts = jnp.arange(key_blocks.shape[0], dtype=jnp.int32) * block_width
    row_shape = (queries.shape[0], HEADS, queries.shape[1])

    def first_pass(running, inputs):
        row_max, row_total = running
        key_block, block_start = inputs
        scores = masked_scores(queries, key_block, block_start, query_pos, lengths, score_scale)
        new_max = jnp.maximum(row_max, jnp.max(scores, axis=-1))
        row_total = row_total * jnp.exp(row_max - new_max) + jnp.sum(
            jnp.exp(scores - new_max[..., None]), axis=-1
        )
        return ((new_max, row_total), None)

    start_state = (jnp.full(row_shape, neg_big, jnp.float32), jnp.zeros(row_shape, jnp.float32))
    (row_max, row_total), unused = lax.scan(first_pass, start_state, (key_blocks, starts))
    log_total = row_max + jnp.log(row_total)

    def second_pass(summed, inputs):
        key_block, value_block, block_start = inputs
        scores = masked_scores(queries, key_block, block_start, query_pos, lengths, score_scale)
        weights = jnp.exp(scores - log_total[..., None]).astype(jnp.bfloat16)
        return (
            summed
            + jnp.einsum(
                "shrk,skhd->srhd", weights, value_block, preferred_element_type=jnp.float32
            ),
            None,
        )

    attended, unused = lax.scan(
        second_pass, jnp.zeros(queries.shape, jnp.float32), (key_blocks, value_blocks, starts)
    )
    return (attended, log_total)


def attend_back(
    queries, keys_all, values_all, grad_out, log_total, query_pos, lengths, score_scale
):
    block_width = min(score_block, keys_all.shape[1])
    key_blocks = to_blocks(keys_all, block_width)
    value_blocks = to_blocks(values_all, block_width)
    starts = jnp.arange(key_blocks.shape[0], dtype=jnp.int32) * block_width

    def weights_of(key_block, value_block, block_start):
        scores = masked_scores(queries, key_block, block_start, query_pos, lengths, score_scale)
        weights = jnp.exp(scores - log_total[..., None])
        grad_weights = jnp.einsum(
            "srhd,skhd->shrk", grad_out, value_block, preferred_element_type=jnp.float32
        )
        return (weights, grad_weights)

    def delta_pass(row_delta, inputs):
        weights, grad_weights = weights_of(inputs[0], inputs[1], inputs[2])
        return (row_delta + jnp.sum(weights * grad_weights, axis=-1), None)

    row_delta, unused = lax.scan(
        delta_pass, jnp.zeros(log_total.shape, jnp.float32), (key_blocks, value_blocks, starts)
    )

    def grad_pass(grad_query, inputs):
        key_block = inputs[0]
        weights, grad_weights = weights_of(inputs[0], inputs[1], inputs[2])
        grad_scores = (weights * (grad_weights - row_delta[..., None])).astype(jnp.bfloat16)
        grad_query = grad_query + jnp.einsum(
            "shrk,skhd->srhd", grad_scores, key_block, preferred_element_type=jnp.float32
        )
        grad_key = jnp.einsum(
            "shrk,srhd->skhd", grad_scores, queries, preferred_element_type=jnp.float32
        )
        grad_value = jnp.einsum(
            "shrk,srhd->skhd",
            weights.astype(jnp.bfloat16),
            grad_out,
            preferred_element_type=jnp.float32,
        )
        return (grad_query, (grad_key, grad_value))

    grad_query, (grad_keys, grad_values) = lax.scan(
        grad_pass, jnp.zeros(queries.shape, jnp.float32), (key_blocks, value_blocks, starts)
    )
    return (
        grad_query * score_scale,
        from_blocks(grad_keys) * score_scale,
        from_blocks(grad_values),
    )


def project(left_side, right_side):
    return jnp.einsum("srd,df->srf", left_side, right_side, preferred_element_type=jnp.float32)


def project_back(left_side, right_side):
    return jnp.einsum("srf,df->srd", left_side, right_side, preferred_element_type=jnp.float32)


def local(
    block_in,
    out_grad,
    lengths,
    ln1_gain,
    ln1_bias,
    qkv_weight,
    qkv_bias,
    out_weight,
    out_bias,
    ln2_gain,
    ln2_bias,
    fc1_weight,
    fc1_bias,
    fc2_weight,
    fc2_bias,
):
    params = (
        ln1_gain,
        ln1_bias,
        qkv_weight,
        qkv_bias,
        out_weight,
        out_bias,
        ln2_gain,
        ln2_bias,
        fc1_weight,
        fc1_bias,
        fc2_weight,
        fc2_bias,
    )
    seqs_here, local_rows = (block_in.shape[0], block_in.shape[1])
    ctx_size = lax.axis_size("ctx")
    dp_size = lax.axis_size("dp")
    ctx_place = lax.axis_index("ctx")
    score_scale = HEAD_DIM ** (-0.5)
    query_pos = ctx_place * local_rows + jnp.arange(local_rows, dtype=jnp.int32)
    cosine, sine_table = rotary_tables(query_pos)
    heads_shape = (seqs_here, local_rows, HEADS, HEAD_DIM)
    flat_shape = (seqs_here, local_rows, D)
    gathered = (
        lax.all_gather(ln1_gain, ("dp", "ctx"), axis=0, tiled=True),
        lax.all_gather(ln1_bias, ("dp", "ctx"), axis=0, tiled=True),
        lax.all_gather(qkv_weight, ("dp", "ctx"), axis=0, tiled=True),
        lax.all_gather(qkv_bias, ("dp", "ctx"), axis=0, tiled=True),
        lax.all_gather(out_weight, ("dp", "ctx"), axis=0, tiled=True),
        lax.all_gather(out_bias, ("dp", "ctx"), axis=0, tiled=True),
        lax.all_gather(ln2_gain, ("dp", "ctx"), axis=0, tiled=True),
        lax.all_gather(ln2_bias, ("dp", "ctx"), axis=0, tiled=True),
        lax.all_gather(fc1_weight, ("dp", "ctx"), axis=0, tiled=True),
        lax.all_gather(fc1_bias, ("dp", "ctx"), axis=0, tiled=True),
        lax.all_gather(fc2_weight, ("dp", "ctx"), axis=0, tiled=True),
        lax.all_gather(fc2_bias, ("dp", "ctx"), axis=0, tiled=True),
    )
    (
        gain_one,
        shift_one,
        w_qkv,
        b_qkv,
        w_out,
        b_out,
        gain_two,
        shift_two,
        w_up,
        b_up,
        w_down,
        b_down,
    ) = gathered
    block_rows = block_in.astype(jnp.float32)
    normed_one, inverse_one, attn_in = norm_parts(
        block_rows, gain_one.astype(jnp.float32), shift_one.astype(jnp.float32)
    )
    attn_in = attn_in.astype(jnp.bfloat16)
    qkv_all = project(attn_in, w_qkv) + b_qkv.astype(jnp.float32)
    queries = turn(qkv_all[..., :D].reshape(heads_shape), cosine, sine_table).astype(jnp.bfloat16)
    key_rows = (
        turn(qkv_all[..., D : 2 * D].reshape(heads_shape), cosine, sine_table)
        .astype(jnp.bfloat16)
        .reshape(flat_shape)
    )
    value_rows = qkv_all[..., 2 * D :].astype(jnp.bfloat16)
    keys_all, values_all = (
        lax.all_gather(key_rows, "ctx", axis=1, tiled=True),
        lax.all_gather(value_rows, "ctx", axis=1, tiled=True),
    )
    attended, log_total = attend(queries, keys_all, values_all, query_pos, lengths, score_scale)
    context = attended.reshape(flat_shape).astype(jnp.bfloat16)
    attn_out = project(context, w_out) + b_out.astype(jnp.float32)
    normed_two, inverse_two, mlp_in = norm_parts(
        block_rows, gain_two.astype(jnp.float32), shift_two.astype(jnp.float32)
    )
    mlp_in = mlp_in.astype(jnp.bfloat16)
    pre_act = project(mlp_in, w_up) + b_up.astype(jnp.float32)
    activated, slope = gelu_parts(pre_act)
    hidden = activated.astype(jnp.bfloat16)
    mlp_out = project(hidden, w_down) + b_down.astype(jnp.float32)
    block_out = (block_rows + attn_out + mlp_out).astype(jnp.bfloat16)
    gathered_back = (
        lax.all_gather(ln1_gain, ("dp", "ctx"), axis=0, tiled=True),
        lax.all_gather(ln1_bias, ("dp", "ctx"), axis=0, tiled=True),
        lax.all_gather(qkv_weight, ("dp", "ctx"), axis=0, tiled=True),
        lax.all_gather(qkv_bias, ("dp", "ctx"), axis=0, tiled=True),
        lax.all_gather(out_weight, ("dp", "ctx"), axis=0, tiled=True),
        lax.all_gather(out_bias, ("dp", "ctx"), axis=0, tiled=True),
        lax.all_gather(ln2_gain, ("dp", "ctx"), axis=0, tiled=True),
        lax.all_gather(ln2_bias, ("dp", "ctx"), axis=0, tiled=True),
        lax.all_gather(fc1_weight, ("dp", "ctx"), axis=0, tiled=True),
        lax.all_gather(fc1_bias, ("dp", "ctx"), axis=0, tiled=True),
        lax.all_gather(fc2_weight, ("dp", "ctx"), axis=0, tiled=True),
        lax.all_gather(fc2_bias, ("dp", "ctx"), axis=0, tiled=True),
    )
    keys_back, values_back = (
        lax.all_gather(key_rows, "ctx", axis=1, tiled=True),
        lax.all_gather(value_rows, "ctx", axis=1, tiled=True),
    )
    (
        gain_one,
        unused,
        w_qkv,
        unused,
        w_out,
        unused,
        gain_two,
        unused,
        w_up,
        unused,
        w_down,
        unused,
    ) = gathered_back
    live_rows = (query_pos[None, :] < lengths[:, None]).astype(jnp.float32)
    grad_rows = (out_grad.astype(jnp.float32) * live_rows[..., None]).astype(jnp.bfloat16)
    cotangent = grad_rows.astype(jnp.float32)
    grad_context = project_back(grad_rows, w_out).astype(jnp.bfloat16)
    grad_pre = (project_back(grad_rows, w_down) * slope).astype(jnp.bfloat16)
    grad_query, grad_keys, grad_values = attend_back(
        queries,
        keys_back,
        values_back,
        grad_context.reshape(heads_shape),
        log_total,
        query_pos,
        lengths,
        score_scale,
    )
    own_keys, own_values = (
        lax.psum_scatter(grad_keys, "ctx", scatter_dimension=1, tiled=True),
        lax.psum_scatter(grad_values, "ctx", scatter_dimension=1, tiled=True),
    )
    grad_qkv = jnp.concatenate(
        [
            turn(grad_query, cosine, -sine_table).reshape(flat_shape),
            turn(own_keys.reshape(heads_shape), cosine, -sine_table).reshape(flat_shape),
            own_values,
        ],
        axis=-1,
    ).astype(jnp.bfloat16)
    grad_attn_in = project_back(grad_qkv, w_qkv)
    grad_mlp_in = project_back(grad_pre, w_up)
    grad_input = (
        cotangent
        + norm_back(grad_attn_in, normed_one, inverse_one, gain_one.astype(jnp.float32))
        + norm_back(grad_mlp_in, normed_two, inverse_two, gain_two.astype(jnp.float32))
    )
    vector_terms = (
        jnp.sum(grad_attn_in * normed_one, axis=1),
        jnp.sum(grad_attn_in, axis=1),
        jnp.sum(grad_qkv.astype(jnp.float32), axis=1),
        jnp.sum(cotangent, axis=1),
        jnp.sum(grad_mlp_in * normed_two, axis=1),
        jnp.sum(grad_mlp_in, axis=1),
        jnp.sum(grad_pre.astype(jnp.float32), axis=1),
        jnp.sum(cotangent, axis=1),
    )
    vector_sizes = [term.shape[-1] for term in vector_terms]
    vector_starts = [sum(vector_sizes[:place]) for place in range(len(vector_sizes))]
    local_vectors = jnp.concatenate(vector_terms, axis=-1)
    matrix_pairs = (
        (attn_in, grad_qkv),
        (context, grad_rows),
        (mlp_in, grad_pre),
        (hidden, grad_rows),
    )
    per_example = [
        jnp.einsum("srd,srf->sdf", left_side, right_side, preferred_element_type=jnp.float32)
        for left_side, right_side in matrix_pairs
    ]
    sectioned = [
        matrix.reshape(
            seqs_here, dp_size, ctx_size, matrix.shape[1] // (dp_size * ctx_size), matrix.shape[2]
        )
        for matrix in per_example
    ]
    quarters = (
        lax.psum_scatter(sectioned[0], "ctx", scatter_dimension=2, tiled=True),
        lax.psum_scatter(sectioned[1], "ctx", scatter_dimension=2, tiled=True),
        lax.psum_scatter(sectioned[2], "ctx", scatter_dimension=2, tiled=True),
        lax.psum_scatter(sectioned[3], "ctx", scatter_dimension=2, tiled=True),
    )
    matrix_squares = sum((jnp.sum(quarter * quarter, axis=(1, 2, 3, 4)) for quarter in quarters))
    vector_totals, matrix_totals = lax.psum((local_vectors, matrix_squares), "ctx")
    example_norms = jnp.sqrt(matrix_totals + jnp.sum(vector_totals * vector_totals, axis=-1))
    mean_norm = lax.psum(jnp.sum(example_norms), "dp") / (seqs_here * dp_size)
    factors = mean_norm / jnp.maximum(example_norms, mean_norm)
    vec_parts = []
    for begin, extent in zip(vector_starts, vector_sizes):
        shaped = vector_totals[:, begin : begin + extent].reshape(
            seqs_here, dp_size, ctx_size, extent // (dp_size * ctx_size)
        )
        mine = lax.dynamic_slice_in_dim(shaped, ctx_place, 1, axis=2)
        vec_parts.append(jnp.sum(factors[:, None, None, None] * mine, axis=0))
    mat_parts = [
        jnp.sum(factors[:, None, None, None, None] * quarter, axis=0) for quarter in quarters
    ]
    results = (
        lax.psum_scatter(vec_parts[0], "dp", scatter_dimension=0, tiled=True),
        lax.psum_scatter(vec_parts[1], "dp", scatter_dimension=0, tiled=True),
        lax.psum_scatter(mat_parts[0], "dp", scatter_dimension=0, tiled=True),
        lax.psum_scatter(vec_parts[2], "dp", scatter_dimension=0, tiled=True),
        lax.psum_scatter(mat_parts[1], "dp", scatter_dimension=0, tiled=True),
        lax.psum_scatter(vec_parts[3], "dp", scatter_dimension=0, tiled=True),
        lax.psum_scatter(vec_parts[4], "dp", scatter_dimension=0, tiled=True),
        lax.psum_scatter(vec_parts[5], "dp", scatter_dimension=0, tiled=True),
        lax.psum_scatter(mat_parts[2], "dp", scatter_dimension=0, tiled=True),
        lax.psum_scatter(vec_parts[6], "dp", scatter_dimension=0, tiled=True),
        lax.psum_scatter(mat_parts[3], "dp", scatter_dimension=0, tiled=True),
        lax.psum_scatter(vec_parts[7], "dp", scatter_dimension=0, tiled=True),
    )
    shaped_results = [
        result.reshape(param_shard.shape) for result, param_shard in zip(results, params)
    ]
    return (
        block_out,
        grad_input.astype(jnp.bfloat16),
        shaped_results[0],
        shaped_results[1],
        shaped_results[2],
        shaped_results[3],
        shaped_results[4],
        shaped_results[5],
        shaped_results[6],
        shaped_results[7],
        shaped_results[8],
        shaped_results[9],
        shaped_results[10],
        shaped_results[11],
        example_norms,
    )


def solution(mesh):
    placed = (
        P("dp", "ctx", None),
        P("dp", "ctx", None),
        P("dp"),
        P(("dp", "ctx")),
        P(("dp", "ctx")),
        P(("dp", "ctx"), None),
        P(("dp", "ctx")),
        P(("dp", "ctx"), None),
        P(("dp", "ctx")),
        P(("dp", "ctx")),
        P(("dp", "ctx")),
        P(("dp", "ctx"), None),
        P(("dp", "ctx")),
        P(("dp", "ctx"), None),
        P(("dp", "ctx")),
    )
    return jax.shard_map(
        local,
        mesh=mesh,
        in_specs=placed,
        out_specs=(
            P("dp", "ctx", None),
            P("dp", "ctx", None),
            P(("dp", "ctx")),
            P(("dp", "ctx")),
            P(("dp", "ctx"), None),
            P(("dp", "ctx")),
            P(("dp", "ctx"), None),
            P(("dp", "ctx")),
            P(("dp", "ctx")),
            P(("dp", "ctx")),
            P(("dp", "ctx"), None),
            P(("dp", "ctx")),
            P(("dp", "ctx"), None),
            P(("dp", "ctx")),
            P("dp"),
        ),
        check_vma=False,
    )
```

profile of v0, /device:TPU:1, one launch (start us, length us, event | category | flops | bytes accessed | tf_op | source)
XLA Modules:
  0.0 2033.8 jit_solution(10436694236008981039)
XLA Ops:
  15.5 41.6 %all-reduce.23 = (bf16[768]{0:T(1024)(128)(2,1)}, bf16[768]{0:T(1024)(128)(2,1)}, bf16[3072]{0:T(1024)(128)(2,1)}, bf16[2304]{0:T(1024)(128)(2,1)S(1)}, bf16[768...) all-reduce(bf16[768]{0:T(1024)(128)(2,1)S(1)} %dynamic-update-slice, ...), channel_id=1, replica_groups=mesh['dp'=8,'ctx'=4] {'dp','ctx'}, use_global_device_ids=true, to_apply=%add.5 | all-reduce | flops 9984 | bytes 39936
  59.9 13.7 all-gather.7.cloned.1.call-done
  92.9 36.5 %all-gather.13.cloned.1.call-done = bf16[768,768]{1,0:T(8,128)(2,1)} async-done(((bf16[24,768]{1,0:T(8,128)(2,1)}), bf16[768,768]{1,0:T(8,128)(2,1)}) %all-gather.13.cloned.1.call-update) | async-done | bytes 1179664 | tf_op jit(solution)/shard_map/all_gather | solution.py:236
  134.8 58.7 %all-gather.9.cloned.1.call-done = bf16[1,2048,768]{2,1,0:T(8,128)(2,1)} async-done(((bf16[1,512,768]{2,1,0:T(8,128)(2,1)}), bf16[1,2048,768]{2,1,0:T(8,128)(2,1)}) %all-gather.9.cloned.1.call-update) | async-done | bytes 3145744 | tf_op jit(solution)/shard_map/all_gather | solution.py:274
  209.0 48.7 %all-gather.11.cloned.1.call-done = bf16[1,2048,768]{1,2,0:T(8,128)(2,1)} async-done(((bf16[1,512,768]{1,2,0:T(8,128)(2,1)}), bf16[1,2048,768]{1,2,0:T(8,128)(2,1)}) %all-gather.11.cloned.1.call-update) | async-done | bytes 3145744 | tf_op jit(solution)/shard_map/all_gather | solution.py:273
  268.1 34.6 %while.50 = (s32[]{:T(128)}, f32[1,12,512]{2,1,0:T(8,128)S(1)}, f32[1,12,512]{2,1,0:T(8,128)S(1)}, s32[4]{0:T(128)S(1)}, s32[1]{0:T(128)}, /*index=5*/bf16[4,1,5...) while((s32[]{:T(128)}, f32[1,12,512]{2,1,0:T(8,128)S(1)}, ...), condition=%wide.region_5.6_spmd.clone, body=%wide.region_2.5_spmd.clone.sunk | while | flops 425230336 | bytes 27853976 | solution.py:110
  302.7 43.6 %while.52 = (s32[]{:T(128)}, f32[1,12,512]{2,1,0:T(8,128)S(1)}, s32[4]{0:T(128)S(1)}, s32[1]{0:T(128)}, bf16[4,1,512,12,64]{2,4,3,1,0:T(8,128)(2,1)}, /*index=5*...) while((s32[]{:T(128)}, f32[1,12,512]{2,1,0:T(8,128)S(1)}, ...), condition=%wide.region_10.11_spmd.clone, body=%wide.region_8.10_spmd.clone.sunk | while | flops 821567488 | bytes 28968104 | solution.py:151
  346.3 253.9 %while.53 = (s32[]{:T(128)}, f32[1,512,12,64]{1,3,2,0:T(8,128)}, f32[4,1,512,12,64]{2,4,3,1,0:T(8,128)}, f32[4,1,512,12,64]{2,0,4,3,1:T(4,128)}, bf16[4,1,512,12...) while((s32[]{:T(128)}, f32[1,512,12,64]{1,3,2,0:T(8,128)}, ...), condition=%wide.region_12.13_spmd.clone, body=%wide.region_11.12_spmd.clone.sunk | while | flops 2046035968 | bytes 75580624 | solution.py:173
  378.6 30.9 %dynamic_update_slice.13 = f32[4,1,512,12,64]{2,0,4,3,1:T(4,128)} dynamic-update-slice(f32[4,1,512,12,64]{2,0,4,3,1:T(4,128)} %get-tuple-element.1027, f32[1,1,512,12,64]{2,0,4,3,1:T(1,128)S(1)} %copy.157, s32[]{:T(128)S(6)} %copy.193, s32[]{:T(128)} %constant.62.clone.1..sunk.3, s32[]{:T(128)} %constant.62.clone.1..sunk.3, s32[]{:T(128)} %constant.62.clone.1..sunk.3, s32[]{:T(128)} %constant.62.clone.1..sunk.3) | dynamic-update-slice | bytes 3145732 | tf_op jit(solution)/shard_map/while/body/jit(dynamic_update_index_in_dim)/dynamic_update_slice | solution.py:173
  442.1 30.9 %dynamic_update_slice.13 = f32[4,1,512,12,64]{2,0,4,3,1:T(4,128)} dynamic-update-slice(f32[4,1,512,12,64]{2,0,4,3,1:T(4,128)} %get-tuple-element.1027, f32[1,1,512,12,64]{2,0,4,3,1:T(1,128)S(1)} %copy.157, s32[]{:T(128)S(6)} %copy.193, s32[]{:T(128)} %constant.62.clone.1..sunk.3, s32[]{:T(128)} %constant.62.clone.1..sunk.3, s32[]{:T(128)} %constant.62.clone.1..sunk.3, s32[]{:T(128)} %constant.62.clone.1..sunk.3) | dynamic-update-slice | bytes 3145732 | tf_op jit(solution)/shard_map/while/body/jit(dynamic_update_index_in_dim)/dynamic_update_slice | solution.py:173
  505.4 30.9 %dynamic_update_slice.13 = f32[4,1,512,12,64]{2,0,4,3,1:T(4,128)} dynamic-update-slice(f32[4,1,512,12,64]{2,0,4,3,1:T(4,128)} %get-tuple-element.1027, f32[1,1,512,12,64]{2,0,4,3,1:T(1,128)S(1)} %copy.157, s32[]{:T(128)S(6)} %copy.193, s32[]{:T(128)} %constant.62.clone.1..sunk.3, s32[]{:T(128)} %constant.62.clone.1..sunk.3, s32[]{:T(128)} %constant.62.clone.1..sunk.3, s32[]{:T(128)} %constant.62.clone.1..sunk.3) | dynamic-update-slice | bytes 3145732 | tf_op jit(solution)/shard_map/while/body/jit(dynamic_update_index_in_dim)/dynamic_update_slice | solution.py:173
  568.9 30.9 %dynamic_update_slice.13 = f32[4,1,512,12,64]{2,0,4,3,1:T(4,128)} dynamic-update-slice(f32[4,1,512,12,64]{2,0,4,3,1:T(4,128)} %get-tuple-element.1027, f32[1,1,512,12,64]{2,0,4,3,1:T(1,128)S(1)} %copy.157, s32[]{:T(128)S(6)} %copy.193, s32[]{:T(128)} %constant.62.clone.1..sunk.3, s32[]{:T(128)} %constant.62.clone.1..sunk.3, s32[]{:T(128)} %constant.62.clone.1..sunk.3, s32[]{:T(128)} %constant.62.clone.1..sunk.3) | dynamic-update-slice | bytes 3145732 | tf_op jit(solution)/shard_map/while/body/jit(dynamic_update_index_in_dim)/dynamic_update_slice | solution.py:173
  610.5 8.5 mul.488
  619.1 8.8 reshape_transpose.4
  671.6 34.6 %while.51 = (s32[]{:T(128)}, f32[1,512,12,64]{1,3,2,0:T(8,128)S(1)}, bf16[4,1,512,12,64]{2,4,3,1,0:T(8,128)(2,1)}, s32[4]{0:T(128)S(1)}, s32[1]{0:T(128)}, /*ind...) while((s32[]{:T(128)}, ...), condition=%wide.region_7.8_spmd.clone, body=%wide.region_6.7_spmd.clone.sunk | while | flops 819202048 | bytes 6064794 | solution.py:125
  711.7 16.9 reduce-scatter.21.cloned.1.call-done
  733.8 108.4 %reduce-scatter.23.cloned.1.call-done = f32[1,512,768]{2,1,0:T(8,128)} async-done(((f32[1,2048,768]{2,1,0:T(8,128)}), f32[1,512,768]{2,1,0:T(8,128)}) %reduce-scatter.23.cloned.1.call-update) | async-done | bytes 1572880 | tf_op jit(solution)/shard_map/reduce_scatter | solution.py:337
  875.5 929.3 %all-reduce.26.cloned.1.call-done = (f32[1,8,4,24,2304]{4,3,2,1,0:T(8,128)}, f32[1,8,4,24,768]{4,3,2,1,0:T(8,128)}, f32[1,8,4,24,3072]{4,3,2,1,0:T(8,128)}, f32[1,8,4,96,768]{4,3,2,1,0:T(8,128)}) async-done(((f32[1,8,4,24,2304]{4,3,2,1,0:T(8,128)}, f32[1,8,4,24,768]{4,3,2,1,0:T(8,128)}, f32[1,8,4,24,3072]{4,3,2,1,0:T(8,128)}, f32[1,8,4,96,768]{4,3,2,1,0:T(8,128)}), (f32[1,8,4,24,2304]{4,3,2,1,0:T(8,128)}, ...) | async-done | bytes 28311568
  1820.1 15.0 all-reduce.21
  1837.1 16.5 psum.23
  1878.9 19.8 all-reduce.20
  1907.4 25.3 %reduce-scatter.25.cloned.1.call-done = f32[1,1,24,2304]{3,2,0,1:T(8,128)} async-done(((f32[8,1,24,2304]{3,2,0,1:T(8,128)}), f32[1,1,24,2304]{3,2,0,1:T(8,128)}) %reduce-scatter.25.cloned.1.call-update) | async-done | bytes 221200 | tf_op jit(solution)/shard_map/reduce_scatter | solution.py:407
  1932.6 46.6 %reduce-scatter.29.cloned.1.call-done = f32[1,1,24,3072]{3,2,0,1:T(8,128)} async-done(((f32[8,1,24,3072]{3,2,0,1:T(8,128)}), f32[1,1,24,3072]{3,2,0,1:T(8,128)}) %reduce-scatter.29.cloned.1.call-update) | async-done | bytes 294928 | tf_op jit(solution)/shard_map/reduce_scatter | solution.py:413
  1979.3 46.4 %reduce-scatter.31.cloned.1.call-done = f32[1,1,96,768]{3,2,0,1:T(8,128)} async-done(((f32[8,1,96,768]{3,2,0,1:T(8,128)}), f32[1,1,96,768]{3,2,0,1:T(8,128)}) %reduce-scatter.31.cloned.1.call-update) | async-done | bytes 294928 | tf_op jit(solution)/shard_map/reduce_scatter | solution.py:415
  (374 shorter events, 446.2 us)
Async XLA Ops:
  7.2 66.4 %all-gather.7.cloned.1.call-start = ((), (), s32[]{:S(2)}) async-start(), calls=%async_computation.6 | async-start | bytes 3649536 | tf_op jit(solution)/shard_map/all_gather | solution.py:234
  7.9 121.4 %all-gather.13.cloned.1.call-start = ((), (), s32[]{:S(2)}) async-start(), calls=%async_computation.9 | async-start | bytes 1216512 | tf_op jit(solution)/shard_map/all_gather | solution.py:236
  8.7 184.8 %all-gather.9.cloned.1.call-start = ((), (), s32[]{:S(2)}) async-start(), calls=%async_computation.7 | async-start | bytes 3932160 | tf_op jit(solution)/shard_map/all_gather | solution.py:274
  57.1 21.0 %copy-start.20 = (f32[768]{0:T(1024)}, f32[768]{0:T(1024)S(1)}, u32[]{:S(2)}) copy-start(f32[768]{0:T(1024)S(1)} %convert_element_type.154) | copy-start | bytes 9220
  57.1 21.0 %copy-start.29 = (f32[768]{0:T(1024)}, f32[768]{0:T(1024)S(1)}, u32[]{:S(2)}) copy-start(f32[768]{0:T(1024)S(1)} %convert_element_type.155) | copy-start | bytes 9220
  58.4 19.6 copy-start.23
  59.9 18.1 copy-start.27
  81.2 176.5 %all-gather.11.cloned.1.call-start = ((), (), s32[]{:S(2)}) async-start(), calls=%async_computation.8 | async-start | bytes 3932160 | tf_op jit(solution)/shard_map/all_gather | solution.py:273
  87.4 42.0 %copy-start.7 = (bf16[1,512,768]{2,1,0:T(8,128)(2,1)S(1)}, bf16[1,512,768]{2,1,0:T(8,128)(2,1)}, u32[]{:S(2)}) copy-start(bf16[1,512,768]{2,1,0:T(8,128)(2,1)} %param.24) | copy-start | bytes 2359300
  90.9 544.2 %all-gather.15.cloned.1.call-start = ((), (), s32[]{:S(2)}) async-start(), calls=%async_computation.10 | async-start | bytes 4866048 | tf_op jit(solution)/shard_map/all_gather | solution.py:240
  91.5 565.5 %all-gather.17.cloned.1.call-start = ((), (), s32[]{:S(2)}) async-start(), calls=%async_computation.11 | async-start | bytes 4866048 | tf_op jit(solution)/shard_map/all_gather | solution.py:242
  92.1 636.5 %reduce-scatter.21.cloned.1.call-start = ((), (), s32[]{:S(2)}) async-start(), calls=%async_computation.12 | async-start | bytes 7864320 | tf_op jit(solution)/shard_map/reduce_scatter | solution.py:336
  92.9 41.9 %copy-start.25 = (f32[512]{0:T(512)}, f32[512]{0:T(512)S(1)}, u32[]{:S(2)}) copy-start(f32[512]{0:T(512)S(1)} %fusion.127) | copy-start | bytes 6148
  268.1 34.6 %copy-start.14 = (bf16[512,768]{0,1:T(8,128)(2,1)S(1)}, bf16[512,768]{0,1:T(8,128)(2,1)}, u32[]{:S(2)}) copy-start(bf16[512,768]{0,1:T(8,128)(2,1)} %copy.90) | copy-start | bytes 2359300
  619.0 223.2 %reduce-scatter.23.cloned.1.call-start = ((), (), s32[]{:S(2)}) async-start(), calls=%async_computation.13 | async-start | bytes 7864320 | tf_op jit(solution)/shard_map/reduce_scatter | solution.py:337
  634.5 1170.3 %all-reduce.26.cloned.1.call-start = ((), (), s32[]{:S(2)}) async-start(), calls=%async_computation.18 | async-start | bytes 56623104
  708.4 21.5 %copy-start.19 = (f32[512,8]{0,1:T(8,128)S(1)}, f32[512,8]{0,1:T(8,128)}, u32[]{:S(2)}) copy-start(f32[512,8]{0,1:T(8,128)} %copy-done.18) | copy-start | bytes 49156
  708.5 21.5 %copy-start.22 = (f32[512,8]{0,1:T(8,128)S(1)}, f32[512,8]{0,1:T(8,128)}, u32[]{:S(2)}) copy-start(f32[512,8]{0,1:T(8,128)} %get-tuple-element.635) | copy-start | bytes 49156
  732.3 111.4 %copy-start.21 = (f32[768]{0:T(1024)S(1)}, f32[768]{0:T(1024)}, u32[]{:S(2)}) copy-start(f32[768]{0:T(1024)} %copy-done.20) | copy-start | bytes 9220
  732.6 115.8 %copy-start.15 = (bf16[512,768]{1,0:T(8,128)(2,1)}, bf16[512,768]{1,0:T(8,128)(2,1)S(1)}, u32[]{:S(2)}) copy-start(bf16[512,768]{1,0:T(8,128)(2,1)S(1)} %copy.99) | copy-start | bytes 2359300
  866.2 1041.2 %reduce-scatter.27.cloned.1.call-start = ((), (), s32[]{:S(2)}) async-start(), calls=%async_computation.15 | async-start | bytes 663552 | tf_op jit(solution)/shard_map/reduce_scatter | solution.py:409
  1856.9 75.7 %reduce-scatter.25.cloned.1.call-start = ((), (), s32[]{:S(2)}) async-start(), calls=%async_computation.14 | async-start | bytes 1990656 | tf_op jit(solution)/shard_map/reduce_scatter | solution.py:407
  1860.5 118.8 %reduce-scatter.29.cloned.1.call-start = ((), (), s32[]{:S(2)}) async-start(), calls=%async_computation.16 | async-start | bytes 2654208 | tf_op jit(solution)/shard_map/reduce_scatter | solution.py:413
  1864.6 161.1 %reduce-scatter.31.cloned.1.call-start = ((), (), s32[]{:S(2)}) async-start(), calls=%async_computation.17 | async-start | bytes 2654208 | tf_op jit(solution)/shard_map/reduce_scatter | solution.py:415
  (30 other events, 118.0 us)
Sparse Core Ops, SparseCore 0:
  10.8 62.7 all-gather.6
  76.4 52.8 all-gather.12
  131.5 61.9 all-gather.8
  195.5 62.1 all-gather.10
  260.3 62.6 all-gather.14
  325.7 62.3 all-gather.16
  619.1 109.4 reduce-scatter.20
  730.9 111.2 reduce-scatter.22
  866.3 938.4 all-reduce.25
  1857.0 31.3 reduce-scatter.26
  1892.7 39.8 reduce-scatter.24
  1936.8 42.4 reduce-scatter.28
  1983.2 42.4 reduce-scatter.30
where the time goes:
time: 2050 us; the launch traced here: 2030 us
  waiting for transfers between devices  1330 us (65%)
  matrix products  246 us (12%)
  local copies, waits for them, and re-layouts  242 us (12%)
  other arithmetic  96.1 us (5%)
  blocking collectives  92.9 us (5%)
  between operations  21.6 us (1%)
    unnamed x14, waiting for transfers between devices  932 us
    dynamic_update_slice x8, local copies, waits for them, and re-layouts, attend_back(): lax.scan(grad_pass, jnp.zeros(queries.shape, jnp.float32), (key_blocks, v...  130 us
    reduce_scatter x1, waiting for transfers between devices, local(): lax.psum_scatter(grad_values, 'ctx', scatter_dimension=1, tiled=True)  108 us
    unnamed x2, blocking collectives  61.4 us
    all_gather x1, waiting for transfers between devices, local(): lax.all_gather(value_rows, 'ctx', axis=1, tiled=True)  58.7 us
    dot_general x12, matrix products, masked_scores(): jnp.einsum('srhd,skhd->shrk', queries, key_block, preferred_element_type=...  54.9 us
    dot_general x8, matrix products, weights_of(): jnp.einsum('srhd,skhd->shrk', grad_out, value_block, preferred_element_ty...  49.5 us
    all_gather x1, waiting for transfers between devices, local(): lax.all_gather(key_rows, 'ctx', axis=1, tiled=True)  48.7 us
  transfers between devices with their start and end apart: 13, of which 10 were waited for; matrix products, arithmetic and copies ran while one was open for 27% of the time, Pallas kernels for 0%

commit v1 on v0

v1 whole, which is shorter than its diff:
```python
import functools
import math

import jax
import jax.numpy as jnp
import numpy as np
from jax import lax
from jax.experimental import pallas as pl
from jax.experimental.pallas import tpu as pltpu
from jax.sharding import PartitionSpec as P

D = 768
HEADS = 12
HEAD_DIM = 64
ROT = 16
PAD = 128
eps_norm = 1e-05
neg_big = -1e30
root_half = math.sqrt(0.5)
inv_root_two_pi = 1.0 / math.sqrt(2.0 * math.pi)
f32 = jnp.float32
bf16 = jnp.bfloat16
VMEM_BYTES = 60 * 2**20


def dot(a, b, dims=((1,), (0,))):
    return lax.dot_general(a, b, (dims, ((), ())), preferred_element_type=f32)


def norm_parts(values):
    centered = values - jnp.mean(values, axis=-1, keepdims=True)
    row_var = jnp.mean(centered * centered, axis=-1, keepdims=True)
    inverse = lax.rsqrt(row_var + eps_norm)
    return centered * inverse, inverse


def turn(u, cosine, sine, first):
    partner = jnp.where(first, pltpu.roll(u, PAD - ROT // 2, 1), pltpu.roll(u, ROT // 2, 1))
    return u * cosine + partner * sine


def split3(v):
    hi = v.astype(bf16).astype(f32)
    mid = (v - hi).astype(bf16).astype(f32)
    low = (v - hi - mid).astype(bf16).astype(f32)
    return hi, mid, low


def fold(op, s):
    out = s[:, :PAD]
    for t in range(1, s.shape[1] // PAD):
        out = op(out, s[:, t * PAD : (t + 1) * PAD])
    return out


def attn_fwd_kernel(
    len_ref, x_ref, g_ref, b_ref, w_ref, wb_ref, cos_ref, sin_ref,
    q_ref, k_ref, v_ref, cf_ref, s_scr, q_scr, m_scr, l_scr, acc_scr,
):
    i = pl.program_id(0)
    nh = k_ref.shape[0]
    rows = x_ref.shape[0]
    length = len_ref[0]
    xhat, unused = norm_parts(x_ref[...].astype(f32))
    a1 = (xhat * g_ref[...] + b_ref[...]).astype(bf16)
    cosine, sine = cos_ref[...], sin_ref[...]
    lane = lax.broadcasted_iota(jnp.int32, (rows, PAD), 1)
    first = lane < ROT // 2
    key_pos = i * rows + lax.broadcasted_iota(jnp.int32, (rows, PAD), 0)
    key_bias = jnp.where(key_pos < length, 0.0, neg_big)
    here = pl.ds(pl.multiple_of(i * rows, rows), rows)
    qkv = dot(a1, w_ref[...]) + wb_ref[...]
    for h in range(nh):
        q = turn(qkv[:, h * PAD : (h + 1) * PAD], cosine, sine, first) * HEAD_DIM**-0.5
        q_scr[h] = q.astype(bf16)
        k = turn(qkv[:, (nh + h) * PAD : (nh + h + 1) * PAD], cosine, sine, first)
        k_ref[h, here] = jnp.where(lane == HEAD_DIM, key_bias, k).astype(bf16)
        v_ref[h, here] = qkv[:, (2 * nh + h) * PAD : (2 * nh + h + 1) * PAD].astype(bf16)

    causal = lax.broadcasted_iota(jnp.int32, (rows, rows), 0) >= lax.broadcasted_iota(
        jnp.int32, (rows, rows), 1
    )
    for h in range(nh):
        s = dot(q_scr[h], k_ref[h, here], ((1,), (1,)))
        s = jnp.where(causal, s, neg_big)
        s_scr[h, i] = s
        m_scr[h] = fold(jnp.maximum, s)

    def scores(j, carry):
        there = pl.ds(pl.multiple_of(j * rows, rows), rows)
        for h in range(nh):
            s = dot(q_scr[h], k_ref[h, there], ((1,), (1,)))
            s_scr[h, j] = s
            m_scr[h] = jnp.maximum(m_scr[h], fold(jnp.maximum, s))
        return carry

    lax.fori_loop(0, i, scores, 0)
    for h in range(nh):
        m_scr[h] = jnp.broadcast_to(jnp.max(m_scr[h], axis=-1, keepdims=True), (rows, PAD))
        l_scr[h] = jnp.zeros((rows, PAD), f32)
        acc_scr[h] = jnp.zeros((rows, PAD), f32)

    def weigh(j, carry):
        there = pl.ds(pl.multiple_of(j * rows, rows), rows)
        for h in range(nh):
            p = jnp.exp(s_scr[h, j] - m_scr[h][:, :1])
            l_scr[h] += fold(jnp.add, p)
            acc_scr[h] += dot(p.astype(bf16), v_ref[h, there])
        return carry

    lax.fori_loop(0, i + 1, weigh, 0)
    for h in range(nh):
        total = jnp.sum(l_scr[h], axis=-1, keepdims=True)
        cf_ref[:, h * PAD : (h + 1) * PAD] = acc_scr[h] / total
        hi, mid, low = split3(-(m_scr[h][:, :1] + jnp.log(total)))
        q = q_scr[h].astype(f32)
        q = jnp.where(lane == HEAD_DIM + 1, hi, q)
        q = jnp.where(lane == HEAD_DIM + 2, mid, q)
        q = jnp.where(lane == HEAD_DIM + 3, low, q)
        q_ref[h] = q.astype(bf16)


def mlp_kernel(
    x_ref, dy_ref, cf_ref, g_ref, b_ref, wo_ref, w1_ref, b1_ref, w2_ref,
    part_ref, u_ref, dw1_ref, dw2_ref, vec_ref,
):
    i = pl.program_id(0)
    xhat, unused = norm_parts(x_ref[...].astype(f32))
    gain = g_ref[...]
    a2 = (xhat * gain + b_ref[...]).astype(bf16)
    z = dot(a2, w1_ref[...]) + b1_ref[...]
    cdf = 0.5 * (1.0 + lax.erf(z * root_half))
    hidden = (z * cdf).astype(bf16)
    part = dot(hidden, w2_ref[...]) + dot(cf_ref[...].astype(bf16), wo_ref[...])
    part_ref[...] = part.astype(part_ref.dtype)
    dy = dy_ref[...]
    slope = cdf + z * jnp.exp(-0.5 * z * z) * inv_root_two_pi
    dz = (dot(dy, w2_ref[...], ((1,), (1,))) * slope).astype(bf16)
    da2 = dot(dz, w1_ref[...], ((1,), (1,)))
    u_ref[...] = (da2 * gain).astype(u_ref.dtype)
    dw1 = dot(a2, dz, ((0,), (0,)))
    dw2 = dot(hidden, dy, ((0,), (0,)))
    sums = [
        jnp.sum(dz.astype(f32), axis=0, keepdims=True),
        jnp.sum(da2 * xhat, axis=0, keepdims=True),
        jnp.sum(da2, axis=0, keepdims=True),
        jnp.sum(dy.astype(f32), axis=0, keepdims=True),
    ]

    @pl.when(i == 0)
    def _():
        dw1_ref[...] = dw1
        dw2_ref[...] = dw2
        for t in range(4):
            vec_ref[t : t + 1] = sums[t]

    @pl.when(i > 0)
    def _():
        dw1_ref[...] += dw1
        dw2_ref[...] += dw2
        for t in range(4):
            vec_ref[t : t + 1] += sums[t]


def attn_bwd_kernel(
    x_ref, dy_ref, cf_ref, u_in_ref, q_ref, k_ref, v_ref, g_ref, b_ref, w_ref, wo_ref,
    cos_ref, sin_ref,
    u_ref, dw_ref, dwo_ref, vec_ref, dwb_ref, dk_scr, dv_scr, dq_scr, dc_scr, dqkv_scr,
):
    step = pl.program_id(0)
    blocks = pl.num_programs(0)
    i = blocks - 1 - step
    nh = k_ref.shape[0]
    rows = x_ref.shape[0]
    lane = lax.broadcasted_iota(jnp.int32, (rows, PAD), 1)
    first = lane < ROT // 2
    here = pl.ds(pl.multiple_of(i * rows, rows), rows)
    dy = dy_ref[...]
    dc_all = dot(dy, wo_ref[...], ((1,), (1,))).astype(bf16)
    for h in range(nh):
        dc = dc_all[:, h * PAD : (h + 1) * PAD].astype(f32)
        delta = jnp.sum(dc * cf_ref[:, h * PAD : (h + 1) * PAD], axis=-1, keepdims=True)
        hi, mid, low = split3(-delta)
        dc = jnp.where(lane == HEAD_DIM, hi, dc)
        dc = jnp.where(lane == HEAD_DIM + 1, mid, dc)
        dc = jnp.where(lane == HEAD_DIM + 2, low, dc)
        dc_scr[h] = dc.astype(bf16)

    @pl.when(step == 0)
    def _():
        dk_scr[...] = jnp.zeros_like(dk_scr)
        dv_scr[...] = jnp.zeros_like(dv_scr)

    causal = lax.broadcasted_iota(jnp.int32, (rows, rows), 0) <= lax.broadcasted_iota(
        jnp.int32, (rows, rows), 1
    )

    def block(j, diagonal):
        there = pl.ds(pl.multiple_of(j * rows, rows), rows)
        for h in range(nh):
            k = k_ref[h, there]
            q = q_ref[h]
            dc = dc_scr[h]
            st = dot(k, q, ((1,), (1,)))
            pt = jnp.exp(st)
            if diagonal:
                pt = jnp.where(causal, pt, 0.0)
            dpt = dot(v_ref[h, there], dc, ((1,), (1,)))
            dst = (pt * dpt).astype(bf16)
            dv_scr[h, there] += dot(pt.astype(bf16), dc)
            dk_scr[h, there] += dot(dst, q)
            dq = dot(dst, k, ((0,), (0,)))
            if diagonal:
                dq_scr[h] = dq
            else:
                dq_scr[h] += dq

    block(i, True)

    def off(j, carry):
        block(j, False)
        return carry

    lax.fori_loop(0, i, off, 0)
    cosine, sine = cos_ref[...], -sin_ref[...]
    real = lane < HEAD_DIM
    for h in range(nh):
        dq = turn(dq_scr[h], cosine, sine, first) * HEAD_DIM**-0.5
        dk = turn(dk_scr[h, here], cosine, sine, first)
        for place, part in ((h, dq), (nh + h, dk), (2 * nh + h, dv_scr[h, here])):
            dqkv_scr[:, place * PAD : (place + 1) * PAD] = jnp.where(real, part, 0.0).astype(bf16)
    dqkv = dqkv_scr[...]
    xhat, unused = norm_parts(x_ref[...].astype(f32))
    gain = g_ref[...]
    a1 = (xhat * gain + b_ref[...]).astype(bf16)
    da1 = dot(dqkv, w_ref[...], ((1,), (1,)))
    u_ref[...] = (u_in_ref[...].astype(f32) + da1 * gain).astype(u_ref.dtype)
    dw = dot(a1, dqkv, ((0,), (0,)))
    dwo = dot(cf_ref[...].astype(bf16), dy, ((0,), (0,)))
    sums = [jnp.sum(da1 * xhat, axis=0, keepdims=True), jnp.sum(da1, axis=0, keepdims=True)]
    dwb = jnp.sum(dqkv.astype(f32), axis=0, keepdims=True)

    @pl.when(step == 0)
    def _():
        dw_ref[...] = dw
        dwo_ref[...] = dwo
        dwb_ref[...] = dwb
        for t in range(2):
            vec_ref[t : t + 1] = sums[t]

    @pl.when(step > 0)
    def _():
        dw_ref[...] += dw
        dwo_ref[...] += dwo
        dwb_ref[...] += dwb
        for t in range(2):
            vec_ref[t : t + 1] += sums[t]


def whole(shape):
    return pl.BlockSpec(shape, lambda i: (0,) * len(shape), pipeline_mode=pl.Buffered(1))


def sds(shape, dtype):
    return jax.ShapeDtypeStruct(shape, dtype)


def params():
    return pltpu.CompilerParams(
        dimension_semantics=("arbitrary",), vmem_limit_bytes=VMEM_BYTES
    )


def attn_fwd(length, x, g1, b1, w, wb, cosine, sine, nh, rows):
    t = x.shape[0]
    return pl.pallas_call(
        attn_fwd_kernel,
        grid=(t // rows,),
        out_shape=(
            sds((nh, t, PAD), bf16), sds((nh, t, PAD), bf16), sds((nh, t, PAD), bf16),
            sds((t, nh * PAD), f32),
        ),
        in_specs=[
            pl.BlockSpec(memory_space=pltpu.SMEM),
            pl.BlockSpec((rows, D), lambda i: (i, 0)),
            whole((1, D)), whole((1, D)), whole(w.shape), whole(wb.shape),
            pl.BlockSpec((rows, PAD), lambda i: (i, 0)),
            pl.BlockSpec((rows, PAD), lambda i: (i, 0)),
        ],
        out_specs=(
            pl.BlockSpec((nh, rows, PAD), lambda i: (0, i, 0)),
            whole((nh, t, PAD)), whole((nh, t, PAD)),
            pl.BlockSpec((rows, nh * PAD), lambda i: (i, 0)),
        ),
        scratch_shapes=[
            pltpu.VMEM((nh, t // rows, rows, rows), f32),
            pltpu.VMEM((nh, rows, PAD), bf16),
            pltpu.VMEM((nh, rows, PAD), f32),
            pltpu.VMEM((nh, rows, PAD), f32),
            pltpu.VMEM((nh, rows, PAD), f32),
        ],
        compiler_params=params(),
        name="attn_fwd",
    )(length, x, g1, b1, w, wb, cosine, sine)


def mlp(x, dy, cf, g2, b2, wo, w1, bias1, w2, rows):
    t = x.shape[0]
    ff = w1.shape[1]
    row = pl.BlockSpec((rows, D), lambda i: (i, 0))
    return pl.pallas_call(
        mlp_kernel,
        grid=(t // rows,),
        out_shape=(
            sds((t, D), bf16), sds((t, D), f32), sds((D, ff), f32), sds((ff, D), f32),
            sds((8, D), f32),
        ),
        in_specs=[
            row, row, pl.BlockSpec((rows, cf.shape[1]), lambda i: (i, 0)),
            whole((1, D)), whole((1, D)), whole(wo.shape), whole(w1.shape), whole((1, ff)),
            whole(w2.shape),
        ],
        out_specs=(row, row, whole((D, ff)), whole((ff, D)), whole((8, D))),
        compiler_params=params(),
        name="mlp",
    )(x, dy, cf, g2, b2, wo, w1, bias1, w2)


def attn_bwd(x, dy, cf, u_in, q, k, v, g1, b1, w, wo, cosine, sine, rows):
    t = x.shape[0]
    nh = q.shape[0]
    n = t // rows
    wide = w.shape[1]
    row = pl.BlockSpec((rows, D), lambda i: (n - 1 - i, 0))
    lanes = pl.BlockSpec((rows, PAD), lambda i: (n - 1 - i, 0))
    return pl.pallas_call(
        attn_bwd_kernel,
        grid=(n,),
        out_shape=(
            sds((t, D), bf16), sds((D, wide), f32), sds((nh * PAD, D), f32), sds((8, D), f32),
            sds((1, wide), f32),
        ),
        in_specs=[
            row, row, pl.BlockSpec((rows, nh * PAD), lambda i: (n - 1 - i, 0)), row,
            pl.BlockSpec((nh, rows, PAD), lambda i: (0, n - 1 - i, 0)),
            whole(k.shape), whole(v.shape), whole((1, D)), whole((1, D)), whole(w.shape),
            whole(wo.shape), lanes, lanes,
        ],
        out_specs=(
            row, whole((D, wide)), whole((nh * PAD, D)), whole((8, D)), whole((1, wide)),
        ),
        scratch_shapes=[
            pltpu.VMEM((nh, t, PAD), f32),
            pltpu.VMEM((nh, t, PAD), f32),
            pltpu.VMEM((nh, rows, PAD), f32),
            pltpu.VMEM((nh, rows, PAD), bf16),
            pltpu.VMEM((rows, wide), bf16),
        ],
        compiler_params=params(),
        name="attn_bwd",
    )(x, dy, cf, u_in, q, k, v, g1, b1, w, wo, cosine, sine)


def tables(t):
    inv_freqs = np.exp(np.arange(ROT // 2, dtype=np.float32) * np.float32(-2.0 * math.log(10000.0) / ROT))
    angles = np.arange(t, dtype=np.float32)[:, None] * inv_freqs.astype(np.float32)[None, :]
    cosine = np.ones((t, PAD), np.float32)
    sine = np.zeros((t, PAD), np.float32)
    half = ROT // 2
    cosine[:, :half] = cosine[:, half:ROT] = np.cos(angles)
    sine[:, :half] = -np.sin(angles)
    sine[:, half:ROT] = np.sin(angles)
    return jnp.asarray(cosine), jnp.asarray(sine)


def local(
    block_in, out_grad, lengths, ln1_gain, ln1_bias, qkv_weight, qkv_bias, out_weight, out_bias,
    ln2_gain, ln2_bias, fc1_weight, fc1_bias, fc2_weight, fc2_bias,
):
    tp = lax.axis_size("ctx")
    dp = lax.axis_size("dp")
    world = dp * tp
    z = lax.axis_index("ctx")
    d = lax.axis_index("dp")
    nh = HEADS // tp
    local_rows = block_in.shape[1]
    t = local_rows * tp
    rows = min(512, local_rows)
    part = D // tp
    r_in = D // world
    r_ff = fc2_weight.shape[0]
    ff = r_ff * dp

    x_own = block_in[0]
    pos = z * local_rows + jnp.arange(local_rows, dtype=jnp.int32)
    dy_own = jnp.where((pos < lengths[0])[:, None], out_grad[0], jnp.zeros((), bf16))
    x = lax.all_gather(x_own, "ctx", axis=0, tiled=True)
    dy = lax.all_gather(dy_own, "ctx", axis=0, tiled=True)

    w_qkv = jnp.moveaxis(qkv_weight.reshape(r_in, 3, tp, part), 2, 0).reshape(tp, r_in, 3 * part)
    w_qkv = lax.all_to_all(w_qkv, "ctx", 0, 0)
    w_qkv = lax.all_gather(w_qkv, "dp", axis=0, tiled=True).reshape(D, 3 * part)
    w1 = jnp.moveaxis(fc1_weight.reshape(r_in, dp, tp, r_ff), 2, 0).reshape(tp, r_in, ff)
    w1 = lax.all_to_all(w1, "ctx", 0, 0)
    w1 = lax.all_gather(w1, "dp", axis=0, tiled=True).reshape(D, ff)
    w2 = lax.all_gather(fc2_weight, "dp", axis=0, tiled=True)
    wo = lax.all_gather(out_weight, ("dp", "ctx"), axis=0, tiled=True)
    wo = lax.dynamic_slice_in_dim(wo, z * part, part, axis=0)
    vectors = jnp.concatenate(
        [ln1_gain, ln1_bias, out_bias, ln2_gain, ln2_bias, fc2_bias, qkv_bias, fc1_bias]
    )
    vectors = lax.all_gather(vectors, ("dp", "ctx"), axis=0).astype(f32)
    g1, b1, b_out, g2, b2, b_down = [
        vectors[:, s * r_in : (s + 1) * r_in].reshape(1, D) for s in range(6)
    ]
    b_qkv = vectors[:, 6 * r_in : 9 * r_in].reshape(3, tp, part)
    b_qkv = lax.dynamic_slice_in_dim(b_qkv, z, 1, axis=1).reshape(3 * nh, HEAD_DIM)
    b_up = vectors[:, 9 * r_in :].reshape(dp, tp, r_ff)
    b_up = lax.dynamic_slice_in_dim(b_up, z, 1, axis=1).reshape(1, ff)

    w_pad = jnp.pad(w_qkv.reshape(D, 3 * nh, HEAD_DIM), ((0, 0), (0, 0), (0, PAD - HEAD_DIM)))
    w_pad = w_pad.reshape(D, 3 * nh * PAD)
    extra = np.zeros((3 * nh, PAD - HEAD_DIM), np.float32)
    extra[:nh, 0] = HEAD_DIM**0.5
    extra[nh : 2 * nh, 1:4] = 1.0
    extra[2 * nh :, 0:3] = 1.0
    b_pad = jnp.concatenate([b_qkv, jnp.asarray(extra)], axis=1).reshape(1, 3 * nh * PAD)
    wo_pad = jnp.pad(wo.reshape(nh, HEAD_DIM, D), ((0, 0), (0, PAD - HEAD_DIM), (0, 0)))
    wo_pad = wo_pad.reshape(nh * PAD, D)
    cosine, sine = tables(t)

    q, k, v, cf = attn_fwd(lengths, x, g1, b1, w_pad, b_pad, cosine, sine, nh, rows)
    out_part, u_mlp, dw1, dw2, vec2 = mlp(x, dy, cf, g2, b2, wo_pad, w1, b_up, w2, rows // 2)
    out_sum = lax.psum_scatter(out_part, "ctx", scatter_dimension=0, tiled=True)
    block_out = (x_own.astype(f32) + b_out + b_down + out_sum.astype(f32)).astype(bf16)
    u_part, dw_pad, dwo_pad, vec1, dwb_pad = attn_bwd(
        x, dy, cf, u_mlp, q, k, v, g1, b1, w_pad, wo_pad, cosine, sine, rows
    )
    u = lax.psum_scatter(u_part, "ctx", scatter_dimension=0, tiled=True).astype(f32)
    xhat, inverse = norm_parts(x_own.astype(f32))
    back = inverse * (
        u
        - jnp.mean(u, axis=-1, keepdims=True)
        - xhat * jnp.mean(u * xhat, axis=-1, keepdims=True)
    )
    input_grad = (dy_own.astype(f32) + back).astype(bf16)

    dw = dw_pad.reshape(D, 3 * nh, PAD)[:, :, :HEAD_DIM].reshape(D, 3 * part)
    dwo = dwo_pad.reshape(nh, PAD, D)[:, :HEAD_DIM].reshape(part, D)
    dwb = dwb_pad.reshape(3 * nh, PAD)[:, :HEAD_DIM].reshape(3, part)
    squares = sum(jnp.sum(m * m) for m in (dw, dwo, dwb, dw1, dw2, vec2[0]))
    norm_vecs, squares = lax.psum(
        (jnp.stack([vec1[0], vec1[1], vec2[1], vec2[2]]), squares), "ctx"
    )
    squares = squares + jnp.sum(norm_vecs * norm_vecs) + 2.0 * jnp.sum(vec2[3] * vec2[3])
    example_norm = jnp.sqrt(squares)
    mean_norm = lax.psum(example_norm, "dp") / dp
    factor = mean_norm / jnp.maximum(example_norm, mean_norm)

    def over_dp(m):
        return lax.psum_scatter(
            (m * factor).astype(bf16), "dp", scatter_dimension=0, tiled=True
        )

    def back_rows(m):
        m = lax.all_to_all(m.reshape(tp, r_in, m.shape[1]), "ctx", 0, 0)
        return m.astype(f32)

    g_qkv = back_rows(over_dp(dw)).reshape(tp, r_in, 3, part)
    g_qkv = jnp.moveaxis(g_qkv, 0, 2).reshape(r_in, 3 * D)
    g_fc1 = back_rows(over_dp(dw1)).reshape(tp, r_in, dp, r_ff)
    g_fc1 = jnp.moveaxis(g_fc1, 0, 2).reshape(r_in, ff * tp)
    g_fc2 = over_dp(dw2).astype(f32)
    moves = []
    for zz in range(tp):
        for dd in range(dp):
            moves.append((dd * tp + zz, zz * dp + dd))
    g_out = lax.ppermute(over_dp(dwo), ("dp", "ctx"), moves).astype(f32)

    share = jnp.where(z == 0, factor, 0.0)
    full_qkv = lax.dynamic_update_slice_in_dim(
        jnp.zeros((3, tp, part), f32), dwb[:, None] * factor, z, axis=1
    )
    full_up = lax.dynamic_update_slice_in_dim(
        jnp.zeros((dp, tp, r_ff), f32), vec2[0].reshape(dp, 1, r_ff) * factor, z, axis=1
    )
    small = jnp.concatenate(
        [
            (norm_vecs * share).reshape(4, world, r_in).swapaxes(0, 1).reshape(world, 4 * r_in),
            (vec2[3] * share).reshape(world, r_in),
            full_qkv.reshape(world, 3 * r_in),
            full_up.reshape(world, r_ff),
        ],
        axis=1,
    )
    small = lax.psum(small, ("dp", "ctx"))
    mine = lax.dynamic_slice_in_dim(small, d * tp + z, 1, axis=0)[0]
    cut = [mine[s * r_in : (s + 1) * r_in] for s in range(5)]
    return (
        block_out[None], input_grad[None],
        cut[0], cut[1], g_qkv, mine[5 * r_in : 8 * r_in], g_out, cut[4],
        cut[2], cut[3], g_fc1, mine[8 * r_in :], g_fc2, cut[4],
        example_norm[None],
    )


def solution(mesh):
    both = ("dp", "ctx")
    vec, mat, act = P(both), P(both, None), P("dp", "ctx", None)
    weights = (vec, vec, mat, vec, mat, vec, vec, vec, mat, vec, mat, vec)
    return jax.shard_map(
        local,
        mesh=mesh,
        in_specs=(act, act, P("dp")) + weights,
        out_specs=(act, act) + weights + (P("dp"),),
        check_vma=False,
    )
```

time: 2050 us -> 671 us (0.33)
  waiting for transfers between devices: 1330 us -> 327 us
  matrix products: 246 us -> 0 us
  local copies, waits for them, and re-layouts: 242 us -> 34.1 us
  Pallas kernels: 0 us -> 107 us
  other arithmetic: 96.1 us -> 24.7 us
  blocking collectives: 92.9 us -> 137 us
    unnamed x14 -> x11, waiting for transfers between devices: 932 us -> 3.34 us
    dot_general x48 -> x0, matrix products: 246 us -> none  [the longest x12 54.9 us: masked_scores(): jnp.einsum('srhd,skhd->shrk', queries, key_block, preferred_element_type=...]
    dynamic_update_slice x8 -> x2, local copies, waits for them, and re-layouts: 130 us -> 0.09 us  [the longest x1 0.04 us: local(): lax.dynamic_update_slice_in_dim(jnp.zeros((dp, tp, r_ff), f32), vec2[0].r...]
    pallas_call x0 -> x3, Pallas kernels: none -> 107 us  [the longest x1 48.6 us: attn_bwd(): pl.pallas_call(attn_bwd_kernel, grid=(n,), out_shape=(sds((t, D), bf16),...]
    all_gather x6 -> x5, waiting for transfers between devices: 157 us -> 118 us  [the longest x1 65 us: local(): dy = lax.all_gather(dy_own, 'ctx', axis=0, tiled=True)]
    psum x2 -> x3, blocking collectives: 31.5 us -> 70.4 us  [the longest x1 39.9 us: local(): small = lax.psum(small, ('dp', 'ctx'))]
    reduce_scatter x6, waiting for transfers between devices: 244 us -> 205 us  [the longest x4 85 us: over_dp(): lax.psum_scatter((m * factor).astype(bf16), 'dp', scatter_dimension=0, ti...]
    reduce_sum x17 -> x8, other arithmetic: 45.1 us -> 10.9 us  [the longest x4 5.99 us: local(): squares = sum((jnp.sum(m * m) for m in (dw, dwo, dwb, dw1, dw2, vec2[0])))]
  transfers between devices with their start and end apart: 13 -> 15, of which waited for: 10 -> 9; matrix products, arithmetic and copies ran while one was open for 27% -> 5% of each run, Pallas kernels for 0% -> 4%
where the time goes in v1:
time: 671 us; the launch traced here: 669 us
  waiting for transfers between devices  327 us (49%)
  blocking collectives  137 us (20%)
  Pallas kernels  107 us (16%)
  local copies, waits for them, and re-layouts  34.1 us (5%)
  other arithmetic  24.7 us (4%)
  between operations  22.8 us (3%)
  starting transfers between devices  15.8 us (2%)
    reduce_scatter x4, waiting for transfers between devices, over_dp(): lax.psum_scatter((m * factor).astype(bf16), 'dp', scatter_dimension=0, ti...  85 us
    all_gather x1, waiting for transfers between devices, local(): dy = lax.all_gather(dy_own, 'ctx', axis=0, tiled=True)  65 us
    reduce_scatter x1, waiting for transfers between devices, local(): out_sum = lax.psum_scatter(out_part, 'ctx', scatter_dimension=0, tiled=True)  60.8 us
    reduce_scatter x1, waiting for transfers between devices, local(): lax.psum_scatter(u_part, 'ctx', scatter_dimension=0, tiled=True).astype(f32)  59.3 us
    pallas_call x1, Pallas kernels, attn_bwd(): pl.pallas_call(attn_bwd_kernel, grid=(n,), out_shape=(sds((t, D), bf16),...  48.6 us
    unnamed x1, blocking collectives  41.7 us
    psum x1, blocking collectives, local(): small = lax.psum(small, ('dp', 'ctx'))  39.9 us
    all_gather x1, waiting for transfers between devices, local(): x = lax.all_gather(x_own, 'ctx', axis=0, tiled=True)  30.7 us
  transfers between devices with their start and end apart: 15, of which 9 were waited for; matrix products, arithmetic and copies ran while one was open for 5% of the time, Pallas kernels for 4%

profile of v1, /device:TPU:1, one launch (start us, length us, event | category | flops | bytes accessed | tf_op | source)
XLA Modules:
  0.0 668.7 jit_solution(15086862832186778780)
XLA Ops:
  10.8 10.9 %all_to_all.20 = bf16[4,24,768]{2,1,0:T(8,128)(2,1)} all-to-all(bf16[4,24,768]{2,1,0:T(8,128)(2,1)S(1)} %reshape.220), channel_id=1, replica_groups=mesh['dp'=8,'ctx'=4] {'ctx'}, dimensions={0} | all-to-all | bytes 294912 | tf_op jit(solution)/shard_map/all_to_all | solution.py:404
  24.7 3.3 all-to-all-start
  28.6 41.7 %all-reduce.2 = bf16[9984]{0:T(1024)(128)(2,1)S(1)} all-reduce(bf16[9984]{0:T(1024)(128)(2,1)S(1)} %dynamic-update-slice), channel_id=2, replica_groups=mesh['dp'=8,'ctx'=4] {'dp','ctx'}, use_global_device_ids=true, to_apply=%add.2 | all-reduce | flops 9984 | bytes 39936
  75.4 14.0 %all_gather.28 = bf16[32,24,576]{2,1,0:T(8,128)(2,1)} all-gather(bf16[4,24,576]{2,1,0:T(8,128)(2,1)S(1)} %all-to-all-done), channel_id=1, replica_groups=mesh['dp'=8,'ctx'=4] {'dp'}, dimensions={0}, use_global_device_ids=true | all-gather | bytes 995328 | tf_op jit(solution)/shard_map/all_gather | solution.py:402
  89.4 3.1 reshape_reshape.3
  100.6 30.7 %all-gather.16.cloned.1.call-done = bf16[1,2048,768]{2,1,0:T(8,128)(2,1)} async-done(((bf16[1,512,768]{2,1,0:T(8,128)(2,1)}), bf16[1,2048,768]{2,1,0:T(8,128)(2,1)}) %all-gather.16.cloned.1.call-update) | async-done | bytes 3145744 | tf_op jit(solution)/shard_map/all_gather | solution.py:397
  131.3 28.9 %attn_fwd.1 = (bf16[3,2048,128]{2,1,0:T(8,128)(2,1)}, bf16[3,2048,128]{2,1,0:T(8,128)(2,1)}, bf16[3,2048,128]{2,1,0:T(8,128)(2,1)}, f32[2048,384]{1,0:T(8,128)}) custom-call(s32[1]{0:T(128)} %copy.94.len_ref, bf16[2048,768]{1,0:T(8,128)(2,1)} %bitcast.99, f32[1,768]{1,0:T(1,128)} %reshape.207.g_ref, f32[1,768]{1,0:T(1,128)} %reshape.208.b_ref, ...), custom_call_target="tpu_custom_call" | custom-call | tf_op jit(solution)/shard_map/attn_fwd/pallas_call | solution.py:276
  160.3 22.0 %all-gather.12.cloned.1.call-done = bf16[32,24,768]{2,1,0:T(8,128)(2,1)} async-done(((bf16[4,24,768]{2,1,0:T(8,128)(2,1)}), bf16[32,24,768]{2,1,0:T(8,128)(2,1)}) %all-gather.12.cloned.1.call-update) | async-done | bytes 1179664 | tf_op jit(solution)/shard_map/all_gather | solution.py:405
  182.3 65.0 %all-gather.8.cloned.1.call-done.dy_ref = bf16[2048,768]{1,0:T(8,128)(2,1)} async-done(((bf16[512,768]{1,0:T(8,128)(2,1)}), bf16[2048,768]{1,0:T(8,128)(2,1)}) %all-gather.8.cloned.1.call-update) | async-done | bytes 3145744 | tf_op jit(solution)/shard_map/all_gather | solution.py:398
  247.3 29.4 %mlp.1 = (bf16[2048,768]{1,0:T(8,128)(2,1)}, f32[2048,768]{1,0:T(8,128)}, f32[768,768]{1,0:T(8,128)}, f32[768,768]{1,0:T(8,128)}, f32[8,768]{1,0:T(8,128)}) custom-call(bf16[2048,768]{1,0:T(8,128)(2,1)} %bitcast.100, bf16[2048,768]{1,0:T(8,128)(2,1)} %all-gather.8.cloned.1.call-done.dy_ref, f32[2048,384]{1,0:T(8,128)} %get-tuple-element.29.cf_ref, ...), custom_call_target="tpu_custom_call" | custom-call | tf_op jit(solution)/shard_map/mlp/pallas_call | solution.py:311
  278.9 48.6 %attn_bwd.1 = (bf16[2048,768]{1,0:T(8,128)(2,1)}, f32[768,1152]{1,0:T(8,128)}, f32[384,768]{1,0:T(8,128)}, f32[8,768]{1,0:T(8,128)}, f32[1,1152]{1,0:T(1,128)}) custom-call(bf16[2048,768]{1,0:T(8,128)(2,1)} %bitcast.101, bf16[2048,768]{1,0:T(8,128)(2,1)} %all-gather.8.cloned.1.call-done.dy_ref, f32[2048,384]{1,0:T(8,128)} %get-tuple-element.29.cf_ref, ...), custom_call_target="tpu_custom_call" | custom-call | tf_op jit(solution)/shard_map/attn_bwd/pallas_call | solution.py:336
  328.8 3.3 copy.70
  336.8 3.6 multiply_reduce_fusion
  344.2 13.8 %all-reduce.3 = (f32[]{:T(128)}, f32[4,768]{1,0:T(4,128)}) all-reduce(f32[]{:T(128)S(6)} %add.125, f32[4,768]{1,0:T(4,128)} %pad_maximum_fusion.1), channel_id=1, replica_groups=mesh['dp'=8,'ctx'=4] {'ctx'}, use_global_device_ids=true, to_apply=%region_13.14 | all-reduce | flops 3073 | bytes 24584 | tf_op jit(solution)/shard_map/psum | solution.py:452
  361.4 16.6 %psum.30 = f32[]{:T(128)} all-reduce(f32[]{:T(128)} %sqrt.3), channel_id=1, replica_groups=mesh['dp'=8,'ctx'=4] {'dp'}, use_global_device_ids=true, to_apply=%region_16.17 | all-reduce | flops 1 | bytes 8 | tf_op jit(solution)/shard_map/psum | solution.py:457
  390.7 24.7 %reduce-scatter.19.cloned.1.call-done = bf16[96,576]{1,0:T(8,128)(2,1)} async-done(((bf16[768,576]{1,0:T(8,128)(2,1)}), bf16[96,576]{1,0:T(8,128)(2,1)}) %reduce-scatter.19.cloned.1.call-update) | async-done | bytes 110608 | tf_op jit(solution)/shard_map/reduce_scatter | solution.py:461
  415.5 4.3 all-to-all-start.2
  419.9 39.9 %psum.31 = f32[32,288]{1,0:T(8,128)S(1)} all-reduce(f32[32,288]{1,0:T(8,128)S(1)} %pad_maximum_fusion), channel_id=1, replica_groups=mesh['dp'=8,'ctx'=4] {'dp','ctx'}, use_global_device_ids=true, to_apply=%region_17.18 | all-reduce | flops 9216 | bytes 73728 | tf_op jit(solution)/shard_map/psum | solution.py:496
  460.4 3.3 all-to-all-start.3
  464.4 27.8 %reduce-scatter.13.cloned.1.call-done = bf16[24,768]{1,0:T(8,128)(2,1)} async-done(((bf16[192,768]{1,0:T(8,128)(2,1)}), bf16[24,768]{1,0:T(8,128)(2,1)}) %reduce-scatter.13.cloned.1.call-update) | async-done | bytes 36880 | tf_op jit(solution)/shard_map/reduce_scatter | solution.py:461
  492.1 4.1 collective-permute-start
  500.0 32.5 %reduce-scatter.17.cloned.1.call-done = bf16[96,768]{1,0:T(8,128)(2,1)} async-done(((bf16[768,768]{1,0:T(8,128)(2,1)}), bf16[96,768]{1,0:T(8,128)(2,1)}) %reduce-scatter.17.cloned.1.call-update) | async-done | bytes 147472 | tf_op jit(solution)/shard_map/reduce_scatter | solution.py:461
  535.7 59.3 %reduce-scatter.11.cloned.1.call-done = bf16[512,768]{1,0:T(8,128)(2,1)} async-done(((bf16[2048,768]{1,0:T(8,128)(2,1)}), bf16[512,768]{1,0:T(8,128)(2,1)}) %reduce-scatter.11.cloned.1.call-update) | async-done | bytes 786448 | tf_op jit(solution)/shard_map/reduce_scatter | solution.py:439
  596.9 60.8 %reduce-scatter.9.cloned.1.call-done = bf16[512,768]{1,0:T(8,128)(2,1)} async-done(((bf16[2048,768]{1,0:T(8,128)(2,1)}), bf16[512,768]{1,0:T(8,128)(2,1)}) %reduce-scatter.9.cloned.1.call-update) | async-done | bytes 786448 | tf_op jit(solution)/shard_map/reduce_scatter | solution.py:434
  (158 shorter events, 54.1 us)
Async XLA Ops:
  7.2 15.3 %copy-start.3 = (bf16[1,512,768]{2,1,0:T(8,128)(2,1)S(1)}, bf16[1,512,768]{2,1,0:T(8,128)(2,1)}, u32[]{:S(2)}) copy-start(bf16[1,512,768]{2,1,0:T(8,128)(2,1)} %param.19) | copy-start | bytes 2359300
  7.2 91.5 %all-gather.10.cloned.1.call-start = ((), (), s32[]{:S(2)}) async-start(), calls=%async_computation.11 | async-start | bytes 1216512 | tf_op jit(solution)/shard_map/all_gather | solution.py:407
  7.9 123.4 %all-gather.16.cloned.1.call-start = ((), (), s32[]{:S(2)}) async-start(), calls=%async_computation.19 | async-start | bytes 3932160 | tf_op jit(solution)/shard_map/all_gather | solution.py:397
  8.7 151.6 %all-gather.14.cloned.1.call-start = ((), (), s32[]{:S(2)}) async-start(), calls=%async_computation.13 | async-start | bytes 1327104 | tf_op jit(solution)/shard_map/all_gather | solution.py:406
  9.4 172.9 %all-gather.12.cloned.1.call-start = ((), (), s32[]{:S(2)}) async-start(), calls=%async_computation.12 | async-start | bytes 1327104 | tf_op jit(solution)/shard_map/all_gather | solution.py:405
  10.6 13.0 %copy-start.8 = (bf16[24,2304]{1,0:T(8,128)(2,1)S(1)}, bf16[24,2304]{1,0:T(8,128)(2,1)}, u32[]{:S(2)}) copy-start(bf16[24,2304]{1,0:T(8,128)(2,1)} %param.23) | copy-start | bytes 331780
  21.8 225.5 %all-gather.8.cloned.1.call-start = ((), (), s32[]{:S(2)}) async-start(), calls=%async_computation.10 | async-start | bytes 3932160 | tf_op jit(solution)/shard_map/all_gather | solution.py:398
  22.5 5.6 copy-start.15
  22.5 5.6 copy-start.16
  23.6 47.7 %copy-start.12 = (f32[9,64]{1,0:T(8,128)S(1)}, f32[9,64]{1,0:T(8,128)}, u32[]{:S(2)}) copy-start(f32[9,64]{1,0:T(8,128)} %constant.47.clone) | copy-start | bytes 6916
  24.7 50.7 %all-to-all-start = ((bf16[4,24,576]{2,1,0:T(8,128)(2,1)}), bf16[4,24,576]{2,1,0:T(8,128)(2,1)S(1)}, u32[]{:S(2)}, u32[]{:S(2)}) async-start(bf16[4,24,576]{2,1,0:T(8,128)(2,1)} %reshape.210), calls=%async_computation | async-start | bytes 245760 | tf_op jit(solution)/shard_map/all_to_all | solution.py:401
  28.1 387.4 %reduce-scatter.19.cloned.1.call-start = ((), (), s32[]{:S(2)}) async-start(), calls=%async_computation.20 | async-start | bytes 1105920 | tf_op jit(solution)/shard_map/reduce_scatter | solution.py:461
  382.3 78.1 %reduce-scatter.15.cloned.1.call-start = ((), (), s32[]{:S(2)}) async-start(), calls=%async_computation.17 | async-start | bytes 1327104 | tf_op jit(solution)/shard_map/reduce_scatter | solution.py:461
  383.8 108.3 %reduce-scatter.13.cloned.1.call-start = ((), (), s32[]{:S(2)}) async-start(), calls=%async_computation.16 | async-start | bytes 331776 | tf_op jit(solution)/shard_map/reduce_scatter | solution.py:461
  384.7 147.8 %reduce-scatter.17.cloned.1.call-start = ((), (), s32[]{:S(2)}) async-start(), calls=%async_computation.18 | async-start | bytes 1327104 | tf_op jit(solution)/shard_map/reduce_scatter | solution.py:461
  386.8 208.1 %reduce-scatter.11.cloned.1.call-start = ((), (), s32[]{:S(2)}) async-start(), calls=%async_computation.15 | async-start | bytes 3932160 | tf_op jit(solution)/shard_map/reduce_scatter | solution.py:439
  387.4 270.3 %reduce-scatter.9.cloned.1.call-start = ((), (), s32[]{:S(2)}) async-start(), calls=%async_computation.14 | async-start | bytes 3932160 | tf_op jit(solution)/shard_map/reduce_scatter | solution.py:434
  415.5 44.9 %all-to-all-start.2 = ((bf16[4,24,576]{2,1,0:T(8,128)(2,1)}), bf16[4,24,576]{2,1,0:T(8,128)(2,1)S(1)}, u32[]{:S(2)}, u32[]{:S(2)}) async-start(bf16[4,24,576]{2,1,0:T(8,128)(2,1)} %bitcast.119), calls=%async_computation.4 | async-start | bytes 245760 | tf_op jit(solution)/shard_map/all_to_all | solution.py:466
  460.4 200.2 %copy-start.23 = (f32[24]{0:T(128)}, f32[24]{0:T(128)S(1)}, u32[]{:S(2)}) copy-start(f32[24]{0:T(128)S(1)} %get-tuple-element.96) | copy-start | bytes 292
  460.4 73.7 %all-to-all-start.3 = ((bf16[4,24,768]{2,1,0:T(8,128)(2,1)}), bf16[4,24,768]{2,1,0:T(8,128)(2,1)S(1)}, u32[]{:S(2)}, u32[]{:S(2)}) async-start(bf16[4,24,768]{2,1,0:T(8,128)(2,1)} %bitcast.118), calls=%async_computation.7 | async-start | bytes 294912 | tf_op jit(solution)/shard_map/all_to_all | solution.py:466
  492.1 5.9 collective-permute-start
  534.4 123.4 %copy-start.4 = (bf16[1,512,768]{2,1,0:T(8,128)(2,1)S(1)}, bf16[1,512,768]{2,1,0:T(8,128)(2,1)}, u32[]{:S(2)}) copy-start(bf16[1,512,768]{2,1,0:T(8,128)(2,1)} %param.19) | copy-start | bytes 2359300
  534.4 123.3 %copy-start.14 = (pred[512]{0:T(512)(128)(4,1)S(1)}, pred[512]{0:T(512)(128)(4,1)}, u32[]{:S(2)}) copy-start(pred[512]{0:T(512)(128)(4,1)} %copy-done.13) | copy-start | bytes 1540
  595.0 62.8 %copy-start.5 = (bf16[512,768]{1,0:T(8,128)(2,1)S(1)}, bf16[512,768]{1,0:T(8,128)(2,1)}, u32[]{:S(2)}) copy-start(bf16[512,768]{1,0:T(8,128)(2,1)} %reduce-scatter.11.cloned.1.call-done) | copy-start | bytes 2359300
  (15 other events, 47.0 us)
Sparse Core Ops, SparseCore 0:
  10.8 56.8 all-gather.9
  69.3 62.0 all-gather.15
  133.2 23.1 all-gather.13
  158.2 24.0 all-gather.11
  184.2 63.0 all-gather.7
  382.4 33.0 reduce-scatter.18
  419.0 36.7 reduce-scatter.14
  459.5 32.5 reduce-scatter.12
  495.4 37.0 reduce-scatter.16
  534.8 60.1 reduce-scatter.10
  597.4 60.2 reduce-scatter.8

commit v2 on v1

v2 whole, which is shorter than its diff:
```python
import functools
import math

import jax
import jax.numpy as jnp
import numpy as np
from jax import lax
from jax.experimental import pallas as pl
from jax.experimental.pallas import tpu as pltpu
from jax.sharding import PartitionSpec as P

D = 768
HEADS = 12
HEAD_DIM = 64
ROT = 16
PAD = 128
eps_norm = 1e-05
neg_big = -1e30
root_half = math.sqrt(0.5)
inv_root_two_pi = 1.0 / math.sqrt(2.0 * math.pi)
f32 = jnp.float32
bf16 = jnp.bfloat16
VMEM_BYTES = 60 * 2**20


def dot(a, b, dims=((1,), (0,))):
    return lax.dot_general(a, b, (dims, ((), ())), preferred_element_type=f32)


def norm_parts(values):
    centered = values - jnp.mean(values, axis=-1, keepdims=True)
    row_var = jnp.mean(centered * centered, axis=-1, keepdims=True)
    inverse = lax.rsqrt(row_var + eps_norm)
    return centered * inverse, inverse


def turn(u, cosine, sine, first):
    partner = jnp.where(first, pltpu.roll(u, PAD - ROT // 2, 1), pltpu.roll(u, ROT // 2, 1))
    return u * cosine + partner * sine


def split3(v):
    hi = v.astype(bf16).astype(f32)
    mid = (v - hi).astype(bf16).astype(f32)
    low = (v - hi - mid).astype(bf16).astype(f32)
    return hi, mid, low


def fold(op, s):
    out = s[:, :PAD]
    for t in range(1, s.shape[1] // PAD):
        out = op(out, s[:, t * PAD : (t + 1) * PAD])
    return out


def attn_fwd_kernel(
    len_ref, x_ref, g_ref, b_ref, w_ref, wb_ref, cos_ref, sin_ref,
    q_ref, k_ref, v_ref, cf_ref, c_ref, w_scr, s_scr, q_scr, m_scr, l_scr, acc_scr,
):
    i = pl.program_id(0)
    nh = k_ref.shape[0]
    rows = x_ref.shape[0]
    length = len_ref[0]

    @pl.when(i == 0)
    def _():
        for h in range(3 * nh):
            w_scr[:, h * PAD : h * PAD + HEAD_DIM] = w_ref[:, h * HEAD_DIM : (h + 1) * HEAD_DIM]
            w_scr[:, h * PAD + HEAD_DIM : (h + 1) * PAD] = jnp.zeros((D, PAD - HEAD_DIM), bf16)

    xhat, unused = norm_parts(x_ref[...].astype(f32))
    a1 = (xhat * g_ref[...] + b_ref[...]).astype(bf16)
    cosine, sine = cos_ref[...], sin_ref[...]
    lane = lax.broadcasted_iota(jnp.int32, (rows, PAD), 1)
    first = lane < ROT // 2
    key_pos = i * rows + lax.broadcasted_iota(jnp.int32, (rows, PAD), 0)
    key_bias = jnp.where(key_pos < length, 0.0, neg_big)
    here = pl.ds(pl.multiple_of(i * rows, rows), rows)
    qkv = dot(a1, w_scr[...]) + wb_ref[...]
    for h in range(nh):
        q = turn(qkv[:, h * PAD : (h + 1) * PAD], cosine, sine, first) * HEAD_DIM**-0.5
        q_scr[h] = q.astype(bf16)
        k = turn(qkv[:, (nh + h) * PAD : (nh + h + 1) * PAD], cosine, sine, first)
        k_ref[h, here] = jnp.where(lane == HEAD_DIM, key_bias, k).astype(bf16)
        v_ref[h, here] = qkv[:, (2 * nh + h) * PAD : (2 * nh + h + 1) * PAD].astype(bf16)

    causal = lax.broadcasted_iota(jnp.int32, (rows, rows), 0) >= lax.broadcasted_iota(
        jnp.int32, (rows, rows), 1
    )
    for h in range(nh):
        s = dot(q_scr[h], k_ref[h, here], ((1,), (1,)))
        s = jnp.where(causal, s, neg_big)
        s_scr[h, i] = s
        m_scr[h] = fold(jnp.maximum, s)

    def scores(j, carry):
        there = pl.ds(pl.multiple_of(j * rows, rows), rows)
        for h in range(nh):
            s = dot(q_scr[h], k_ref[h, there], ((1,), (1,)))
            s_scr[h, j] = s
            m_scr[h] = jnp.maximum(m_scr[h], fold(jnp.maximum, s))
        return carry

    lax.fori_loop(0, i, scores, 0)
    for h in range(nh):
        m_scr[h] = jnp.broadcast_to(jnp.max(m_scr[h], axis=-1, keepdims=True), (rows, PAD))
        l_scr[h] = jnp.zeros((rows, PAD), f32)
        acc_scr[h] = jnp.zeros((rows, PAD), f32)

    def weigh(j, carry):
        there = pl.ds(pl.multiple_of(j * rows, rows), rows)
        for h in range(nh):
            p = jnp.exp(s_scr[h, j] - m_scr[h][:, :1])
            l_scr[h] += fold(jnp.add, p)
            acc_scr[h] += dot(p.astype(bf16), v_ref[h, there])
        return carry

    lax.fori_loop(0, i + 1, weigh, 0)
    for h in range(nh):
        total = jnp.sum(l_scr[h], axis=-1, keepdims=True)
        context = acc_scr[h] / total
        cf_ref[:, h * PAD : (h + 1) * PAD] = context
        c_ref[:, h * HEAD_DIM : (h + 1) * HEAD_DIM] = context[:, :HEAD_DIM].astype(bf16)
        hi, mid, low = split3(-(m_scr[h][:, :1] + jnp.log(total)))
        q = q_scr[h].astype(f32)
        q = jnp.where(lane == HEAD_DIM + 1, hi, q)
        q = jnp.where(lane == HEAD_DIM + 2, mid, q)
        q = jnp.where(lane == HEAD_DIM + 3, low, q)
        q_ref[h] = q.astype(bf16)


def squares_of(m):
    return jnp.sum(jnp.sum(m * m, axis=0, keepdims=True), axis=1, keepdims=True)


def mlp_kernel(
    x_ref, dy_ref, c_ref, g_ref, b_ref, wo_ref, w1_ref, b1_ref, w2_ref,
    part_ref, u_ref, dw1_ref, dw2_ref, vec_ref, dw1_scr, dw2_scr,
):
    i = pl.program_id(0)
    xhat, unused = norm_parts(x_ref[...].astype(f32))
    gain = g_ref[...]
    a2 = (xhat * gain + b_ref[...]).astype(bf16)
    z = dot(a2, w1_ref[...]) + b1_ref[...]
    cdf = 0.5 * (1.0 + lax.erf(z * root_half))
    hidden = (z * cdf).astype(bf16)
    part = dot(hidden, w2_ref[...]) + dot(c_ref[...], wo_ref[...])
    part_ref[...] = part.astype(part_ref.dtype)
    dy = dy_ref[...]
    slope = cdf + z * jnp.exp(-0.5 * z * z) * inv_root_two_pi
    dz = (dot(dy, w2_ref[...], ((1,), (1,))) * slope).astype(bf16)
    da2 = dot(dz, w1_ref[...], ((1,), (1,)))
    u_ref[...] = (da2 * gain).astype(u_ref.dtype)

    @pl.when(i == 0)
    def _():
        dw1_scr[...] = jnp.zeros_like(dw1_scr)
        dw2_scr[...] = jnp.zeros_like(dw2_scr)
        vec_ref[...] = jnp.zeros_like(vec_ref)

    dw1_scr[...] += dot(a2, dz, ((0,), (0,)))
    dw2_scr[...] += dot(hidden, dy, ((0,), (0,)))
    vec_ref[2:3] += jnp.sum(da2 * xhat, axis=0, keepdims=True)
    vec_ref[3:4] += jnp.sum(da2, axis=0, keepdims=True)
    vec_ref[4:5] += jnp.sum(dz.astype(f32), axis=0, keepdims=True)
    vec_ref[6:7] += jnp.sum(dy.astype(f32), axis=0, keepdims=True)

    @pl.when(i == pl.num_programs(0) - 1)
    def _():
        dw1_ref[...] = dw1_scr[...].astype(bf16)
        dw2_ref[...] = dw2_scr[...].astype(bf16)
        vec_ref[7:8, 0:1] = squares_of(dw1_scr[...]) + squares_of(dw2_scr[...])


def attn_bwd_kernel(
    x_ref, dy_ref, cf_ref, c_ref, u_in_ref, q_ref, k_ref, v_ref, g_ref, b_ref, w_ref, wo_ref,
    cos_ref, sin_ref, vec_in_ref,
    u_ref, dw_ref, dwo_ref, vec_ref,
    wo_scr, dk_scr, dv_scr, dq_scr, dc_scr, dqkv_scr, dw_scr, dwo_scr,
):
    step = pl.program_id(0)
    blocks = pl.num_programs(0)
    i = blocks - 1 - step
    nh = k_ref.shape[0]
    rows = x_ref.shape[0]
    wide = 3 * nh * HEAD_DIM
    lane = lax.broadcasted_iota(jnp.int32, (rows, PAD), 1)
    first = lane < ROT // 2
    here = pl.ds(pl.multiple_of(i * rows, rows), rows)

    @pl.when(step == 0)
    def _():
        dk_scr[...] = jnp.zeros_like(dk_scr)
        dv_scr[...] = jnp.zeros_like(dv_scr)
        dw_scr[...] = jnp.zeros_like(dw_scr)
        dwo_scr[...] = jnp.zeros_like(dwo_scr)
        vec_ref[...] = vec_in_ref[...]
        for h in range(nh):
            wo_scr[h * PAD : h * PAD + HEAD_DIM] = wo_ref[h * HEAD_DIM : (h + 1) * HEAD_DIM]
            wo_scr[h * PAD + HEAD_DIM : (h + 1) * PAD] = jnp.zeros((PAD - HEAD_DIM, D), bf16)

    dy = dy_ref[...]
    dc_all = dot(dy, wo_scr[...], ((1,), (1,))).astype(bf16)
    for h in range(nh):
        dc = dc_all[:, h * PAD : (h + 1) * PAD].astype(f32)
        delta = jnp.sum(dc * cf_ref[:, h * PAD : (h + 1) * PAD], axis=-1, keepdims=True)
        hi, mid, low = split3(-delta)
        dc = jnp.where(lane == HEAD_DIM, hi, dc)
        dc = jnp.where(lane == HEAD_DIM + 1, mid, dc)
        dc = jnp.where(lane == HEAD_DIM + 2, low, dc)
        dc_scr[h] = dc.astype(bf16)

    causal = lax.broadcasted_iota(jnp.int32, (rows, rows), 0) <= lax.broadcasted_iota(
        jnp.int32, (rows, rows), 1
    )

    def block(j, diagonal):
        there = pl.ds(pl.multiple_of(j * rows, rows), rows)
        for h in range(nh):
            k = k_ref[h, there]
            q = q_ref[h]
            dc = dc_scr[h]
            pt = jnp.exp(dot(k, q, ((1,), (1,))))
            if diagonal:
                pt = jnp.where(causal, pt, 0.0)
            dpt = dot(v_ref[h, there], dc, ((1,), (1,)))
            dst = (pt * dpt).astype(bf16)
            dv_scr[h, there] += dot(pt.astype(bf16), dc)
            dk_scr[h, there] += dot(dst, q)
            dq = dot(dst, k, ((0,), (0,)))
            if diagonal:
                dq_scr[h] = dq
            else:
                dq_scr[h] += dq

    block(i, True)

    def off(j, carry):
        block(j, False)
        return carry

    lax.fori_loop(0, i, off, 0)
    cosine, sine = cos_ref[...], -sin_ref[...]
    for h in range(nh):
        dq = turn(dq_scr[h], cosine, sine, first) * HEAD_DIM**-0.5
        dk = turn(dk_scr[h, here], cosine, sine, first)
        for at, part in ((h, dq), (nh + h, dk), (2 * nh + h, dv_scr[h, here])):
            dqkv_scr[:, at * HEAD_DIM : (at + 1) * HEAD_DIM] = part[:, :HEAD_DIM].astype(bf16)
    dqkv = dqkv_scr[...]
    xhat, unused = norm_parts(x_ref[...].astype(f32))
    gain = g_ref[...]
    a1 = (xhat * gain + b_ref[...]).astype(bf16)
    da1 = dot(dqkv, w_ref[...], ((1,), (1,)))
    u_ref[...] = (u_in_ref[...].astype(f32) + da1 * gain).astype(u_ref.dtype)
    dw_scr[...] += dot(a1, dqkv, ((0,), (0,)))
    dwo_scr[...] += dot(c_ref[...], dy, ((0,), (0,)))
    vec_ref[0:1] += jnp.sum(da1 * xhat, axis=0, keepdims=True)
    vec_ref[1:2] += jnp.sum(da1, axis=0, keepdims=True)
    vec_ref[5:6, :wide] += jnp.sum(dqkv.astype(f32), axis=0, keepdims=True)

    @pl.when(step == blocks - 1)
    def _():
        dw_ref[...] = dw_scr[...].astype(bf16)
        dwo_ref[...] = dwo_scr[...].astype(bf16)
        vec_ref[7:8, 0:1] += squares_of(dw_scr[...]) + squares_of(dwo_scr[...])


def whole(shape):
    return pl.BlockSpec(shape, lambda i: (0,) * len(shape), pipeline_mode=pl.Buffered(1))


def sds(shape, dtype):
    return jax.ShapeDtypeStruct(shape, dtype)


def params():
    return pltpu.CompilerParams(
        dimension_semantics=("arbitrary",), vmem_limit_bytes=VMEM_BYTES
    )


def attn_fwd(length, x, g1, b1, w, wb, cosine, sine, nh, rows):
    t = x.shape[0]
    lanes = pl.BlockSpec((rows, PAD), lambda i: (i, 0))
    return pl.pallas_call(
        attn_fwd_kernel,
        grid=(t // rows,),
        out_shape=(
            sds((nh, t, PAD), bf16), sds((nh, t, PAD), bf16), sds((nh, t, PAD), bf16),
            sds((t, nh * PAD), f32), sds((t, nh * HEAD_DIM), bf16),
        ),
        in_specs=[
            pl.BlockSpec(memory_space=pltpu.SMEM),
            pl.BlockSpec((rows, D), lambda i: (i, 0)),
            whole((1, D)), whole((1, D)), whole(w.shape), whole(wb.shape), lanes, lanes,
        ],
        out_specs=(
            pl.BlockSpec((nh, rows, PAD), lambda i: (0, i, 0)),
            whole((nh, t, PAD)), whole((nh, t, PAD)),
            pl.BlockSpec((rows, nh * PAD), lambda i: (i, 0)),
            pl.BlockSpec((rows, nh * HEAD_DIM), lambda i: (i, 0)),
        ),
        scratch_shapes=[
            pltpu.VMEM((D, 3 * nh * PAD), bf16),
            pltpu.VMEM((nh, t // rows, rows, rows), f32),
            pltpu.VMEM((nh, rows, PAD), bf16),
            pltpu.VMEM((nh, rows, PAD), f32),
            pltpu.VMEM((nh, rows, PAD), f32),
            pltpu.VMEM((nh, rows, PAD), f32),
        ],
        compiler_params=params(),
        name="attn_fwd",
    )(length, x, g1, b1, w, wb, cosine, sine)


def mlp(x, dy, c, g2, b2, wo, w1, bias1, w2, rows):
    t = x.shape[0]
    ff = w1.shape[1]
    row = pl.BlockSpec((rows, D), lambda i: (i, 0))
    return pl.pallas_call(
        mlp_kernel,
        grid=(t // rows,),
        out_shape=(
            sds((t, D), bf16), sds((t, D), f32), sds((D, ff), bf16), sds((ff, D), bf16),
            sds((8, D), f32),
        ),
        in_specs=[
            row, row, pl.BlockSpec((rows, c.shape[1]), lambda i: (i, 0)),
            whole((1, D)), whole((1, D)), whole(wo.shape), whole(w1.shape), whole((1, ff)),
            whole(w2.shape),
        ],
        out_specs=(row, row, whole((D, ff)), whole((ff, D)), whole((8, D))),
        scratch_shapes=[pltpu.VMEM((D, ff), f32), pltpu.VMEM((ff, D), f32)],
        compiler_params=params(),
        name="mlp",
    )(x, dy, c, g2, b2, wo, w1, bias1, w2)


def attn_bwd(x, dy, cf, c, u_in, q, k, v, g1, b1, w, wo, cosine, sine, vec, rows):
    t = x.shape[0]
    nh = q.shape[0]
    n = t // rows
    wide = w.shape[1]
    row = pl.BlockSpec((rows, D), lambda i: (n - 1 - i, 0))
    lanes = pl.BlockSpec((rows, PAD), lambda i: (n - 1 - i, 0))
    return pl.pallas_call(
        attn_bwd_kernel,
        grid=(n,),
        out_shape=(
            sds((t, D), bf16), sds((D, wide), bf16), sds((nh * HEAD_DIM, D), bf16),
            sds((8, D), f32),
        ),
        in_specs=[
            row, row, pl.BlockSpec((rows, nh * PAD), lambda i: (n - 1 - i, 0)),
            pl.BlockSpec((rows, nh * HEAD_DIM), lambda i: (n - 1 - i, 0)), row,
            pl.BlockSpec((nh, rows, PAD), lambda i: (0, n - 1 - i, 0)),
            whole(k.shape), whole(v.shape), whole((1, D)), whole((1, D)), whole(w.shape),
            whole(wo.shape), lanes, lanes, whole((8, D)),
        ],
        out_specs=(row, whole((D, wide)), whole((nh * HEAD_DIM, D)), whole((8, D))),
        scratch_shapes=[
            pltpu.VMEM((nh * PAD, D), bf16),
            pltpu.VMEM((nh, t, PAD), f32),
            pltpu.VMEM((nh, t, PAD), f32),
            pltpu.VMEM((nh, rows, PAD), f32),
            pltpu.VMEM((nh, rows, PAD), bf16),
            pltpu.VMEM((rows, wide), bf16),
            pltpu.VMEM((D, wide), f32),
            pltpu.VMEM((nh * HEAD_DIM, D), f32),
        ],
        compiler_params=params(),
        name="attn_bwd",
    )(x, dy, cf, c, u_in, q, k, v, g1, b1, w, wo, cosine, sine, vec)


def tables(t):
    inv_freqs = np.exp(np.arange(ROT // 2, dtype=np.float32) * np.float32(-2.0 * math.log(10000.0) / ROT))
    angles = np.arange(t, dtype=np.float32)[:, None] * inv_freqs.astype(np.float32)[None, :]
    cosine = np.ones((t, PAD), np.float32)
    sine = np.zeros((t, PAD), np.float32)
    half = ROT // 2
    cosine[:, :half] = cosine[:, half:ROT] = np.cos(angles)
    sine[:, :half] = -np.sin(angles)
    sine[:, half:ROT] = np.sin(angles)
    return jnp.asarray(cosine), jnp.asarray(sine)


MESH = pl.DeviceIdType.MESH
AX = ("dp", "ctx")
CHUNKS = 2


def place():
    d, z = lax.axis_index("dp"), lax.axis_index("ctx")
    c, pair, g = lax.rem(d, 2), lax.div(d, 2), lax.div(z, 2)
    y = lax.rem(g + lax.rem(z, 2), 2)
    return d, z, c, pair, g, y


def mirror(m, g):
    return jnp.where(g == 0, m, 3 - m)


def rcopy(src, dst, ss, rs, device):
    return pltpu.make_async_remote_copy(
        src_ref=src, dst_ref=dst, send_sem=ss, recv_sem=rs, device_id=device, device_id_type=MESH
    )


def column_peer(pair, c, z, o):
    m = lax.rem(c * 4 + z + o, 8)
    return lax.div(m, 4), lax.rem(m, 4)


def barrier_all(np_, d, z, c, pair):
    bar = pltpu.get_barrier_semaphore()
    for o in range(1, 8):
        c2, z2 = column_peer(pair, c, z, o)
        pl.semaphore_signal(bar, inc=1, device_id=(2 * pair + c2, z2), device_id_type=MESH)
    for o in range(1, np_):
        pl.semaphore_signal(
            bar, inc=1, device_id=(2 * lax.rem(pair + o, np_) + c, z), device_id_type=MESH
        )
    pl.semaphore_wait(bar, 7 + np_ - 1)


class Spread:
    def __init__(self, own, out, ls, ss, rs):
        self.own, self.out, self.ls, self.ss, self.rs = own, out, ls, ss, rs
        self.rows = out.shape[1] // CHUNKS
        d, z, c, pair, g, y = place()
        self.d, self.z, self.c, self.g, self.y = d, z, c, g, y
        self.prim = c == g
        self.sib = (d + 1 - 2 * c, z)
        self.partner = (d, z + 1 - 2 * lax.rem(z, 2))
        self.far = (d, 1 + c)

    def cut(self, ref, j):
        return ref.at[pl.ds(j * self.rows, self.rows)]

    def send(self, q, j, way, device, src=None):
        src = self.cut(self.out.at[q], j) if src is None else src
        return rcopy(
            src, self.cut(self.out.at[q], j), self.ss.at[way, q, j], self.rs.at[q, j], device
        )

    def start(self):
        own = [self.cut(self.own, j) for j in range(CHUNKS)]

        @pl.when(self.prim)
        def _():
            pltpu.make_async_copy(self.own, self.out.at[self.z], self.ls).start()
            for j in range(CHUNKS):
                self.send(self.z, j, 0, self.partner, own[j]).start()
            for j in range(CHUNKS):
                self.send(self.z, j, 1, self.sib, own[j]).start()

        @pl.when(jnp.logical_not(self.prim))
        def _():
            for j in range(CHUNKS):
                self.send(self.z, j, 0, self.far, own[j]).start()

    def wait_recv(self, q, j):
        self.send(q, j, 0, self.sib).wait_recv()

    def finish(self):
        far = (mirror(2, self.g), mirror(3, self.g))
        end, mid = mirror(0, self.g), mirror(1, self.g)

        @pl.when(jnp.logical_and(self.prim, self.y == 1))
        def _():
            for j in range(CHUNKS):
                for q in far:
                    self.wait_recv(q, j)
                    self.send(q, j, 0, self.partner).start()
                    self.send(q, j, 1, self.sib).start()
            for j in range(CHUNKS):
                self.wait_recv(end, j)
                self.send(end, j, 1, self.sib).start()
            for j in range(CHUNKS):
                for q in far + (mid,):
                    self.send(q, j, 0, self.partner).wait_send()

        @pl.when(jnp.logical_and(self.prim, self.y == 0))
        def _():
            for q, j in [(mid, j) for j in range(CHUNKS)] + [
                (q, j) for j in range(CHUNKS) for q in far
            ]:
                self.wait_recv(q, j)
                self.send(q, j, 1, self.sib).start()
            for j in range(CHUNKS):
                self.send(end, j, 0, self.partner).wait_send()

        @pl.when(self.prim)
        def _():
            pltpu.make_async_copy(self.own, self.out.at[self.z], self.ls).wait()
            for q in range(4):
                for j in range(CHUNKS):
                    self.send(q, j, 1, self.sib).wait_send()

        @pl.when(jnp.logical_not(self.prim))
        def _():
            for q in range(4):
                for j in range(CHUNKS):
                    self.wait_recv(q, j)
            for j in range(CHUNKS):
                self.send(self.z, j, 0, self.far).wait_send()


class Weights:
    def __init__(self, np_, sliced, w2, wo, ls, ss, rs):
        self.np_, self.sliced, self.w2, self.wo = np_, sliced, w2, wo
        self.ls, self.ss, self.rs = ls, ss, rs
        self.here = place()

    def first(self, s, o):
        d, z, c, pair, g, y = self.here
        src, out, by_slice = self.sliced[s]
        if o == 0:
            return pltpu.make_async_copy(
                src.at[2 * y + c] if by_slice else src, out.at[pair, c, z], self.ls.at[s]
            )
        c2, z2 = column_peer(pair, c, z, o)
        y2 = lax.rem(lax.div(z2, 2) + lax.rem(z2, 2), 2)
        return rcopy(
            src.at[2 * y2 + c2] if by_slice else src, out.at[pair, c, z],
            self.ss.at[s, o - 1], self.rs.at[s, o - 1], (2 * pair + c2, z2),
        )

    def second(self, s, o):
        d, z, c, pair, g, y = self.here
        out = self.sliced[s][1] if s < len(self.sliced) else self.w2[1]
        return rcopy(
            out.at[pair], out.at[pair], self.ss.at[s, 7 + o - 1], self.rs.at[s, 7 + o - 1],
            (2 * lax.rem(pair + o, self.np_) + c, z),
        )

    def start(self):
        d, z, c, pair, g, y = self.here
        n = len(self.sliced)
        for s in range(n):
            for o in range(8):
                self.first(s, o).start()
        if self.w2 is not None:
            for o in range(2):
                self.w2_first(o).start()
        if self.wo is not None:
            self.wo_first(lambda cp: cp.start())

    def w2_first(self, o):
        d, z, c, pair, g, y = self.here
        src, out = self.w2
        n = len(self.sliced)
        if o == 0:
            return pltpu.make_async_copy(src, out.at[pair, g], self.ls.at[n])
        return rcopy(src, out.at[pair, g], self.ss.at[n, 0], self.rs.at[n, 0], (d, 3 - z))

    def wo_parts(self):
        d, z, c, pair, g, y = self.here
        per = self.np_ // 4
        owner = lax.div(pair, per)
        return per, owner, lax.rem(owner, 2), lax.div(owner, 2)

    def wo_first(self, do, sending=True):
        d, z, c, pair, g, y = self.here
        src, out = self.wo
        n = len(self.sliced) + 1
        per, owner, c_to, y_to = self.wo_parts()
        slot = out.at[lax.rem(pair, per), c, z]
        for t in range(2):
            z_to = jnp.where(t == 0, y_to, 3 - y_to)
            mine = jnp.logical_and(c == c_to, z == z_to)

            @pl.when(mine)
            def _():
                do(pltpu.make_async_copy(src, slot, self.ls.at[n]))

            @pl.when(jnp.logical_not(mine))
            def _():
                cp = rcopy(
                    src, slot, self.ss.at[n, t], self.rs.at[n, c * 4 + z], (2 * pair + c_to, z_to)
                )
                do(cp)

    def wo_second(self, o):
        d, z, c, pair, g, y = self.here
        per = self.np_ // 4
        out = self.wo[1]
        n = len(self.sliced) + 1
        slot = out.at[lax.rem(pair, per)]
        return rcopy(
            slot, slot, self.ss.at[n, 8 + o - 1], self.rs.at[n, 8 + o - 1],
            (2 * lax.rem(pair + o, self.np_) + c, z),
        )

    def between(self, s):
        self.first(s, 0).wait()
        for o in range(1, 8):
            self.first(s, o).wait_recv()
        for o in range(1, self.np_):
            self.second(s, o).start()

    def between_w2(self):
        n = len(self.sliced)
        self.w2_first(0).wait()
        self.w2_first(1).wait_recv()
        for o in range(1, self.np_):
            self.second(n, o).start()

    def between_wo(self):
        d, z, c, pair, g, y = self.here
        n = len(self.sliced) + 1
        per, owner, c_to, y_to = self.wo_parts()

        @pl.when(owner == 2 * y + c)
        def _():
            for c2 in range(2):
                for z2 in range(4):
                    own = jnp.logical_and(c == c2, z == z2)

                    @pl.when(jnp.logical_not(own))
                    def _():
                        slot = self.wo[1].at[0, c2, z2]
                        rcopy(
                            slot, slot, self.ss.at[n, 0], self.rs.at[n, c2 * 4 + z2], (d + 1 - 2 * c, z)
                        ).wait_recv()
            pltpu.make_async_copy(
                self.wo[0], self.wo[1].at[0, c, z], self.ls.at[n]
            ).wait()
            for o in range(1, self.np_):
                self.wo_second(o).start()

    def finish(self, s):
        for o in range(1, 8):
            self.first(s, o).wait_send()
        for o in range(1, self.np_):
            self.second(s, o).wait()

    def finish_w2(self):
        n = len(self.sliced)
        self.w2_first(1).wait_send()
        for o in range(1, self.np_):
            self.second(n, o).wait()

    def finish_wo(self):
        d, z, c, pair, g, y = self.here
        n = len(self.sliced) + 1
        per, owner, c_to, y_to = self.wo_parts()
        for t in range(2):
            z_to = jnp.where(t == 0, y_to, 3 - y_to)

            @pl.when(jnp.logical_not(jnp.logical_and(c == c_to, z == z_to)))
            def _():
                rcopy(
                    self.wo[0], self.wo[1].at[0, c, z], self.ss.at[n, t], self.rs.at[n, 0], (d + 1 - 2 * c, z)
                ).wait_send()

        @pl.when(owner == 2 * y + c)
        def _():
            for o in range(1, self.np_):
                self.wo_second(o).wait_send()

        for o in range(1, self.np_):
            source = lax.div(lax.rem(pair + self.np_ - o, self.np_), per)

            @pl.when(source == 2 * y + c)
            def _():
                self.wo_second(o).wait_recv()


def gather_kernel(
    np_, x, dy, wq, w1, w2, wo, vec, xg, dyg, wqg, w1g, w2g, wog, vecg,
    ls_x, ss_x, rs_x, ls_dy, ss_dy, rs_dy, ls_w, ss_w, rs_w,
):
    d, z, c, pair, g, y = place()
    barrier_all(np_, d, z, c, pair)
    sx = Spread(x, xg, ls_x, ss_x, rs_x)
    sdy = Spread(dy, dyg, ls_dy, ss_dy, rs_dy)
    w = Weights(
        np_, [(vec, vecg, False), (wq, wqg, True), (w1, w1g, True)], (w2, w2g), (wo, wog),
        ls_w, ss_w, rs_w,
    )
    w.start()
    sx.start()
    for s in range(3):
        w.between(s)
    w.between_wo()
    w.between_w2()
    sx.finish()
    sdy.start()
    sdy.finish()
    for s in range(3):
        w.finish(s)
    w.finish_wo()
    w.finish_w2()


def spread_sems():
    return [
        pltpu.SemaphoreType.DMA,
        pltpu.SemaphoreType.DMA((2, 4, CHUNKS)),
        pltpu.SemaphoreType.DMA((4, CHUNKS)),
    ]


def gather(np_, x, dy, wq, w1, w2, wo, vec, collective_id=1):
    rows = x.shape[0]
    any_ = pl.BlockSpec(memory_space=pl.ANY)
    outs = (
        sds((4, rows, D), bf16), sds((4, rows, D), bf16),
        sds((np_, 2, 4) + wq.shape[1:], bf16), sds((np_, 2, 4) + w1.shape[1:], bf16),
        sds((np_, 2) + w2.shape, bf16), sds((np_ // 4, 2, 4) + wo.shape, bf16),
        sds((np_, 2, 4) + vec.shape, bf16),
    )
    return pl.pallas_call(
        functools.partial(gather_kernel, np_),
        out_shape=outs,
        in_specs=[any_] * 7,
        out_specs=(any_,) * 7,
        scratch_shapes=spread_sems() + spread_sems() + [
            pltpu.SemaphoreType.DMA((5,)),
            pltpu.SemaphoreType.DMA((5, 8 + np_)),
            pltpu.SemaphoreType.DMA((5, 8 + np_)),
        ],
        compiler_params=pltpu.CompilerParams(
            collective_id=collective_id, has_side_effects=True, vmem_limit_bytes=VMEM_BYTES
        ),
        name="gather",
    )(x, dy, wq, w1, w2, wo, vec)


PIECES = 4


class Reduce:
    def __init__(self, part, out, extra, bufs, ls, ss, rs):
        self.part, self.out, self.extra = part, out, extra
        self.from_sib, self.from_far, self.to_far, self.mine, self.done = bufs
        self.ls, self.ss, self.rs = ls, ss, rs
        d, z, c, pair, g, y = place()
        self.role = jnp.where(c == g, 0, 1)
        self.y = y
        self.sib = (d + 1 - 2 * c, z)
        self.partner = (d, z + 1 - 2 * lax.rem(z, 2))
        self.q_here = mirror(2 * y + self.role, g)
        self.q_there = mirror(2 * (1 - y) + self.role, g)
        self.sib_here = mirror(2 * y + 1 - self.role, g)
        self.sib_there = mirror(2 * (1 - y) + 1 - self.role, g)
        self.owner = (2 * pair + g, self.q_here)
        self.self_owner = jnp.logical_and(self.role == 0, y == 0)
        self.self_source = jnp.where(c == 0, z, 3 - z) == 0
        self.rows = self.out.shape[0] // PIECES

    def rows_of(self, j):
        return pl.ds(j * self.rows, self.rows)

    def to_sib(self, t, j):
        q = self.sib_there if t == 0 else self.sib_here
        r = self.rows_of(j)
        return rcopy(
            self.part.at[q, r], self.from_sib.at[t, r], self.ss.at[t, j], self.rs.at[t, j], self.sib
        )

    def load(self, t):
        q = self.q_there if t == 0 else self.q_here
        return pltpu.make_async_copy(self.part.at[q], self.mine.at[t], self.ls.at[t])

    def load_extra(self, e):
        src, dst = self.extra[e]
        return pltpu.make_async_copy(src.at[self.q_here], dst, self.ls.at[2 + e])

    def across(self, j):
        r = self.rows_of(j)
        return rcopy(
            self.to_far.at[r], self.from_far.at[r], self.ss.at[2, j], self.rs.at[2, j], self.partner
        )

    def home(self, j):
        r = self.rows_of(j)
        return rcopy(
            self.done.at[r], self.out.at[r], self.ss.at[3, j], self.rs.at[3, j], self.owner
        )

    def keep(self):
        return pltpu.make_async_copy(self.done, self.out, self.ls.at[4])

    def start(self):
        for t in range(2):
            for j in range(PIECES):
                self.to_sib(t, j).start()
        for t in range(2):
            self.load(t).start()
        for e in range(len(self.extra)):
            self.load_extra(e).start()

    def add_near(self):
        self.load(0).wait()
        for j in range(PIECES):
            r = self.rows_of(j)
            self.to_sib(0, j).wait_recv()
            total = self.mine[0, r].astype(f32) + self.from_sib[0, r].astype(f32)
            self.to_far[r] = total.astype(bf16)
            self.across(j).start()
        self.load(1).wait()
        for e in range(len(self.extra)):
            self.load_extra(e).wait()

    def add_far(self, finish):
        for j in range(PIECES):
            r = self.rows_of(j)
            self.to_sib(1, j).wait_recv()
            self.across(j).wait_recv()
            total = self.mine[1, r].astype(f32) + self.from_sib[1, r].astype(f32)
            total = total + self.from_far[r].astype(f32)
            self.done[r] = finish(total, r).astype(bf16)

            @pl.when(jnp.logical_not(self.self_owner))
            def _():
                self.home(j).start()

    def finish(self):
        @pl.when(self.self_owner)
        def _():
            self.keep().start()
            self.keep().wait()

        for j in range(PIECES):
            @pl.when(jnp.logical_not(self.self_source))
            def _():
                self.home(j).wait_recv()

        for j in range(PIECES):
            self.to_sib(0, j).wait_send()
            self.to_sib(1, j).wait_send()
            self.across(j).wait_send()

            @pl.when(jnp.logical_not(self.self_owner))
            def _():
                self.home(j).wait_send()


def reduce_scratch(rows, extras):
    return [
        pltpu.VMEM((2, rows, D), bf16), pltpu.VMEM((rows, D), bf16), pltpu.VMEM((rows, D), bf16),
        pltpu.VMEM((2, rows, D), bf16), pltpu.VMEM((rows, D), bf16),
    ] + [pltpu.VMEM((rows, D), bf16)] * extras + [
        pltpu.SemaphoreType.DMA((5,)),
        pltpu.SemaphoreType.DMA((4, PIECES)),
        pltpu.SemaphoreType.DMA((4, PIECES)),
    ]


def reduce_out_kernel(
    np_, part, xg, bias, out, from_sib, from_far, to_far, mine, done, xq, ls, ss, rs,
):
    d, z, c, pair, g, y = place()
    barrier_all(np_, d, z, c, pair)
    red = Reduce(
        part, out, [(xg, xq)], (from_sib, from_far, to_far, mine, done), ls, ss, rs
    )
    red.start()
    red.add_near()
    red.add_far(lambda total, r: xq[r].astype(f32) + bias[...] + total)
    red.finish()


def reduce_out(np_, part, xg, bias, collective_id=2):
    rows = part.shape[1]
    any_ = pl.BlockSpec(memory_space=pl.ANY)
    return pl.pallas_call(
        functools.partial(reduce_out_kernel, np_),
        out_shape=sds((rows, D), bf16),
        in_specs=[any_, any_, pl.BlockSpec(memory_space=pltpu.VMEM)],
        out_specs=any_,
        scratch_shapes=reduce_scratch(rows, 1),
        compiler_params=pltpu.CompilerParams(
            collective_id=collective_id, has_side_effects=True, vmem_limit_bytes=VMEM_BYTES
        ),
        name="reduce_out",
    )(part, xg, bias)


class Swap:
    def __init__(self, np_, arrays, wo, ls, ss, rs):
        self.np_, self.arrays, self.wo, self.ls, self.ss, self.rs = np_, arrays, wo, ls, ss, rs
        self.here = place()

    def copy(self, s, o):
        d, z, c, pair, g, y = self.here
        src, dst = self.arrays[s]
        to = lax.rem(pair + o, self.np_)
        if o == 0:
            return pltpu.make_async_copy(src.at[pair], dst.at[pair], self.ls.at[s])
        return rcopy(
            src.at[to], dst.at[pair], self.ss.at[s, o], self.rs.at[s, o], (2 * to + c, z)
        )

    def copy_wo(self, o):
        d, z, c, pair, g, y = self.here
        src, dst = self.wo
        n = len(self.arrays)
        per = self.np_ // 4
        to = lax.rem(pair + o, self.np_)
        if o == 0:
            return pltpu.make_async_copy(src.at[lax.rem(pair, per)], dst.at[pair], self.ls.at[n])
        return rcopy(
            src.at[lax.rem(to, per)], dst.at[pair], self.ss.at[n, o], self.rs.at[n, o],
            (2 * to + c, z),
        )

    def collects(self, pair2):
        d, z, c, pair, g, y = self.here
        return lax.div(pair2, self.np_ // 4) == 2 * y + c

    def start(self):
        d, z, c, pair, g, y = self.here
        for s in range(len(self.arrays)):
            for o in range(1, self.np_):
                self.copy(s, o).start()
            self.copy(s, 0).start()
        if self.wo is not None:
            for o in range(self.np_):
                @pl.when(self.collects(lax.rem(pair + o, self.np_)))
                def _():
                    self.copy_wo(o).start()

    def finish(self):
        d, z, c, pair, g, y = self.here
        for s in range(len(self.arrays)):
            for o in range(self.np_):
                self.copy(s, o).wait()
        if self.wo is not None:
            for o in range(self.np_):
                @pl.when(self.collects(lax.rem(pair + o, self.np_)))
                def _():
                    if o == 0:
                        self.copy_wo(o).wait()
                    else:
                        self.copy_wo(o).wait_send()

                if o > 0:
                    @pl.when(self.collects(pair))
                    def _():
                        self.copy_wo(o).wait_recv()


def group_peer(o):
    d, z, c, pair, g, y = place()
    c2 = 1 - c if o % 2 else c
    z2 = z + 1 - 2 * lax.rem(z, 2) if o // 2 else z
    return 2 * pair + c2, z2


class Group:
    def __init__(self, own, all_, ls, ss, rs):
        self.own, self.all_, self.ls, self.ss, self.rs = own, all_, ls, ss, rs
        d, z, c, pair, g, y = place()
        self.k = 2 * y + c

    def copy(self, o):
        if o == 0:
            return pltpu.make_async_copy(self.own, self.all_.at[self.k], self.ls)
        return rcopy(
            self.own, self.all_.at[self.k], self.ss.at[o - 1], self.rs.at[o - 1], group_peer(o)
        )

    def start(self):
        for o in range(4):
            self.copy(o).start()

    def finish(self):
        for o in range(4):
            self.copy(o).wait()


def norm_back(total, x, dy):
    xhat, inverse = norm_parts(x.astype(f32))
    back = inverse * (
        total
        - jnp.mean(total, axis=-1, keepdims=True)
        - xhat * jnp.mean(total * xhat, axis=-1, keepdims=True)
    )
    return dy.astype(f32) + back


def tail_kernel(
    np_, part, xg, dyg, sums, dw1, dw2, dw, dwo,
    out, sums_all, r1, r2, rq, ro,
    from_sib, from_far, to_far, mine, done, xq, dyq, ls, ss, rs,
    ls_s, ss_s, rs_s, ls_g, ss_g, rs_g,
):
    d, z, c, pair, g, y = place()
    barrier_all(np_, d, z, c, pair)
    red = Reduce(
        part, out, [(xg, xq), (dyg, dyq)], (from_sib, from_far, to_far, mine, done), ls, ss, rs
    )
    grp = Group(sums, sums_all, ls_g, ss_g, rs_g)
    swap = Swap(np_, [(dw, rq), (dw1, r1), (dw2, r2)], (dwo, ro), ls_s, ss_s, rs_s)
    red.start()
    grp.start()
    swap.start()
    red.add_near()
    red.add_far(lambda total, r: norm_back(total, xq[r], dyq[r]))
    grp.finish()
    red.finish()
    swap.finish()


def tail(np_, part, xg, dyg, sums, dw1, dw2, dw, dwo, collective_id=3):
    rows = part.shape[1]
    any_ = pl.BlockSpec(memory_space=pl.ANY)
    wo_rows = dwo.shape[1]
    return pl.pallas_call(
        functools.partial(tail_kernel, np_),
        out_shape=(
            sds((rows, D), bf16), sds((4,) + sums.shape, f32),
            sds(dw1.shape, bf16), sds(dw2.shape, bf16), sds(dw.shape, bf16),
            sds((np_, wo_rows, D), bf16),
        ),
        in_specs=[any_] * 8,
        out_specs=(any_,) * 6,
        scratch_shapes=reduce_scratch(rows, 2) + [
            pltpu.SemaphoreType.DMA((4,)),
            pltpu.SemaphoreType.DMA((4, np_)),
            pltpu.SemaphoreType.DMA((4, np_)),
            pltpu.SemaphoreType.DMA,
            pltpu.SemaphoreType.DMA((3,)),
            pltpu.SemaphoreType.DMA((3,)),
        ],
        compiler_params=pltpu.CompilerParams(
            collective_id=collective_id, has_side_effects=True, vmem_limit_bytes=VMEM_BYTES
        ),
        name="tail",
    )(part, xg, dyg, sums, dw1, dw2, dw, dwo)


def same_slice_peer(np_, e):
    d, z, c, pair, g, y = place()
    to = lax.rem(pair * 2 + g + e, 2 * np_)
    pair2, g2 = lax.div(to, 2), lax.rem(to, 2)
    return to, (2 * pair2 + c, jnp.where(g2 == g, z, 3 - z))


def clip_kernel(
    np_, msg, r1, r2, rq, ro,
    t1, tq, t2, to, pieces,
    b1, bq, b2, bo, s1, sq, s2, so, m_all, p_out, ls, ss_m, rs_m, ss, rs,
):
    d, z, c, pair, g, y = place()
    bar = pltpu.get_barrier_semaphore()
    for o in range(1, 8):
        c2, z2 = column_peer(pair, c, z, o)
        pl.semaphore_signal(bar, inc=1, device_id=(2 * pair + c2, z2), device_id_type=MESH)
    for e in range(1, 2 * np_):
        unused, peer = same_slice_peer(np_, e)
        pl.semaphore_signal(bar, inc=1, device_id=peer, device_id_type=MESH)
    loads = [
        pltpu.make_async_copy(src, dst, ls.at[n])
        for n, (src, dst) in enumerate(((rq, bq), (r1, b1), (r2, b2), (ro, bo)))
    ]
    per = np_ // 4
    collects = lax.div(pair, per) == 2 * y + c
    for cp in loads[:3]:
        cp.start()

    @pl.when(collects)
    def _():
        loads[3].start()

    me = pair * 2 + g
    pl.semaphore_wait(bar, 7 + 2 * np_ - 1)

    def tell(e):
        to_, peer = same_slice_peer(np_, e)
        return rcopy(msg.at[to_], m_all.at[me], ss_m.at[e], rs_m.at[e], peer)

    own = pltpu.make_async_copy(msg.at[me], m_all.at[me], ls.at[4])
    own.start()
    for e in range(1, 2 * np_):
        tell(e).start()
    own.wait()
    for e in range(1, 2 * np_):
        tell(e).wait()
    norms = [jnp.sqrt(m_all[e, 3:4, 0:1]) for e in range(2 * np_)]
    mean_norm = sum(norms) / (2 * np_)
    factors = [mean_norm / jnp.maximum(n, mean_norm) for n in norms]
    p_out[...] = sum(f * m_all[e] for e, f in enumerate(factors))
    p_out[4:5, 0:1] = sum(jnp.where(d == e, n, 0.0) for e, n in enumerate(norms))
    group_factors = [
        jnp.where(g == 0, factors[2 * n], factors[2 * n + 1]) for n in range(np_)
    ]
    for cp in loads[:3]:
        cp.wait()

    def rows_to(s, src, dst, o, slot):
        c2, z2 = column_peer(pair, c, z, o)
        if o == 0:
            return pltpu.make_async_copy(src.at[c2, z2], dst.at[slot], ls.at[5 + s])
        return rcopy(
            src.at[c2, z2], dst.at[slot], ss.at[s, o], rs.at[s, o], (2 * pair + c2, z2)
        )

    for n, (buf, acc, dst) in enumerate(((bq, sq, tq), (b1, s1, t1))):
        for c2 in range(2):
            for z2 in range(4):
                total = sum(f * buf[m, c2, z2].astype(f32) for m, f in enumerate(group_factors))
                acc[c2, z2] = total.astype(acc.dtype)
        for o in range(8):
            rows_to(n, acc, dst, o, c * 4 + z).start()

    for t in range(2):
        total = sum(f * b2[m, t].astype(f32) for m, f in enumerate(group_factors))
        s2[t] = total.astype(s2.dtype)
    mirror_copy = rcopy(s2.at[1 - g], t2.at[1], ss.at[2, 0], rs.at[2, 0], (d, 3 - z))
    mirror_copy.start()
    kept = pltpu.make_async_copy(s2.at[g], t2.at[0], ls.at[7])
    kept.start()

    def wo_to(o):
        c2, z2 = column_peer(pair, c, z, o)
        if o == 0:
            return pltpu.make_async_copy(so.at[c2, z2], to.at[g], ls.at[8])
        return rcopy(
            so.at[c2, z2], to.at[g], ss.at[3, o], rs.at[3, g], (2 * pair + c2, z2)
        )

    @pl.when(collects)
    def _():
        loads[3].wait()
        for c2 in range(2):
            for z2 in range(4):
                total = sum(f * bo[m, c2, z2].astype(f32) for m, f in enumerate(group_factors))
                so[c2, z2] = total.astype(so.dtype)
        for o in range(8):
            wo_to(o).start()

    final = pltpu.make_async_copy(p_out, pieces, ls.at[9])
    final.start()
    for n, (acc, dst) in enumerate(((sq, tq), (s1, t1))):
        for o in range(8):
            rows_to(n, acc, dst, o, c * 4 + z).wait()
    mirror_copy.wait()
    kept.wait()

    @pl.when(collects)
    def _():
        wo_to(0).wait()
        for o in range(1, 8):
            wo_to(o).wait_send()

    for t in range(2):
        @pl.when(jnp.logical_or(jnp.logical_not(collects), g != t))
        def _():
            rcopy(so.at[0, 0], to.at[t], ss.at[3, 0], rs.at[3, t], (d, 3 - z)).wait_recv()

    final.wait()


def clip(np_, msg, r1, r2, rq, ro, collective_id=4):
    any_ = pl.BlockSpec(memory_space=pl.ANY)
    dma = pltpu.SemaphoreType.DMA
    return pl.pallas_call(
        functools.partial(clip_kernel, np_),
        out_shape=(
            sds((8,) + r1.shape[3:], bf16), sds((8,) + rq.shape[3:], bf16),
            sds((2,) + r2.shape[2:], bf16), sds((2,) + ro.shape[3:], bf16), sds(msg.shape[1:], f32),
        ),
        in_specs=[any_] * 5,
        out_specs=(any_,) * 5,
        scratch_shapes=[
            pltpu.VMEM(r1.shape, bf16), pltpu.VMEM(rq.shape, bf16), pltpu.VMEM(r2.shape, bf16),
            pltpu.VMEM(ro.shape, bf16),
            pltpu.VMEM(r1.shape[1:], bf16), pltpu.VMEM(rq.shape[1:], bf16),
            pltpu.VMEM(r2.shape[1:], bf16), pltpu.VMEM(ro.shape[1:], bf16),
            pltpu.VMEM(msg.shape, f32), pltpu.VMEM(msg.shape[1:], f32),
            dma((10,)), dma((2 * np_,)), dma((2 * np_,)), dma((4, 8)), dma((4, 8)),
        ],
        compiler_params=pltpu.CompilerParams(
            collective_id=collective_id, has_side_effects=True, vmem_limit_bytes=VMEM_BYTES
        ),
        name="clip",
    )(msg, r1, r2, rq, ro)


def local(
    block_in, out_grad, lengths, ln1_gain, ln1_bias, qkv_weight, qkv_bias, out_weight, out_bias,
    ln2_gain, ln2_bias, fc1_weight, fc1_bias, fc2_weight, fc2_bias,
):
    tp = lax.axis_size("ctx")
    dp = lax.axis_size("dp")
    np_ = dp // 2
    world = dp * tp
    d, z, c, pair, g, y = place()
    slice_at = 2 * y + c
    nh = HEADS // tp
    local_rows = block_in.shape[1]
    t = local_rows * tp
    rows = min(512, local_rows)
    part = D // tp
    r_in = D // world
    r_ff = fc2_weight.shape[0]
    ff = r_ff * dp

    x_own = block_in[0]
    pos = z * local_rows + jnp.arange(local_rows, dtype=jnp.int32)
    dy_own = jnp.where((pos < lengths[0])[:, None], out_grad[0], jnp.zeros((), bf16))

    w_qkv = jnp.moveaxis(qkv_weight.reshape(r_in, 3, tp, part), 2, 0).reshape(tp, r_in, 3 * part)
    w1 = fc1_weight.reshape(r_in, np_, 2, tp, r_ff)
    w1 = jnp.stack([w1[:, :, :, s] for s in (0, 3, 1, 2)], axis=3)
    w1 = w1.reshape(r_in, np_, 2, 2, 2, r_ff).transpose(3, 2, 0, 1, 4, 5).reshape(tp, r_in, ff)
    length_parts = jnp.stack([lengths[0] // 256, lengths[0] % 256]).astype(bf16)
    vectors = jnp.concatenate(
        [
            ln1_gain, ln1_bias, out_bias, ln2_gain, ln2_bias, fc2_bias, qkv_bias, fc1_bias,
            length_parts,
        ]
    )
    n_vec = 9 * r_in + r_ff
    vectors = jnp.pad(vectors, (0, 16 * PAD - n_vec - 2)).reshape(16, PAD)

    x, dy, w_qkv, w1, w2, wo, vectors = gather(
        np_, x_own, dy_own, w_qkv, w1, fc2_weight, out_weight, vectors
    )
    xq, dyq = x, dy
    x, dy = x.reshape(t, D), dy.reshape(t, D)
    w_qkv = w_qkv.reshape(D, 3 * part)
    w1, w2, wo = w1.reshape(D, ff), w2.reshape(ff, D), wo.reshape(part, D)
    vectors = vectors.reshape(np_, 2, tp, 16 * PAD).astype(f32)
    lengths_here = lax.dynamic_slice(vectors, (pair, g, 0, n_vec), (1, 1, 1, 2)).reshape(2)
    length = (lengths_here[0] * 256.0 + lengths_here[1]).astype(jnp.int32).reshape(1)
    b_up = lax.dynamic_slice_in_dim(vectors, c, 1, axis=1)[:, 0, :, 9 * r_in : n_vec]
    b_up = jnp.where(
        y == 0,
        jnp.stack([b_up[:, 0], b_up[:, 3]], axis=1),
        jnp.stack([b_up[:, 1], b_up[:, 2]], axis=1),
    ).reshape(1, ff)
    vectors = vectors.reshape(world, 16 * PAD)
    g1, b1, b_out, g2, b2, b_down = [
        vectors[:, s * r_in : (s + 1) * r_in].reshape(1, D) for s in range(6)
    ]
    b_qkv = vectors[:, 6 * r_in : 9 * r_in].reshape(3, tp, part)
    b_qkv = lax.dynamic_slice_in_dim(b_qkv, slice_at, 1, axis=1).reshape(3 * nh, HEAD_DIM)
    extra = np.zeros((3 * nh, PAD - HEAD_DIM), np.float32)
    extra[:nh, 0] = HEAD_DIM**0.5
    extra[nh : 2 * nh, 1:4] = 1.0
    extra[2 * nh :, 0:3] = 1.0
    b_pad = jnp.concatenate([b_qkv, jnp.asarray(extra)], axis=1).reshape(1, 3 * nh * PAD)
    cosine, sine = tables(t)

    q, k, v, cf, ctx = attn_fwd(length, x, g1, b1, w_qkv, b_pad, cosine, sine, nh, rows)
    out_part, u_mlp, dw1, dw2, vec = mlp(x, dy, ctx, g2, b2, wo, w1, b_up, w2, rows // 2)
    block_out = reduce_out(np_, out_part.reshape(4, local_rows, D), xq, b_out + b_down)
    u_part, dw, dwo, vec = attn_bwd(
        x, dy, cf, ctx, u_mlp, q, k, v, g1, b1, w_qkv, wo, cosine, sine, vec, rows
    )
    per = np_ // 4
    input_grad, sums, r1, r2, rq, ro = tail(
        np_, u_part.reshape(4, local_rows, D), xq, dyq, vec,
        dw1.reshape(np_, D // np_, ff), dw2.reshape(np_, 2 * r_ff, D),
        dw.reshape(np_, D // np_, 3 * part), dwo.reshape(per, part // per, D),
    )
    d_vecs = jnp.concatenate([jnp.sum(sums[:, :4], axis=0), sums[:1, 6]], axis=0)
    squares = (
        jnp.sum(d_vecs * d_vecs) + jnp.sum(sums[0, 6] * sums[0, 6])
        + jnp.sum(sums[:, 4] * sums[:, 4]) + jnp.sum(sums[:, 5] * sums[:, 5])
        + jnp.sum(sums[:, 7, 0])
    )

    def for_owners(m):
        m = lax.dynamic_index_in_dim(m, c, axis=m.ndim - 3, keepdims=False)
        m = jnp.where(
            y == 0,
            jnp.stack([m[..., 0, :], m[..., 3, :]], axis=-2),
            jnp.stack([m[..., 1, :], m[..., 2, :]], axis=-2),
        )
        return m

    p_vecs = jnp.moveaxis(for_owners(d_vecs.reshape(5, np_, 2, tp, r_in)), 0, 2)
    p_vecs = p_vecs.reshape(np_, 2, 5 * r_in)
    p_qkv = sums[:, 5, : 3 * part].reshape(tp, 3, part).swapaxes(0, 1)
    p_qkv = for_owners(p_qkv.reshape(np_, 2, tp, 3 * r_in))
    p_up = vec[4].reshape(np_, 2, r_ff)
    msg = jnp.stack(
        [jnp.pad(m, ((0, 0), (0, 0), (0, PAD - m.shape[2]))) for m in (p_vecs, p_qkv, p_up)]
        + [jnp.broadcast_to(squares, (np_, 2, PAD))] + [jnp.zeros((np_, 2, PAD), f32)] * 4,
        axis=2,
    ).reshape(2 * np_, 8, PAD)
    t1, tq, t2, to, mine = clip(
        np_, msg, r1.reshape(np_, 2, tp, r_in, ff), r2.reshape(np_, 2, r_ff, D),
        rq.reshape(np_, 2, tp, r_in, 3 * part), ro.reshape(np_, 2, tp, r_in, D),
    )
    t1 = t1.reshape(2, tp, r_in, ff).astype(f32)
    t1 = jnp.stack([t1[:, 0] + t1[:, 3], t1[:, 1] + t1[:, 2]], axis=1)
    t1 = t1.reshape(2, 2, r_in, np_, 2, r_ff)
    t1 = jnp.stack([t1[:, s, :, :, e] for s, e in ((0, 0), (1, 0), (1, 1), (0, 1))], axis=0)
    g_fc1 = t1.transpose(2, 3, 1, 0, 4).reshape(r_in, ff * tp)
    tq = tq.reshape(2, tp, r_in, 3, part).astype(f32)
    tq = jnp.stack([tq[:, 0] + tq[:, 3], tq[:, 1] + tq[:, 2]], axis=0)
    g_qkv = tq.reshape(tp, r_in, 3, part).transpose(1, 2, 0, 3).reshape(r_in, 3 * D)
    g_fc2 = jnp.sum(t2.astype(f32), axis=0)
    g_out = jnp.sum(to.astype(f32), axis=0)
    cut = [mine[0, s * r_in : (s + 1) * r_in] for s in range(5)]
    return (
        block_out[None], input_grad[None],
        cut[0], cut[1], g_qkv, mine[1, : 3 * r_in], g_out, cut[4],
        cut[2], cut[3], g_fc1, mine[2, :r_ff], g_fc2, cut[4],
        mine[4, :1],
    )


def solution(mesh):
    both = ("dp", "ctx")
    vec, mat, act = P(both), P(both, None), P("dp", "ctx", None)
    weights = (vec, vec, mat, vec, mat, vec, vec, vec, mat, vec, mat, vec)
    return jax.shard_map(
        local,
        mesh=mesh,
        in_specs=(act, act, P("dp")) + weights,
        out_specs=(act, act) + weights + (P("dp"),),
        check_vma=False,
    )
```

time: 671 us -> 343 us (0.51)
  waiting for transfers between devices: 327 us -> 0 us
  Pallas kernels: 107 us -> 296 us
  blocking collectives: 137 us -> 0 us
  between operations: 22.8 us -> 6.47 us
  starting transfers between devices: 15.8 us -> 0 us
  other arithmetic: 24.7 us -> 11.7 us
  local copies, waits for them, and re-layouts: 34.1 us -> 24.8 us
    reduce_scatter x6 -> x0, waiting for transfers between devices: 205 us -> none  [the longest x4 85 us: over_dp(): lax.psum_scatter((m * factor).astype(bf16), 'dp', scatter_dimension=0, ti...]
    pallas_call x0 -> x4, Pallas kernels: none -> 195 us  [the longest x1 90.7 us: gather(): pl.pallas_call(functools.partial(gather_kernel, np_), out_shape=outs, in_...]
    all_gather x5 -> x0, waiting for transfers between devices: 118 us -> none  [the longest x1 65 us: local(): dy = lax.all_gather(dy_own, 'ctx', axis=0, tiled=True)]
    psum x3 -> x0, blocking collectives: 70.4 us -> none  [the longest x1 39.9 us: local(): small = lax.psum(small, ('dp', 'ctx'))]
    unnamed x1 -> x0, blocking collectives: 41.7 us -> none
    all_gather x1 -> x0, blocking collectives: 14 us -> none  [local(): w_qkv = lax.all_gather(w_qkv, 'dp', axis=0, tiled=True).reshape(D, 3 * part)]
    all_to_all x3 -> x0, starting transfers between devices: 11 us -> none  [the longest x2 7.67 us: back_rows(): m = lax.all_to_all(m.reshape(tp, r_in, m.shape[1]), 'ctx', 0, 0)]
    all_to_all x1 -> x0, blocking collectives: 10.9 us -> none  [local(): w1 = lax.all_to_all(w1, 'ctx', 0, 0)]
  transfers between devices with their start and end apart: 15 -> 0, of which waited for: 9 -> 0; matrix products, arithmetic and copies ran while one was open for 5% -> 0% of each run, Pallas kernels for 4% -> 0%
where the time goes in v2:
time: 343 us; the launch traced here: 339 us
  Pallas kernels  296 us (86%)
  local copies, waits for them, and re-layouts  24.8 us (7%)
  other arithmetic  11.7 us (3%)
  between operations  6.47 us (2%)
    pallas_call x1, Pallas kernels, gather(): pl.pallas_call(functools.partial(gather_kernel, np_), out_shape=outs, in_...  90.7 us
    pallas_call x1, Pallas kernels, tail(): pl.pallas_call(functools.partial(tail_kernel, np_), out_shape=(sds((rows,...  44.6 us
    pallas_call x1, Pallas kernels, attn_bwd(): pl.pallas_call(attn_bwd_kernel, grid=(n,), out_shape=(sds((t, D), bf16),...  42.7 us
    pallas_call x1, Pallas kernels, reduce_out(): pl.pallas_call(functools.partial(reduce_out_kernel, np_), out_shape=sds((...  33 us
    pallas_call x1, Pallas kernels, attn_fwd(): pl.pallas_call(attn_fwd_kernel, grid=(t // rows,), out_shape=(sds((nh, t,...  29.7 us
    pallas_call x1, Pallas kernels, mlp(): pl.pallas_call(mlp_kernel, grid=(t // rows,), out_shape=(sds((t, D), bf16...  28.6 us
    pallas_call x1, Pallas kernels, clip(): pl.pallas_call(functools.partial(clip_kernel, np_), out_shape=(sds((8,) +...  27 us

profile of v2, /device:TPU:1, one launch (start us, length us, event | category | flops | bytes accessed | tf_op | source)
XLA Modules:
  0.0 339.3 jit_solution(15598380529090945726)
XLA Ops:
  1.4 2.2 bitcast_select_fusion.dy
  7.4 90.7 %gather.1 = (bf16[4,512,768]{2,1,0:T(8,128)(2,1)}, bf16[4,512,768]{2,1,0:T(8,128)(2,1)}, bf16[4,2,4,24,576]{4,3,2,1,0:T(8,128)(2,1)}, bf16[4,2,4,24,768]{4,3,2,1...) custom-call(bf16[512,768]{1,0:T(8,128)(2,1)} %bitcast.138, ...), custom_call_target="tpu_custom_call" | custom-call | tf_op jit(solution)/shard_map/gather/pallas_call | solution.py:715
  98.2 1.0 reshape.280
  101.2 0.9 convert_element_type.54
  104.6 29.7 %attn_fwd.1 = (bf16[3,2048,128]{2,1,0:T(8,128)(2,1)}, bf16[3,2048,128]{2,1,0:T(8,128)(2,1)}, bf16[3,2048,128]{2,1,0:T(8,128)(2,1)}, f32[2048,384]{1,0:T(8,128)}, bf16[2048,192]{1,0:T(8,128)(2,1)}) custom-call(s32[1]{0:T(128)} %bitcast.11.len_ref, bf16[2048,768]{1,0:T(8,128)(2,1)} %bitcast.112, f32[1,768]{1,0:T(1,128)} %reshape.253.g_ref, ...), custom_call_target="tpu_custom_call" | custom-call | tf_op jit(solution)/shard_map/attn_fwd/pallas_call | solution.py:285
  136.4 28.6 %mlp.1 = (bf16[2048,768]{1,0:T(8,128)(2,1)}, f32[2048,768]{1,0:T(8,128)}, bf16[768,768]{1,0:T(8,128)(2,1)}, bf16[768,768]{1,0:T(8,128)(2,1)}, f32[8,768]{1,0:T(8,128)}) custom-call(bf16[2048,768]{1,0:T(8,128)(2,1)} %bitcast.113, bf16[2048,768]{1,0:T(8,128)(2,1)} %bitcast.115, bf16[2048,192]{1,0:T(8,128)(2,1)} %get-tuple-element.51.c_ref, ...), custom_call_target="tpu_custom_call" | custom-call | tf_op jit(solution)/shard_map/mlp/pallas_call | solution.py:320
  165.7 33.0 %reduce_out.1 = bf16[512,768]{1,0:T(8,128)(2,1)} custom-call(bf16[4,512,768]{2,1,0:T(8,128)(2,1)} %bitcast.119, bf16[4,512,768]{2,1,0:T(8,128)(2,1)} %get-tuple-element.47.xg, f32[1,768]{1,0:T(1,128)} %add.111.bias), custom_call_target="tpu_custom_call" | custom-call | tf_op jit(solution)/shard_map/reduce_out/pallas_call | solution.py:870
  198.7 42.7 %attn_bwd.1 = (bf16[2048,768]{1,0:T(8,128)(2,1)}, bf16[768,576]{1,0:T(8,128)(2,1)}, bf16[192,768]{1,0:T(8,128)(2,1)}, f32[8,768]{1,0:T(8,128)}) custom-call(bf16[2048,768]{1,0:T(8,128)(2,1)} %bitcast.114, bf16[2048,768]{1,0:T(8,128)(2,1)} %bitcast.116, f32[2048,384]{1,0:T(8,128)} %get-tuple-element.56.cf_ref, bf16[2048,192]{1,0:T(8,128)(2,1)} %get-tuple-element.51.c_ref, ...), custom_call_target="tpu_custom_call" | custom-call | tf_op jit(solution)/shard_map/attn_bwd/pallas_call | solution.py:346
  241.4 44.6 %tail.1 = (bf16[512,768]{1,0:T(8,128)(2,1)}, f32[4,8,768]{2,1,0:T(8,128)}, bf16[4,192,768]{2,1,0:T(8,128)(2,1)}, bf16[4,192,768]{2,1,0:T(8,128)(2,1)}, bf16[4,19...) custom-call(bf16[4,512,768]{2,1,0:T(8,128)(2,1)} %bitcast.120, bf16[4,512,768]{2,1,0:T(8,128)(2,1)} %get-tuple-element.47.xg, ...), custom_call_target="tpu_custom_call" | custom-call | tf_op jit(solution)/shard_map/tail/pallas_call | solution.py:1013
  286.0 0.9 slice_reduce_fusion
  287.0 1.4 multiply_reduce_fusion.2
  288.6 0.9 slice_reduce_fusion.1
  292.6 1.6 multiply_reduce_fusion
  295.5 1.3 slice_reduce_fusion.3
  298.2 27.0 %clip.1 = (bf16[8,24,768]{2,1,0:T(8,128)(2,1)}, bf16[8,24,576]{2,1,0:T(8,128)(2,1)}, bf16[2,96,768]{2,1,0:T(8,128)(2,1)}, bf16[2,24,768]{2,1,0:T(8,128)(2,1)}, f32[8,128]{1,0:T(8,128)}) custom-call(f32[8,8,128]{2,1,0:T(8,128)} %stack.75.msg, bf16[4,2,4,24,768]{4,3,2,1,0:T(8,128)(2,1)} %bitcast.125, bf16[4,2,96,768]{3,2,1,0:T(8,128)(2,1)} %bitcast.126, ...), custom_call_target="tpu_custom_call" | custom-call | tf_op jit(solution)/shard_map/clip/pallas_call | solution.py:1162
  325.2 1.5 slice_bitcast_fusion.3
  326.6 1.3 reshape.282
  328.4 0.9 reshape.278
  329.3 1.2 slice_bitcast_fusion.6
  332.9 1.1 reshape.279
  333.9 1.2 slice_bitcast_fusion.2
  335.9 1.2 slice.204
  337.6 0.9 copy.88
  338.4 0.9 copy.89
  (106 shorter events, 16.3 us)
Async XLA Ops:
  0.6 2.9 copy-start.5
  0.7 4.0 %copy-start.4 = (bf16[24,3072]{1,0:T(8,128)(2,1)S(1)}, bf16[24,3072]{1,0:T(8,128)(2,1)}, u32[]{:S(2)}) copy-start(bf16[24,3072]{1,0:T(8,128)(2,1)} %param.29) | copy-start | bytes 442372
  3.7 3.0 copy-start.8
  3.7 3.0 copy-start.9
  3.7 3.0 copy-start.10
  3.7 2.9 copy-start.11
  3.8 2.9 copy-start.12
  3.8 2.9 copy-start.13
  3.8 2.9 copy-start.14
  3.8 2.9 copy-start.15
  7.4 96.5 %copy-start.7 = (f32[9,64]{1,0:T(8,128)S(1)}, f32[9,64]{1,0:T(8,128)}, u32[]{:S(2)}) copy-start(f32[9,64]{1,0:T(8,128)} %constant.78.clone) | copy-start | bytes 6916
  326.6 10.4 %copy-start.16 = (f32[24]{0:T(128)}, f32[24]{0:T(128)S(1)}, u32[]{:S(2)}) copy-start(f32[24]{0:T(128)S(1)} %get-tuple-element.162) | copy-start | bytes 292
  328.0 2.5 copy-start.6
  328.0 3.2 copy-start.2
  331.6 3.5 %copy-start.3 = (bf16[2,96,768]{2,1,0:T(8,128)(2,1)S(1)}, bf16[2,96,768]{2,1,0:T(8,128)(2,1)}, u32[]{:S(2)}) copy-start(bf16[2,96,768]{2,1,0:T(8,128)(2,1)} %get-tuple-element.78) | copy-start | bytes 884740
  332.0 5.6 %copy-start = (bf16[512,768]{1,0:T(8,128)(2,1)S(1)}, bf16[512,768]{1,0:T(8,128)(2,1)}, u32[]{:S(2)}) copy-start(bf16[512,768]{1,0:T(8,128)(2,1)} %reduce_out.1) | copy-start | bytes 2359300
  332.8 5.6 %copy-start.1 = (bf16[512,768]{1,0:T(8,128)(2,1)S(1)}, bf16[512,768]{1,0:T(8,128)(2,1)}, u32[]{:S(2)}) copy-start(bf16[512,768]{1,0:T(8,128)(2,1)} %get-tuple-element.68) | copy-start | bytes 2359300

commit v3 on v2

--- a/solution.py
+++ b/solution.py
@@ -54,13 +54,35 @@
 
 
 def attn_fwd_kernel(
-    len_ref, x_ref, g_ref, b_ref, w_ref, wb_ref, cos_ref, sin_ref,
-    q_ref, k_ref, v_ref, cf_ref, c_ref, w_scr, s_scr, q_scr, m_scr, l_scr, acc_scr,
+    np_, len_ref, x_ref, tab_ref, w_ref, wb_ref, cos_ref, sin_ref, dy, w2, wo,
+    q_ref, k_ref, v_ref, cf_ref, c_ref, dyg, w2g, wog,
+    w_scr, s_scr, q_scr, m_scr, l_scr, acc_scr, ls_dy, ss_dy, rs_dy, ls_w, ss_w, rs_w,
 ):
     i = pl.program_id(0)
     nh = k_ref.shape[0]
     rows = x_ref.shape[0]
-    length = len_ref[0]
+    spread = Spread(dy, dyg, ls_dy, ss_dy, rs_dy)
+    weights = Weights(np_, [], (w2, w2g), (wo, wog), ls_w, ss_w, rs_w)
+
+    @pl.when(i == 0)
+    def _():
+        d, z, c, pair, g, y = place()
+        barrier_all(np_, d, z, c, pair)
+        weights.start()
+        spread.start()
+
+    @pl.when(i == 1)
+    def _():
+        weights.between_wo()
+        weights.between_w2()
+
+    @pl.when(i == 2)
+    def _():
+        spread.forward(0)
+
+    @pl.when(i == 3)
+    def _():
+        spread.forward(1)
 
     @pl.when(i == 0)
     def _():
@@ -69,12 +91,12 @@
             w_scr[:, h * PAD + HEAD_DIM : (h + 1) * PAD] = jnp.zeros((D, PAD - HEAD_DIM), bf16)
 
     xhat, unused = norm_parts(x_ref[...].astype(f32))
-    a1 = (xhat * g_ref[...] + b_ref[...]).astype(bf16)
+    a1 = (xhat * tab_ref[0:1] + tab_ref[1:2]).astype(bf16)
     cosine, sine = cos_ref[...], sin_ref[...]
     lane = lax.broadcasted_iota(jnp.int32, (rows, PAD), 1)
     first = lane < ROT // 2
     key_pos = i * rows + lax.broadcasted_iota(jnp.int32, (rows, PAD), 0)
-    key_bias = jnp.where(key_pos < length, 0.0, neg_big)
+    key_bias = jnp.where(key_pos.astype(f32) < len_ref[...], 0.0, neg_big)
     here = pl.ds(pl.multiple_of(i * rows, rows), rows)
     qkv = dot(a1, w_scr[...]) + wb_ref[...]
     for h in range(nh):
@@ -128,20 +150,26 @@
         q = jnp.where(lane == HEAD_DIM + 3, low, q)
         q_ref[h] = q.astype(bf16)
 
+    @pl.when(i == pl.num_programs(0) - 1)
+    def _():
+        spread.finish()
+        weights.finish_wo()
+        weights.finish_w2()
+
 
 def squares_of(m):
     return jnp.sum(jnp.sum(m * m, axis=0, keepdims=True), axis=1, keepdims=True)
 
 
 def mlp_kernel(
-    x_ref, dy_ref, c_ref, g_ref, b_ref, wo_ref, w1_ref, b1_ref, w2_ref,
+    x_ref, dy_ref, c_ref, tab_ref, wo_ref, w1_ref, w2_ref,
     part_ref, u_ref, dw1_ref, dw2_ref, vec_ref, dw1_scr, dw2_scr,
 ):
     i = pl.program_id(0)
     xhat, unused = norm_parts(x_ref[...].astype(f32))
-    gain = g_ref[...]
-    a2 = (xhat * gain + b_ref[...]).astype(bf16)
-    z = dot(a2, w1_ref[...]) + b1_ref[...]
+    gain = tab_ref[3:4]
+    a2 = (xhat * gain + tab_ref[4:5]).astype(bf16)
+    z = dot(a2, w1_ref[...]) + tab_ref[5:6]
     cdf = 0.5 * (1.0 + lax.erf(z * root_half))
     hidden = (z * cdf).astype(bf16)
     part = dot(hidden, w2_ref[...]) + dot(c_ref[...], wo_ref[...])
@@ -173,10 +201,14 @@
 
 
 def attn_bwd_kernel(
-    x_ref, dy_ref, cf_ref, c_ref, u_in_ref, q_ref, k_ref, v_ref, g_ref, b_ref, w_ref, wo_ref,
-    cos_ref, sin_ref, vec_in_ref,
-    u_ref, dw_ref, dwo_ref, vec_ref,
-    wo_scr, dk_scr, dv_scr, dq_scr, dc_scr, dqkv_scr, dw_scr, dwo_scr,
+    np_, r_in, r_ff, x_ref, dy_ref, cf_ref, c_ref, u_in_ref, q_ref, k_ref, v_ref, tab_ref, w_ref,
+    wo_ref, cos_ref, sin_ref, vec_in_ref, hot_ref, qkv_at, part, xg, dyg, dw1, dw2,
+    block_out, input_grad, t1, tq, t2, to, pieces,
+    wo_scr, dk_scr, dv_scr, dq_scr, dc_scr, dqkv_scr, dw_scr, dwo_scr, vec_ref, u_scr, dw, dwo,
+    from_sib, from_far, to_far, mine, done, xq, ls_o, ss_o, rs_o,
+    from_sib2, from_far2, to_far2, done2, dyq, ls_u, ss_u, rs_u,
+    ls_s, ss_s, rs_s, ls_w, ss_w, rs_w, sums_all, ls_g, ss_g, rs_g,
+    b1, bq, b2, bo, s1, sq, s2, so, msg, m_all, p_out, ls, ss_m, rs_m, ss, rs,
 ):
     step = pl.program_id(0)
     blocks = pl.num_programs(0)
@@ -187,6 +219,28 @@
     lane = lax.broadcasted_iota(jnp.int32, (rows, PAD), 1)
     first = lane < ROT // 2
     here = pl.ds(pl.multiple_of(i * rows, rows), rows)
+    red = Reduce(
+        part, block_out, [(xg, xq)], (from_sib, from_far, to_far, mine, done), ls_o, ss_o, rs_o
+    )
+    red_u = ReduceQuarters(
+        u_scr, input_grad, (from_sib2, from_far2, to_far2, done2), ls_u, ss_u, rs_u
+    )
+    swap = Swap(np_, [(dw1, b1), (dw2, b2)], None, ls_s, ss_s, rs_s)
+    load_dy = pltpu.make_async_copy(dyg.at[red.q_here], dyq, ls.at[4])
+
+    def back(total, r):
+        return norm_back(total, xq[r], dyq[r])
+
+    @pl.when(step == 0)
+    def _():
+        meet(np_)
+        red.start()
+        load_dy.start()
+        swap.start()
+
+    @pl.when(step == 2)
+    def _():
+        red.add_far(lambda total, r: xq[r].astype(f32) + tab_ref[2:3] + total)
 
     @pl.when(step == 0)
     def _():
@@ -209,6 +263,10 @@
         dc = jnp.where(lane == HEAD_DIM + 1, mid, dc)
         dc = jnp.where(lane == HEAD_DIM + 2, low, dc)
         dc_scr[h] = dc.astype(bf16)
+
+    @pl.when(step == 0)
+    def _():
+        red.add_near()
 
     causal = lax.broadcasted_iota(jnp.int32, (rows, rows), 0) <= lax.broadcasted_iota(
         jnp.int32, (rows, rows), 1
@@ -244,25 +302,39 @@
     for h in range(nh):
         dq = turn(dq_scr[h], cosine, sine, first) * HEAD_DIM**-0.5
         dk = turn(dk_scr[h, here], cosine, sine, first)
-        for at, part in ((h, dq), (nh + h, dk), (2 * nh + h, dv_scr[h, here])):
-            dqkv_scr[:, at * HEAD_DIM : (at + 1) * HEAD_DIM] = part[:, :HEAD_DIM].astype(bf16)
+        for at, piece in ((h, dq), (nh + h, dk), (2 * nh + h, dv_scr[h, here])):
+            dqkv_scr[:, at * HEAD_DIM : (at + 1) * HEAD_DIM] = piece[:, :HEAD_DIM].astype(bf16)
     dqkv = dqkv_scr[...]
     xhat, unused = norm_parts(x_ref[...].astype(f32))
-    gain = g_ref[...]
-    a1 = (xhat * gain + b_ref[...]).astype(bf16)
+    gain = tab_ref[0:1]
+    a1 = (xhat * gain + tab_ref[1:2]).astype(bf16)
     da1 = dot(dqkv, w_ref[...], ((1,), (1,)))
-    u_ref[...] = (u_in_ref[...].astype(f32) + da1 * gain).astype(u_ref.dtype)
+    u_scr[i] = (u_in_ref[...] + da1 * gain).astype(bf16)
+    red_u.ready(i)
     dw_scr[...] += dot(a1, dqkv, ((0,), (0,)))
     dwo_scr[...] += dot(c_ref[...], dy, ((0,), (0,)))
     vec_ref[0:1] += jnp.sum(da1 * xhat, axis=0, keepdims=True)
     vec_ref[1:2] += jnp.sum(da1, axis=0, keepdims=True)
     vec_ref[5:6, :wide] += jnp.sum(dqkv.astype(f32), axis=0, keepdims=True)
+    red_u.push(i)
 
     @pl.when(step == blocks - 1)
     def _():
-        dw_ref[...] = dw_scr[...].astype(bf16)
-        dwo_ref[...] = dwo_scr[...].astype(bf16)
         vec_ref[7:8, 0:1] += squares_of(dw_scr[...]) + squares_of(dwo_scr[...])
+        share = D // np_
+        for n in range(np_):
+            dw[n] = dw_scr[n * share : (n + 1) * share].astype(bf16)
+        per = np_ // 4
+        share_o = dwo_scr.shape[0] // per
+        for n in range(per):
+            dwo[n] = dwo_scr[n * share_o : (n + 1) * share_o].astype(bf16)
+        load_dy.wait()
+        finish_all(
+            np_, r_in, r_ff, wide // 3, red, red_u, swap, back,
+            dw, dwo, vec_ref, hot_ref, qkv_at, t1, tq, t2, to, pieces,
+            ls_w, ss_w, rs_w, sums_all, ls_g, ss_g, rs_g,
+            b1, bq, b2, bo, s1, sq, s2, so, msg, m_all, p_out, ls, ss_m, rs_m, ss, rs,
+        )
 
 
 def whole(shape):
@@ -273,32 +345,45 @@
     return jax.ShapeDtypeStruct(shape, dtype)
 
 
-def params():
+def params(collective_id=None):
     return pltpu.CompilerParams(
-        dimension_semantics=("arbitrary",), vmem_limit_bytes=VMEM_BYTES
+        dimension_semantics=("arbitrary",), vmem_limit_bytes=VMEM_BYTES,
+        collective_id=collective_id, has_side_effects=collective_id is not None,
     )
 
 
-def attn_fwd(length, x, g1, b1, w, wb, cosine, sine, nh, rows):
+def weight_sems(np_, n):
+    return [
+        pltpu.SemaphoreType.DMA((n,)),
+        pltpu.SemaphoreType.DMA((n, 8 + np_)),
+        pltpu.SemaphoreType.DMA((n, 8 + np_)),
+    ]
+
+
+def attn_fwd(np_, length, x, tab, w, wb, cosine, sine, dy, w2, wo, nh, rows):
     t = x.shape[0]
     lanes = pl.BlockSpec((rows, PAD), lambda i: (i, 0))
+    any_ = pl.BlockSpec(memory_space=pl.ANY)
     return pl.pallas_call(
-        attn_fwd_kernel,
+        functools.partial(attn_fwd_kernel, np_),
         grid=(t // rows,),
         out_shape=(
             sds((nh, t, PAD), bf16), sds((nh, t, PAD), bf16), sds((nh, t, PAD), bf16),
             sds((t, nh * PAD), f32), sds((t, nh * HEAD_DIM), bf16),
+            sds((4,) + dy.shape, bf16),
+            sds((np_, 2) + w2.shape, bf16), sds((np_ // 4, 2, 4) + wo.shape, bf16),
         ),
         in_specs=[
-            pl.BlockSpec(memory_space=pltpu.SMEM),
-            pl.BlockSpec((rows, D), lambda i: (i, 0)),
-            whole((1, D)), whole((1, D)), whole(w.shape), whole(wb.shape), lanes, lanes,
+            whole((1, PAD)), pl.BlockSpec((rows, D), lambda i: (i, 0)),
+            whole((8, D)), whole(w.shape), whole(wb.shape), lanes, lanes,
+            any_, any_, any_,
         ],
         out_specs=(
             pl.BlockSpec((nh, rows, PAD), lambda i: (0, i, 0)),
             whole((nh, t, PAD)), whole((nh, t, PAD)),
             pl.BlockSpec((rows, nh * PAD), lambda i: (i, 0)),
             pl.BlockSpec((rows, nh * HEAD_DIM), lambda i: (i, 0)),
+            any_, any_, any_,
         ),
         scratch_shapes=[
             pltpu.VMEM((D, 3 * nh * PAD), bf16),
@@ -307,13 +392,13 @@
             pltpu.VMEM((nh, rows, PAD), f32),
             pltpu.VMEM((nh, rows, PAD), f32),
             pltpu.VMEM((nh, rows, PAD), f32),
-        ],
-        compiler_params=params(),
+        ] + spread_sems() + weight_sems(np_, 2),
+        compiler_params=params(2),
         name="attn_fwd",
-    )(length, x, g1, b1, w, wb, cosine, sine)
-
-
-def mlp(x, dy, c, g2, b2, wo, w1, bias1, w2, rows):
+    )(length, x, tab, w, wb, cosine, sine, dy, w2, wo)
+
+
+def mlp(x, dy, c, tab, wo, w1, w2, rows):
     t = x.shape[0]
     ff = w1.shape[1]
     row = pl.BlockSpec((rows, D), lambda i: (i, 0))
@@ -326,51 +411,80 @@
         ),
         in_specs=[
             row, row, pl.BlockSpec((rows, c.shape[1]), lambda i: (i, 0)),
-            whole((1, D)), whole((1, D)), whole(wo.shape), whole(w1.shape), whole((1, ff)),
-            whole(w2.shape),
+            whole((8, D)), whole(wo.shape), whole(w1.shape), whole(w2.shape),
         ],
         out_specs=(row, row, whole((D, ff)), whole((ff, D)), whole((8, D))),
         scratch_shapes=[pltpu.VMEM((D, ff), f32), pltpu.VMEM((ff, D), f32)],
         compiler_params=params(),
         name="mlp",
-    )(x, dy, c, g2, b2, wo, w1, bias1, w2)
-
-
-def attn_bwd(x, dy, cf, c, u_in, q, k, v, g1, b1, w, wo, cosine, sine, vec, rows):
+    )(x, dy, c, tab, wo, w1, w2)
+
+
+def attn_bwd(
+    np_, r_in, r_ff, x, dy, cf, c, u_in, q, k, v, tab, w, wo, cosine, sine, vec,
+    part, xg, dyg, dw1, dw2, rows,
+):
     t = x.shape[0]
     nh = q.shape[0]
     n = t // rows
     wide = w.shape[1]
+    part_w = wide // 3
+    quarter = part.shape[1]
+    ff = dw1.shape[2]
+    per = np_ // 4
     row = pl.BlockSpec((rows, D), lambda i: (n - 1 - i, 0))
     lanes = pl.BlockSpec((rows, PAD), lambda i: (n - 1 - i, 0))
+    any_ = pl.BlockSpec(memory_space=pl.ANY)
+    dma = pltpu.SemaphoreType.DMA
+    vm = pltpu.VMEM
+    hot, qkv_at = one_hot_tables(np_, r_in, r_ff, part_w)
+    per_owner = lambda cols: vm((2, 4, r_in, cols), bf16)
+    block = vm((quarter, D), bf16)
     return pl.pallas_call(
-        attn_bwd_kernel,
+        functools.partial(attn_bwd_kernel, np_, r_in, r_ff),
         grid=(n,),
         out_shape=(
-            sds((t, D), bf16), sds((D, wide), bf16), sds((nh * HEAD_DIM, D), bf16),
-            sds((8, D), f32),
+            sds((quarter, D), bf16), sds((quarter, D), bf16), sds((8, r_in, ff), bf16),
+            sds((8, r_in, wide), bf16), sds((2, r_ff, D), bf16), sds((2, r_in, D), bf16),
+            sds((8, PAD), f32),
         ),
         in_specs=[
             row, row, pl.BlockSpec((rows, nh * PAD), lambda i: (n - 1 - i, 0)),
             pl.BlockSpec((rows, nh * HEAD_DIM), lambda i: (n - 1 - i, 0)), row,
             pl.BlockSpec((nh, rows, PAD), lambda i: (0, n - 1 - i, 0)),
-            whole(k.shape), whole(v.shape), whole((1, D)), whole((1, D)), whole(w.shape),
-            whole(wo.shape), lanes, lanes, whole((8, D)),
+            whole(k.shape), whole(v.shape), whole((8, D)), whole(w.shape),
+            whole(wo.shape), lanes, lanes, whole((8, D)), whole(hot.shape), whole(qkv_at.shape),
+            any_, any_, any_, any_, any_,
         ],
-        out_specs=(row, whole((D, wide)), whole((nh * HEAD_DIM, D)), whole((8, D))),
+        out_specs=(any_,) * 7,
         scratch_shapes=[
-            pltpu.VMEM((nh * PAD, D), bf16),
-            pltpu.VMEM((nh, t, PAD), f32),
-            pltpu.VMEM((nh, t, PAD), f32),
-            pltpu.VMEM((nh, rows, PAD), f32),
-            pltpu.VMEM((nh, rows, PAD), bf16),
-            pltpu.VMEM((rows, wide), bf16),
-            pltpu.VMEM((D, wide), f32),
-            pltpu.VMEM((nh * HEAD_DIM, D), f32),
+            vm((nh * PAD, D), bf16), vm((nh, t, PAD), f32), vm((nh, t, PAD), f32),
+            vm((nh, rows, PAD), f32), vm((nh, rows, PAD), bf16), vm((rows, wide), bf16),
+            vm((D, wide), f32), vm((nh * HEAD_DIM, D), f32), vm((8, D), f32),
+            vm((4, quarter, D), bf16), vm((np_, D // np_, wide), bf16),
+            vm((per, part_w // per, D), bf16),
+        ] + reduce_scratch(quarter, 1) + [
+            vm((2, quarter, D), bf16), block, block, block, block,
+            dma((5,)), dma((4, PIECES)), dma((4, PIECES)),
+        ] + swap_sems(np_, 2) + swap_sems(np_, 2) + [
+            vm((4, 8, D), f32), dma, dma((3,)), dma((3,)),
+            vm(dw1.shape, bf16), vm((np_, D // np_, wide), bf16), vm(dw2.shape, bf16),
+            vm((np_, part_w // per, D), bf16),
+            per_owner(ff), per_owner(wide), vm((2, r_ff, D), bf16), per_owner(D),
+            vm((2 * np_, 8, PAD), f32), vm((2 * np_, 8, PAD), f32), vm((8, PAD), f32),
+            dma((10,)), dma((2 * np_,)), dma((2 * np_,)), dma((4, 8)), dma((4, 8)),
         ],
-        compiler_params=params(),
+        compiler_params=params(3),
         name="attn_bwd",
-    )(x, dy, cf, c, u_in, q, k, v, g1, b1, w, wo, cosine, sine, vec)
+    )(x, dy, cf, c, u_in, q, k, v, tab, w, wo, cosine, sine, vec, hot, qkv_at, part, xg, dyg, dw1, dw2)
+
+
+def swap_sems(np_, n):
+    return [
+        pltpu.SemaphoreType.DMA((n,)),
+        pltpu.SemaphoreType.DMA((n, np_)),
+        pltpu.SemaphoreType.DMA((n, np_)),
+    ]
 
 
 def tables(t):
@@ -463,33 +577,45 @@
     def wait_recv(self, q, j):
         self.send(q, j, 0, self.sib).wait_recv()
 
+    def forward(self, j):
+        far = (mirror(2, self.g), mirror(3, self.g))
+        end, mid = mirror(0, self.g), mirror(1, self.g)
+
+        @pl.when(jnp.logical_and(self.prim, self.y == 1))
+        def _():
+            for q in far:
+                self.wait_recv(q, j)
+                self.send(q, j, 0, self.partner).start()
+                self.send(q, j, 1, self.sib).start()
+            self.wait_recv(end, j)
+            self.send(end, j, 1, self.sib).start()
+
+        @pl.when(jnp.logical_and(self.prim, self.y == 0))
+        def _():
+            self.wait_recv(mid, j)
+            self.send(mid, j, 1, self.sib).start()
+            if j > 0:
+                for q in far:
+                    self.wait_recv(q, j - 1)
+                    self.send(q, j - 1, 1, self.sib).start()
+
     def finish(self):
         far = (mirror(2, self.g), mirror(3, self.g))
         end, mid = mirror(0, self.g), mirror(1, self.g)
 
+        @pl.when(jnp.logical_and(self.prim, self.y == 0))
+        def _():
+            for q in far:
+                self.wait_recv(q, CHUNKS - 1)
+                self.send(q, CHUNKS - 1, 1, self.sib).start()
+            for j in range(CHUNKS):
+                self.send(end, j, 0, self.partner).wait_send()
+
         @pl.when(jnp.logical_and(self.prim, self.y == 1))
         def _():
             for j in range(CHUNKS):
-                for q in far:
-                    self.wait_recv(q, j)
-                    self.send(q, j, 0, self.partner).start()
-                    self.send(q, j, 1, self.sib).start()
-            for j in range(CHUNKS):
-                self.wait_recv(end, j)
-                self.send(end, j, 1, self.sib).start()
-            for j in range(CHUNKS):
                 for q in far + (mid,):
                     self.send(q, j, 0, self.partner).wait_send()
-
-        @pl.when(jnp.logical_and(self.prim, self.y == 0))
-        def _():
-            for q, j in [(mid, j) for j in range(CHUNKS)] + [
-                (q, j) for j in range(CHUNKS) for q in far
-            ]:
-                self.wait_recv(q, j)
-                self.send(q, j, 1, self.sib).start()
-            for j in range(CHUNKS):
-                self.send(end, j, 0, self.partner).wait_send()
 
         @pl.when(self.prim)
         def _():
@@ -668,31 +794,86 @@
                 self.wo_second(o).wait_recv()
 
 
+def decode_tables(np_, r_in, r_ff, part, nh):
+    wide = 3 * nh * PAD
+    f = np.arange(D)
+    by_d = np.zeros((8, D), np.int32)
+    by_d[0], by_d[1] = f // r_in, f % r_in
+    by_d[2], by_d[3], by_d[4] = f // (2 * r_ff), (f // r_ff) % 2, f % r_ff
+    p = np.arange(wide)
+    head, lane = p // PAD, p % PAD
+    by_q = np.full((8, wide), -1, np.int32)
+    for k in range(4):
+        at = (head // nh) * D + k * part + (head % nh) * HEAD_DIM + lane
+        real = lane < HEAD_DIM
+        by_q[k, real] = (at // (3 * r_in))[real]
+        by_q[4 + k, real] = (r_in + at % (3 * r_in))[real]
+    extra = np.zeros((1, wide), np.float32)
+    extra[0, (head < nh) & (lane == HEAD_DIM)] = HEAD_DIM**0.5
+    keys = (head >= nh) & (head < 2 * nh)
+    extra[0, keys & (lane > HEAD_DIM) & (lane < HEAD_DIM + 4)] = 1.0
+    extra[0, (head >= 2 * nh) & (lane >= HEAD_DIM) & (lane < HEAD_DIM + 3)] = 1.0
+    return jnp.asarray(by_d), jnp.asarray(by_q), jnp.asarray(extra)
+
+
+def decode(np_, r_in, r_ff, vec, by_d, by_q, extra, tab, b_pad, length):
+    d, z, c, pair, g, y = place()
+    world = 8 * np_
+    packed = vec[...].reshape(world * 16, PAD)
+    m = lax.broadcasted_iota(jnp.int32, (world, world * 16), 1)
+    n = lax.broadcasted_iota(jnp.int32, (world, world * 16), 0)
+    row = [
+        dot(jnp.where(m == 16 * n + r, 1.0, 0.0).astype(bf16), packed).astype(bf16)
+        for r in range(3)
+    ]
+
+    def pick(x, lanes, owner):
+        w = lanes.shape[1]
+        hot = lax.broadcasted_iota(jnp.int32, (PAD, w), 0) == lanes
+        got = dot(x, jnp.where(hot, 1.0, 0.0).astype(bf16))
+        mine = lax.broadcasted_iota(jnp.int32, (world, w), 0) == owner
+        return jnp.sum(jnp.where(mine, got, 0.0), axis=0, keepdims=True)
+
+    owner, lanes = by_d[0:1], by_d[1:2]
+    tab[0:1] = pick(row[0], lanes, owner)
+    tab[1:2] = pick(row[0], lanes + r_in, owner)
+    tab[2:3] = pick(row[0], lanes + 2 * r_in, owner) + pick(row[1], lanes, owner)
+    tab[3:4] = pick(row[0], lanes + 3 * r_in, owner)
+    tab[4:5] = pick(row[0], lanes + 4 * r_in, owner)
+    owner = by_d[2:3] * 8 + c * 4 + jnp.where(by_d[3:4] == 0, y, 3 - y)
+    tab[5:6] = pick(row[2], by_d[4:5], owner)
+    tab[6:8] = jnp.zeros((2, D), f32)
+    k = 2 * y + c
+    b_pad[...] = pick(row[1], by_q[pl.ds(4 + k, 1)], by_q[pl.ds(k, 1)]) + extra[...]
+    mine = lax.broadcasted_iota(jnp.int32, (world, PAD), 0) == (2 * pair + g) * 4
+    parts = jnp.sum(jnp.where(mine, row[2].astype(f32), 0.0), axis=0, keepdims=True)
+    lane = lax.broadcasted_iota(jnp.int32, (1, PAD), 1)
+    parts = jnp.where(lane == r_ff, parts * 256.0, jnp.where(lane == r_ff + 1, parts, 0.0))
+    length[...] = jnp.broadcast_to(jnp.sum(parts, axis=1, keepdims=True), (1, PAD))
+
+
 def gather_kernel(
-    np_, x, dy, wq, w1, w2, wo, vec, xg, dyg, wqg, w1g, w2g, wog, vecg,
-    ls_x, ss_x, rs_x, ls_dy, ss_dy, rs_dy, ls_w, ss_w, rs_w,
+    np_, r_in, r_ff, x, wq, w1, vec_own, by_d, by_q, extra,
+    xg, wqg, w1g, tab, b_pad, length, vec, ls_x, ss_x, rs_x, ls_w, ss_w, rs_w,
 ):
     d, z, c, pair, g, y = place()
     barrier_all(np_, d, z, c, pair)
-    sx = Spread(x, xg, ls_x, ss_x, rs_x)
-    sdy = Spread(dy, dyg, ls_dy, ss_dy, rs_dy)
-    w = Weights(
-        np_, [(vec, vecg, False), (wq, wqg, True), (w1, w1g, True)], (w2, w2g), (wo, wog),
+    spread = Spread(x, xg, ls_x, ss_x, rs_x)
+    weights = Weights(
+        np_, [(vec_own, vec, False), (wq, wqg, True), (w1, w1g, True)], None, None,
         ls_w, ss_w, rs_w,
     )
-    w.start()
-    sx.start()
+    weights.start()
+    spread.start()
     for s in range(3):
-        w.between(s)
-    w.between_wo()
-    w.between_w2()
-    sx.finish()
-    sdy.start()
-    sdy.finish()
-    for s in range(3):
-        w.finish(s)
-    w.finish_wo()
-    w.finish_w2()
+        weights.between(s)
+    spread.forward(0)
+    weights.finish(0)
+    decode(np_, r_in, r_ff, vec, by_d, by_q, extra, tab, b_pad, length)
+    spread.forward(1)
+    spread.finish()
+    for s in range(1, 3):
+        weights.finish(s)
 
 
 def spread_sems():
@@ -703,30 +884,26 @@
     ]
 
 
-def gather(np_, x, dy, wq, w1, w2, wo, vec, collective_id=1):
-    rows = x.shape[0]
+def gather(np_, r_in, r_ff, nh, x, wq, w1, vec, collective_id=1):
     any_ = pl.BlockSpec(memory_space=pl.ANY)
-    outs = (
-        sds((4, rows, D), bf16), sds((4, rows, D), bf16),
-        sds((np_, 2, 4) + wq.shape[1:], bf16), sds((np_, 2, 4) + w1.shape[1:], bf16),
-        sds((np_, 2) + w2.shape, bf16), sds((np_ // 4, 2, 4) + wo.shape, bf16),
-        sds((np_, 2, 4) + vec.shape, bf16),
-    )
+    vmem = pl.BlockSpec(memory_space=pltpu.VMEM)
+    wide = 3 * nh * PAD
     return pl.pallas_call(
-        functools.partial(gather_kernel, np_),
-        out_shape=outs,
-        in_specs=[any_] * 7,
-        out_specs=(any_,) * 7,
-        scratch_shapes=spread_sems() + spread_sems() + [
-            pltpu.SemaphoreType.DMA((5,)),
-            pltpu.SemaphoreType.DMA((5, 8 + np_)),
-            pltpu.SemaphoreType.DMA((5, 8 + np_)),
-        ],
+        functools.partial(gather_kernel, np_, r_in, r_ff),
+        out_shape=(
+            sds((4,) + x.shape, bf16), sds((np_, 2, 4) + wq.shape[1:], bf16),
+            sds((np_, 2, 4) + w1.shape[1:], bf16),
+            sds((8, D), f32), sds((1, wide), f32), sds((1, PAD), f32),
+        ),
+        in_specs=[any_] * 4 + [vmem] * 3,
+        out_specs=(any_,) * 3 + (vmem,) * 3,
+        scratch_shapes=[pltpu.VMEM((np_, 2, 4, 16, PAD), bf16)] + spread_sems()
+        + weight_sems(np_, 3),
         compiler_params=pltpu.CompilerParams(
             collective_id=collective_id, has_side_effects=True, vmem_limit_bytes=VMEM_BYTES
         ),
         name="gather",
-    )(x, dy, wq, w1, w2, wo, vec)
+    )(x, wq, w1, vec, *decode_tables(np_, r_in, r_ff, wq.shape[2] // 3, nh))
 
 
 PIECES = 4
@@ -850,34 +1027,42 @@
     ]
 
 
-def reduce_out_kernel(
-    np_, part, xg, bias, out, from_sib, from_far, to_far, mine, done, xq, ls, ss, rs,
-):
-    d, z, c, pair, g, y = place()
-    barrier_all(np_, d, z, c, pair)
-    red = Reduce(
-        part, out, [(xg, xq)], (from_sib, from_far, to_far, mine, done), ls, ss, rs
-    )
-    red.start()
-    red.add_near()
-    red.add_far(lambda total, r: xq[r].astype(f32) + bias[...] + total)
-    red.finish()
-
-
-def reduce_out(np_, part, xg, bias, collective_id=2):
-    rows = part.shape[1]
-    any_ = pl.BlockSpec(memory_space=pl.ANY)
-    return pl.pallas_call(
-        functools.partial(reduce_out_kernel, np_),
-        out_shape=sds((rows, D), bf16),
-        in_specs=[any_, any_, pl.BlockSpec(memory_space=pltpu.VMEM)],
-        out_specs=any_,
-        scratch_shapes=reduce_scratch(rows, 1),
-        compiler_params=pltpu.CompilerParams(
-            collective_id=collective_id, has_side_effects=True, vmem_limit_bytes=VMEM_BYTES
-        ),
-        name="reduce_out",
-    )(part, xg, bias)
+class ReduceQuarters(Reduce):
+    def __init__(self, part, out, bufs, ls, ss, rs):
+        from_sib, from_far, to_far, done = bufs
+        super().__init__(part, out, [], (from_sib, from_far, to_far, None, done), ls, ss, rs)
+
+    def ready(self, q):
+        for t, mine in ((0, self.sib_there), (1, self.sib_here)):
+            @pl.when(mine == q)
+            def _():
+                for j in range(PIECES):
+                    self.to_sib(t, j).start()
+
+    def push(self, q):
+        @pl.when(self.q_there == q)
+        def _():
+            for j in range(PIECES):
+                r = self.rows_of(j)
+                self.to_sib(0, j).wait_recv()
+                total = self.part[q, r].astype(f32) + self.from_sib[0, r].astype(f32)
+                self.to_far[r] = total.astype(bf16)
+                self.across(j).start()
+
+    def pull(self, q, finish):
+        @pl.when(self.q_here == q)
+        def _():
+            for j in range(PIECES):
+                r = self.rows_of(j)
+                self.to_sib(1, j).wait_recv()
+                self.across(j).wait_recv()
+                total = self.part[q, r].astype(f32) + self.from_sib[1, r].astype(f32)
+                total = total + self.from_far[r].astype(f32)
+                self.done[r] = finish(total, r).astype(bf16)
+
+                @pl.when(jnp.logical_not(self.self_owner))
+                def _():
+                    self.home(j).start()
 
 
 class Swap:
@@ -983,57 +1168,6 @@
     return dy.astype(f32) + back
 
 
-def tail_kernel(
-    np_, part, xg, dyg, sums, dw1, dw2, dw, dwo,
-    out, sums_all, r1, r2, rq, ro,
-    from_sib, from_far, to_far, mine, done, xq, dyq, ls, ss, rs,
-    ls_s, ss_s, rs_s, ls_g, ss_g, rs_g,
-):
-    d, z, c, pair, g, y = place()
-    barrier_all(np_, d, z, c, pair)
-    red = Reduce(
-        part, out, [(xg, xq), (dyg, dyq)], (from_sib, from_far, to_far, mine, done), ls, ss, rs
-    )
-    grp = Group(sums, sums_all, ls_g, ss_g, rs_g)
-    swap = Swap(np_, [(dw, rq), (dw1, r1), (dw2, r2)], (dwo, ro), ls_s, ss_s, rs_s)
-    red.start()
-    grp.start()
-    swap.start()
-    red.add_near()
-    red.add_far(lambda total, r: norm_back(total, xq[r], dyq[r]))
-    grp.finish()
-    red.finish()
-    swap.finish()
-
-
-def tail(np_, part, xg, dyg, sums, dw1, dw2, dw, dwo, collective_id=3):
-    rows = part.shape[1]
-    any_ = pl.BlockSpec(memory_space=pl.ANY)
-    wo_rows = dwo.shape[1]
-    return pl.pallas_call(
-        functools.partial(tail_kernel, np_),
-        out_shape=(
-            sds((rows, D), bf16), sds((4,) + sums.shape, f32),
-            sds(dw1.shape, bf16), sds(dw2.shape, bf16), sds(dw.shape, bf16),
-            sds((np_, wo_rows, D), bf16),
-        ),
-        in_specs=[any_] * 8,
-        out_specs=(any_,) * 6,
-        scratch_shapes=reduce_scratch(rows, 2) + [
-            pltpu.SemaphoreType.DMA((4,)),
-            pltpu.SemaphoreType.DMA((4, np_)),
-            pltpu.SemaphoreType.DMA((4, np_)),
-            pltpu.SemaphoreType.DMA,
-            pltpu.SemaphoreType.DMA((3,)),
-            pltpu.SemaphoreType.DMA((3,)),
-        ],
-        compiler_params=pltpu.CompilerParams(
-            collective_id=collective_id, has_side_effects=True, vmem_limit_bytes=VMEM_BYTES
-        ),
-        name="tail",
-    )(part, xg, dyg, sums, dw1, dw2, dw, dwo)
-
-
 def same_slice_peer(np_, e):
     d, z, c, pair, g, y = place()
     to = lax.rem(pair * 2 + g + e, 2 * np_)
@@ -1041,11 +1175,62 @@
     return to, (2 * pair2 + c, jnp.where(g2 == g, z, 3 - z))
 
 
-def clip_kernel(
-    np_, msg, r1, r2, rq, ro,
-    t1, tq, t2, to, pieces,
-    b1, bq, b2, bo, s1, sq, s2, so, m_all, p_out, ls, ss_m, rs_m, ss, rs,
-):
+def one_hot_tables(np_, r_in, r_ff, part):
+    f = np.arange(D)
+    lane = np.arange(PAD)
+    place_qkv = (f // part) * D + f % part
+    tables_ = [f % r_in, f % r_ff] + [(place_qkv + k * part) % (3 * r_in) for k in range(4)]
+    hot = np.stack([(t[:, None] == lane[None, :]) for t in tables_]).astype(np.float32)
+    hot[2:, 3 * part :] = 0.0
+    return jnp.asarray(hot, bf16), jnp.asarray(place_qkv[None], jnp.int32)
+
+
+def pieces_of(np_, sums_all, sums, hot_ref, qkv_at, r_in, r_ff, part, msg):
+    d, z, c, pair, g, y = place()
+    n = 2 * np_
+    e = lax.broadcasted_iota(jnp.int32, (n, D), 0)
+    f = lax.broadcasted_iota(jnp.int32, (n, D), 1)
+    group = lax.rem(e, 2)
+    index = (lax.div(e, 2) * 2 + c) * 4 + jnp.where(group == 0, y, 3 - y)
+
+    def select(rows_, inside, hot):
+        picked = []
+        for row in rows_:
+            for v in split3(row):
+                picked.append(jnp.where(inside, v, 0.0))
+        got = dot(jnp.concatenate(picked, axis=0).astype(bf16), hot)
+        return [
+            got[3 * s * n : (3 * s + 1) * n] + got[(3 * s + 1) * n : (3 * s + 2) * n]
+            + got[(3 * s + 2) * n : (3 * s + 3) * n]
+            for s in range(len(rows_))
+        ]
+
+    d_vecs = sums_all[0, 0:4] + sums_all[1, 0:4] + sums_all[2, 0:4] + sums_all[3, 0:4]
+    rows_ = [d_vecs[s : s + 1] for s in range(4)] + [sums[6:7]]
+    inside = jnp.logical_and(f >= index * r_in, f < (index + 1) * r_in)
+    got = select(rows_, inside, hot_ref[0])
+    first = got[0]
+    for s in range(1, 5):
+        first = first + pltpu.roll(got[s], s * r_in, 1)
+    second = jnp.zeros((n, PAD), f32)
+    for k in range(4):
+        at = qkv_at[...] + k * part
+        inside = jnp.logical_and(at >= index * (3 * r_in), at < (index + 1) * (3 * r_in))
+        second = second + select([sums_all[k, 5:6]], inside, hot_ref[2 + k])[0]
+    inside = jnp.logical_and(f >= e * r_ff, f < (e + 1) * r_ff)
+    third = select([sums[4:5]], inside, hot_ref[1])[0]
+    squares = squares_of(d_vecs) + 2.0 * squares_of(sums[6:7])
+    for k in range(4):
+        squares = squares + squares_of(sums_all[k, 4:6]) + sums_all[k, 7:8, 0:1]
+    for s in range(n):
+        msg[s, 0:1] = first[s : s + 1]
+        msg[s, 1:2] = second[s : s + 1]
+        msg[s, 2:3] = third[s : s + 1]
+        msg[s, 3:4] = jnp.broadcast_to(squares, (1, PAD))
+        msg[s, 4:8] = jnp.zeros((4, PAD), f32)
+
+
+def meet(np_):
     d, z, c, pair, g, y = place()
     bar = pltpu.get_barrier_semaphore()
     for o in range(1, 8):
@@ -1054,30 +1239,35 @@
     for e in range(1, 2 * np_):
         unused, peer = same_slice_peer(np_, e)
         pl.semaphore_signal(bar, inc=1, device_id=peer, device_id_type=MESH)
-    loads = [
-        pltpu.make_async_copy(src, dst, ls.at[n])
-        for n, (src, dst) in enumerate(((rq, bq), (r1, b1), (r2, b2), (ro, bo)))
-    ]
-    per = np_ // 4
-    collects = lax.div(pair, per) == 2 * y + c
-    for cp in loads[:3]:
-        cp.start()
-
-    @pl.when(collects)
-    def _():
-        loads[3].start()
-
+    pl.semaphore_wait(bar, 7 + 2 * np_ - 1)
+
+
+def finish_all(
+    np_, r_in, r_ff, part_w, red_out, red, swap1, back,
+    dw, dwo, sums, hot_ref, qkv_at, t1, tq, t2, to, pieces,
+    ls_w, ss_w, rs_w, sums_all, ls_g, ss_g, rs_g,
+    b1, bq, b2, bo, s1, sq, s2, so, msg, m_all, p_out, ls, ss_m, rs_m, ss, rs,
+):
+    d, z, c, pair, g, y = place()
+    grp = Group(sums, sums_all, ls_g, ss_g, rs_g)
+    swap = Swap(np_, [(dw, bq)], (dwo, bo), ls_w, ss_w, rs_w)
+    grp.start()
+    swap.start()
+    red.pull(3, back)
+    grp.finish()
+    pieces_of(np_, sums_all, sums, hot_ref, qkv_at, r_in, r_ff, part_w, msg)
     me = pair * 2 + g
-    pl.semaphore_wait(bar, 7 + 2 * np_ - 1)
 
     def tell(e):
         to_, peer = same_slice_peer(np_, e)
         return rcopy(msg.at[to_], m_all.at[me], ss_m.at[e], rs_m.at[e], peer)
 
-    own = pltpu.make_async_copy(msg.at[me], m_all.at[me], ls.at[4])
+    own = pltpu.make_async_copy(msg.at[me], m_all.at[me], ls.at[0])
     own.start()
     for e in range(1, 2 * np_):
         tell(e).start()
+    red.pull(2, back)
+    red.pull(1, back)
     own.wait()
     for e in range(1, 2 * np_):
         tell(e).wait()
@@ -1089,8 +1279,10 @@
     group_factors = [
         jnp.where(g == 0, factors[2 * n], factors[2 * n + 1]) for n in range(np_)
     ]
-    for cp in loads[:3]:
-        cp.wait()
+    final = pltpu.make_async_copy(p_out, pieces, ls.at[9])
+    final.start()
+    collects = swap.collects(pair)
+    swap1.finish()
 
     def rows_to(s, src, dst, o, slot):
         c2, z2 = column_peer(pair, c, z, o)
@@ -1100,21 +1292,26 @@
             src.at[c2, z2], dst.at[slot], ss.at[s, o], rs.at[s, o], (2 * pair + c2, z2)
         )
 
-    for n, (buf, acc, dst) in enumerate(((bq, sq, tq), (b1, s1, t1))):
+    def scaled(n, buf, acc, dst):
         for c2 in range(2):
             for z2 in range(4):
-                total = sum(f * buf[m, c2, z2].astype(f32) for m, f in enumerate(group_factors))
+                at = pl.ds((c2 * 4 + z2) * r_in, r_in)
+                total = sum(f * buf[m, at].astype(f32) for m, f in enumerate(group_factors))
                 acc[c2, z2] = total.astype(acc.dtype)
         for o in range(8):
             rows_to(n, acc, dst, o, c * 4 + z).start()
 
     for t in range(2):
-        total = sum(f * b2[m, t].astype(f32) for m, f in enumerate(group_factors))
+        at = pl.ds(t * r_ff, r_ff)
+        total = sum(f * b2[m, at].astype(f32) for m, f in enumerate(group_factors))
         s2[t] = total.astype(s2.dtype)
     mirror_copy = rcopy(s2.at[1 - g], t2.at[1], ss.at[2, 0], rs.at[2, 0], (d, 3 - z))
     mirror_copy.start()
     kept = pltpu.make_async_copy(s2.at[g], t2.at[0], ls.at[7])
     kept.start()
+    scaled(1, b1, s1, t1)
+    swap.finish()
+    scaled(0, bq, sq, tq)
 
     def wo_to(o):
         c2, z2 = column_peer(pair, c, z, o)
@@ -1126,16 +1323,15 @@
 
     @pl.when(collects)
     def _():
-        loads[3].wait()
         for c2 in range(2):
             for z2 in range(4):
-                total = sum(f * bo[m, c2, z2].astype(f32) for m, f in enumerate(group_factors))
+                at = pl.ds((c2 * 4 + z2) * r_in, r_in)
+                total = sum(f * bo[m, at].astype(f32) for m, f in enumerate(group_factors))
                 so[c2, z2] = total.astype(so.dtype)
         for o in range(8):
             wo_to(o).start()
 
-    final = pltpu.make_async_copy(p_out, pieces, ls.at[9])
-    final.start()
+    red.pull(0, back)
     for n, (acc, dst) in enumerate(((sq, tq), (s1, t1))):
         for o in range(8):
             rows_to(n, acc, dst, o, c * 4 + z).wait()
@@ -1154,32 +1350,8 @@
             rcopy(so.at[0, 0], to.at[t], ss.at[3, 0], rs.at[3, t], (d, 3 - z)).wait_recv()
 
     final.wait()
-
-
-def clip(np_, msg, r1, r2, rq, ro, collective_id=4):
-    any_ = pl.BlockSpec(memory_space=pl.ANY)
-    dma = pltpu.SemaphoreType.DMA
-    return pl.pallas_call(
-        functools.partial(clip_kernel, np_),
-        out_shape=(
-            sds((8,) + r1.shape[3:], bf16), sds((8,) + rq.shape[3:], bf16),
-            sds((2,) + r2.shape[2:], bf16), sds((2,) + ro.shape[3:], bf16), sds(msg.shape[1:], f32),
-        ),
-        in_specs=[any_] * 5,
-        out_specs=(any_,) * 5,
-        scratch_shapes=[
-            pltpu.VMEM(r1.shape, bf16), pltpu.VMEM(rq.shape, bf16), pltpu.VMEM(r2.shape, bf16),
-            pltpu.VMEM(ro.shape, bf16),
-            pltpu.VMEM(r1.shape[1:], bf16), pltpu.VMEM(rq.shape[1:], bf16),
-            pltpu.VMEM(r2.shape[1:], bf16), pltpu.VMEM(ro.shape[1:], bf16),
-            pltpu.VMEM(msg.shape, f32), pltpu.VMEM(msg.shape[1:], f32),
-            dma((10,)), dma((2 * np_,)), dma((2 * np_,)), dma((4, 8)), dma((4, 8)),
-        ],
-        compiler_params=pltpu.CompilerParams(
-            collective_id=collective_id, has_side_effects=True, vmem_limit_bytes=VMEM_BYTES
-        ),
-        name="clip",
-    )(msg, r1, r2, rq, ro)
+    red_out.finish()
+    red.finish()
 
 
 def local(
@@ -1191,7 +1363,6 @@
     np_ = dp // 2
     world = dp * tp
     d, z, c, pair, g, y = place()
-    slice_at = 2 * y + c
     nh = HEADS // tp
     local_rows = block_in.shape[1]
     t = local_rows * tp
@@ -1210,85 +1381,32 @@
     w1 = jnp.stack([w1[:, :, :, s] for s in (0, 3, 1, 2)], axis=3)
     w1 = w1.reshape(r_in, np_, 2, 2, 2, r_ff).transpose(3, 2, 0, 1, 4, 5).reshape(tp, r_in, ff)
     length_parts = jnp.stack([lengths[0] // 256, lengths[0] % 256]).astype(bf16)
-    vectors = jnp.concatenate(
-        [
-            ln1_gain, ln1_bias, out_bias, ln2_gain, ln2_bias, fc2_bias, qkv_bias, fc1_bias,
-            length_parts,
-        ]
+    packed, at = jnp.zeros((16 * PAD,), bf16), 0
+    for row_of in (
+        (ln1_gain, ln1_bias, out_bias, ln2_gain, ln2_bias), (fc2_bias, qkv_bias),
+        (fc1_bias, length_parts),
+    ):
+        start = at
+        for one in row_of:
+            packed = packed + jnp.pad(one, (start, 16 * PAD - start - one.shape[0]))
+            start += one.shape[0]
+        at += PAD
+    xq, w_qkv, w1, tab, b_pad, length = gather(
+        np_, r_in, r_ff, nh, x_own, w_qkv, w1, packed.reshape(16, PAD)
     )
-    n_vec = 9 * r_in + r_ff
-    vectors = jnp.pad(vectors, (0, 16 * PAD - n_vec - 2)).reshape(16, PAD)
-
-    x, dy, w_qkv, w1, w2, wo, vectors = gather(
-        np_, x_own, dy_own, w_qkv, w1, fc2_weight, out_weight, vectors
+    x = xq.reshape(t, D)
+    w_qkv, w1 = w_qkv.reshape(D, 3 * part), w1.reshape(D, ff)
+    cosine, sine = tables(t)
+    q, k, v, cf, ctx, dyq, w2, wo = attn_fwd(
+        np_, length, x, tab, w_qkv, b_pad, cosine, sine, dy_own, fc2_weight, out_weight, nh, rows
     )
-    xq, dyq = x, dy
-    x, dy = x.reshape(t, D), dy.reshape(t, D)
-    w_qkv = w_qkv.reshape(D, 3 * part)
-    w1, w2, wo = w1.reshape(D, ff), w2.reshape(ff, D), wo.reshape(part, D)
-    vectors = vectors.reshape(np_, 2, tp, 16 * PAD).astype(f32)
-    lengths_here = lax.dynamic_slice(vectors, (pair, g, 0, n_vec), (1, 1, 1, 2)).reshape(2)
-    length = (lengths_here[0] * 256.0 + lengths_here[1]).astype(jnp.int32).reshape(1)
-    b_up = lax.dynamic_slice_in_dim(vectors, c, 1, axis=1)[:, 0, :, 9 * r_in : n_vec]
-    b_up = jnp.where(
-        y == 0,
-        jnp.stack([b_up[:, 0], b_up[:, 3]], axis=1),
-        jnp.stack([b_up[:, 1], b_up[:, 2]], axis=1),
-    ).reshape(1, ff)
-    vectors = vectors.reshape(world, 16 * PAD)
-    g1, b1, b_out, g2, b2, b_down = [
-        vectors[:, s * r_in : (s + 1) * r_in].reshape(1, D) for s in range(6)
-    ]
-    b_qkv = vectors[:, 6 * r_in : 9 * r_in].reshape(3, tp, part)
-    b_qkv = lax.dynamic_slice_in_dim(b_qkv, slice_at, 1, axis=1).reshape(3 * nh, HEAD_DIM)
-    extra = np.zeros((3 * nh, PAD - HEAD_DIM), np.float32)
-    extra[:nh, 0] = HEAD_DIM**0.5
-    extra[nh : 2 * nh, 1:4] = 1.0
-    extra[2 * nh :, 0:3] = 1.0
-    b_pad = jnp.concatenate([b_qkv, jnp.asarray(extra)], axis=1).reshape(1, 3 * nh * PAD)
-    cosine, sine = tables(t)
-
-    q, k, v, cf, ctx = attn_fwd(length, x, g1, b1, w_qkv, b_pad, cosine, sine, nh, rows)
-    out_part, u_mlp, dw1, dw2, vec = mlp(x, dy, ctx, g2, b2, wo, w1, b_up, w2, rows // 2)
-    block_out = reduce_out(np_, out_part.reshape(4, local_rows, D), xq, b_out + b_down)
-    u_part, dw, dwo, vec = attn_bwd(
-        x, dy, cf, ctx, u_mlp, q, k, v, g1, b1, w_qkv, wo, cosine, sine, vec, rows
-    )
-    per = np_ // 4
-    input_grad, sums, r1, r2, rq, ro = tail(
-        np_, u_part.reshape(4, local_rows, D), xq, dyq, vec,
-        dw1.reshape(np_, D // np_, ff), dw2.reshape(np_, 2 * r_ff, D),
-        dw.reshape(np_, D // np_, 3 * part), dwo.reshape(per, part // per, D),
-    )
-    d_vecs = jnp.concatenate([jnp.sum(sums[:, :4], axis=0), sums[:1, 6]], axis=0)
-    squares = (
-        jnp.sum(d_vecs * d_vecs) + jnp.sum(sums[0, 6] * sums[0, 6])
-        + jnp.sum(sums[:, 4] * sums[:, 4]) + jnp.sum(sums[:, 5] * sums[:, 5])
-        + jnp.sum(sums[:, 7, 0])
-    )
-
-    def for_owners(m):
-        m = lax.dynamic_index_in_dim(m, c, axis=m.ndim - 3, keepdims=False)
-        m = jnp.where(
-            y == 0,
-            jnp.stack([m[..., 0, :], m[..., 3, :]], axis=-2),
-            jnp.stack([m[..., 1, :], m[..., 2, :]], axis=-2),
-        )
-        return m
-
-    p_vecs = jnp.moveaxis(for_owners(d_vecs.reshape(5, np_, 2, tp, r_in)), 0, 2)
-    p_vecs = p_vecs.reshape(np_, 2, 5 * r_in)
-    p_qkv = sums[:, 5, : 3 * part].reshape(tp, 3, part).swapaxes(0, 1)
-    p_qkv = for_owners(p_qkv.reshape(np_, 2, tp, 3 * r_in))
-    p_up = vec[4].reshape(np_, 2, r_ff)
-    msg = jnp.stack(
-        [jnp.pad(m, ((0, 0), (0, 0), (0, PAD - m.shape[2]))) for m in (p_vecs, p_qkv, p_up)]
-        + [jnp.broadcast_to(squares, (np_, 2, PAD))] + [jnp.zeros((np_, 2, PAD), f32)] * 4,
-        axis=2,
-    ).reshape(2 * np_, 8, PAD)
-    t1, tq, t2, to, mine = clip(
-        np_, msg, r1.reshape(np_, 2, tp, r_in, ff), r2.reshape(np_, 2, r_ff, D),
-        rq.reshape(np_, 2, tp, r_in, 3 * part), ro.reshape(np_, 2, tp, r_in, D),
+    dy = dyq.reshape(t, D)
+    w2, wo = w2.reshape(ff, D), wo.reshape(part, D)
+    out_part, u_mlp, dw1, dw2, vec = mlp(x, dy, ctx, tab, wo, w1, w2, rows // 2)
+    block_out, input_grad, t1, tq, t2, to, mine = attn_bwd(
+        np_, r_in, r_ff, x, dy, cf, ctx, u_mlp, q, k, v, tab, w_qkv, wo, cosine, sine, vec,
+        out_part.reshape(4, local_rows, D), xq, dyq, dw1.reshape(np_, D // np_, ff),
+        dw2.reshape(np_, 2 * r_ff, D), rows,
     )
     t1 = t1.reshape(2, tp, r_in, ff).astype(f32)
     t1 = jnp.stack([t1[:, 0] + t1[:, 3], t1[:, 1] + t1[:, 2]], axis=1)

time: 343 us -> 259 us (0.76); the launches traced: 339 us -> 259 us
  Pallas kernels: 296 us -> 234 us
  local copies, waits for them, and re-layouts: 24.8 us -> 15.3 us
  between operations: 6.47 us -> 1.58 us
  other arithmetic: 11.7 us -> 7.85 us
    pallas_call x6 -> x3, Pallas kernels: 268 us -> 205 us  [the longest x1 105 us: attn_bwd(): pl.pallas_call(functools.partial(attn_bwd_kernel, np_, r_in, r_ff), grid=...]
    reduce_sum x5 -> x0, other arithmetic: 5.81 us -> none  [the longest x1 1.61 us: local(): jnp.sum(sums[:, 5] * sums[:, 5])]
    reshape x10 -> x0, local copies, waits for them, and re-layouts: 4.28 us -> none  [the longest x4 2.67 us: local(): vectors[:, s * r_in:(s + 1) * r_in].reshape(1, D)]
where the time goes in v3:
time: 259 us
  Pallas kernels  234 us (90%)
  local copies, waits for them, and re-layouts  15.3 us (6%)
  other arithmetic  7.85 us (3%)
    pallas_call x1, Pallas kernels, attn_bwd(): pl.pallas_call(functools.partial(attn_bwd_kernel, np_, r_in, r_ff), grid=...  105 us
    pallas_call x1, Pallas kernels, gather(): pl.pallas_call(functools.partial(gather_kernel, np_, r_in, r_ff), out_sha...  52.1 us
    pallas_call x1, Pallas kernels, attn_fwd(): pl.pallas_call(functools.partial(attn_fwd_kernel, np_), grid=(t // rows,)...  48.7 us
    pallas_call x1, Pallas kernels, mlp(): pl.pallas_call(mlp_kernel, grid=(t // rows,), out_shape=(sds((t, D), bf16...  28.7 us

profile of v3, /device:TPU:1, one launch (start us, length us, event | category | flops | bytes accessed | tf_op | source)
XLA Modules:
  0.0 258.8 jit_solution(8593137136781866835)
XLA Ops:
  1.3 1.5 fusion.8.vec_own
  2.8 1.1 reshape.134
  4.0 0.8 reshape.135.wq
  4.8 1.1 reshape.136
  6.2 0.4 pad_maximum_fusion.1
  6.8 0.8 reshape.138.w1
  7.7 1.0 bitcast_select_fusion.dy
  8.7 52.1 %gather.1 = (bf16[4,512,768]{2,1,0:T(8,128)(2,1)}, bf16[4,2,4,24,576]{4,3,2,1,0:T(8,128)(2,1)}, bf16[4,2,4,24,768]{4,3,2,1,0:T(8,128)(2,1)}, f32[8,768]{1,0:T(8,...) custom-call(bf16[512,768]{1,0:T(8,128)(2,1)} %bitcast.92, bf16[4,24,576]{2,1,0:T(8,128)(2,1)} %reshape.135.wq, ...), custom_call_target="tpu_custom_call" | custom-call | tf_op jit(solution)/shard_map/gather/pallas_call | solution.py:891
  60.8 48.7 %attn_fwd.1 = (bf16[3,2048,128]{2,1,0:T(8,128)(2,1)}, bf16[3,2048,128]{2,1,0:T(8,128)(2,1)}, bf16[3,2048,128]{2,1,0:T(8,128)(2,1)}, f32[2048,384]{1,0:T(8,128)},...) custom-call(f32[1,128]{1,0:T(1,128)} %get-tuple-element.42.len_ref, ...), custom_call_target="tpu_custom_call" | custom-call | tf_op jit(solution)/shard_map/attn_fwd/pallas_call | solution.py:367
  109.6 28.7 %mlp.1 = (bf16[2048,768]{1,0:T(8,128)(2,1)}, f32[2048,768]{1,0:T(8,128)}, bf16[768,768]{1,0:T(8,128)(2,1)}, bf16[768,768]{1,0:T(8,128)(2,1)}, f32[8,768]{1,0:T(8,128)}) custom-call(bf16[2048,768]{1,0:T(8,128)(2,1)} %bitcast.75, bf16[2048,768]{1,0:T(8,128)(2,1)} %bitcast.77, bf16[2048,192]{1,0:T(8,128)(2,1)} %get-tuple-element.48.c_ref, ...), custom_call_target="tpu_custom_call" | custom-call | tf_op jit(solution)/shard_map/mlp/pallas_call | solution.py:405
  138.2 104.6 %attn_bwd.1 = (bf16[512,768]{1,0:T(8,128)(2,1)}, bf16[512,768]{1,0:T(8,128)(2,1)}, bf16[8,24,768]{2,1,0:T(8,128)(2,1)}, bf16[8,24,576]{2,1,0:T(8,128)(2,1)}, bf1...) custom-call(bf16[2048,768]{1,0:T(8,128)(2,1)} %bitcast.76, bf16[2048,768]{1,0:T(8,128)(2,1)} %bitcast.78, ...), custom_call_target="tpu_custom_call" | custom-call | tf_op jit(solution)/shard_map/attn_bwd/pallas_call | solution.py:443
  242.8 1.2 slice.97
  244.0 1.2 slice_bitcast_fusion.2
  245.2 1.2 slice_bitcast_fusion.6
  246.4 1.5 slice_bitcast_fusion.3
  247.9 1.5 convert_reduce_fusion.1
  249.4 1.7 convert_reduce_fusion
  251.1 1.0 convert.12
  253.4 0.4 maximum_bitcast_fusion
  253.8 1.1 reshape.151
  255.7 0.9 reshape.150
  256.6 0.5 copy.76
  257.1 0.9 copy.77
  258.0 0.9 copy.78
  (30 shorter events, 2.5 us)
Async XLA Ops:
  3.9 3.8 %copy-start = (bf16[1,512,768]{2,1,0:T(8,128)(2,1)S(1)}, bf16[1,512,768]{2,1,0:T(8,128)(2,1)}, u32[]{:S(2)}) copy-start(bf16[1,512,768]{2,1,0:T(8,128)(2,1)} %param.23) | copy-start | bytes 2359300
  247.9 8.7 %copy-start.4 = (f32[24]{0:T(128)}, f32[24]{0:T(128)S(1)}, u32[]{:S(2)}) copy-start(f32[24]{0:T(128)S(1)} %get-tuple-element.132) | copy-start | bytes 292
  252.6 2.3 copy-start.3
  255.2 1.8 copy-start.2
  255.5 2.5 copy-start.1

commit v4 on v3

--- a/solution.py
+++ b/solution.py
@@ -62,7 +62,7 @@
     nh = k_ref.shape[0]
     rows = x_ref.shape[0]
     spread = Spread(dy, dyg, ls_dy, ss_dy, rs_dy)
-    weights = Weights(np_, [], (w2, w2g), (wo, wog), ls_w, ss_w, rs_w)
+    weights = Rows(np_, (w2, w2g), (wo, wog), ls_w, ss_w, rs_w)
 
     @pl.when(i == 0)
     def _():
@@ -71,18 +71,13 @@
         weights.start()
         spread.start()
 
-    @pl.when(i == 1)
-    def _():
-        weights.between_wo()
-        weights.between_w2()
-
     @pl.when(i == 2)
     def _():
-        spread.forward(0)
+        spread.forward(1)
 
     @pl.when(i == 3)
     def _():
-        spread.forward(1)
+        spread.forward(3)
 
     @pl.when(i == 0)
     def _():
@@ -124,6 +119,15 @@
         return carry
 
     lax.fori_loop(0, i, scores, 0)
+
+    @pl.when(i == 1)
+    def _():
+        spread.forward(0)
+
+    @pl.when(i == 2)
+    def _():
+        spread.forward(2)
+
     for h in range(nh):
         m_scr[h] = jnp.broadcast_to(jnp.max(m_scr[h], axis=-1, keepdims=True), (rows, PAD))
         l_scr[h] = jnp.zeros((rows, PAD), f32)
@@ -153,8 +157,7 @@
     @pl.when(i == pl.num_programs(0) - 1)
     def _():
         spread.finish()
-        weights.finish_wo()
-        weights.finish_w2()
+        weights.finish()
 
 
 def squares_of(m):
@@ -162,98 +165,40 @@
 
 
 def mlp_kernel(
-    x_ref, dy_ref, c_ref, tab_ref, wo_ref, w1_ref, w2_ref,
-    part_ref, u_ref, dw1_ref, dw2_ref, vec_ref, dw1_scr, dw2_scr,
+    x_ref, dy_ref, c_ref, cf_ref, tab_ref, wo_ref, w1_ref, w2_ref,
+    part_ref, u_ref, dc_ref, dw1_ref, dw2_ref, dwo_ref, vec_ref,
+    dw1_scr, dw2_scr, dwo_scr, wo_scr,
 ):
     i = pl.program_id(0)
+    nh = wo_ref.shape[0] // HEAD_DIM
+    rows = x_ref.shape[0]
+
+    @pl.when(i == 0)
+    def _():
+        dw1_scr[...] = jnp.zeros_like(dw1_scr)
+        dw2_scr[...] = jnp.zeros_like(dw2_scr)
+        dwo_scr[...] = jnp.zeros_like(dwo_scr)
+        vec_ref[...] = jnp.zeros_like(vec_ref)
+        for h in range(nh):
+            wo_scr[h * PAD : h * PAD + HEAD_DIM] = wo_ref[h * HEAD_DIM : (h + 1) * HEAD_DIM]
+            wo_scr[h * PAD + HEAD_DIM : (h + 1) * PAD] = jnp.zeros((PAD - HEAD_DIM, D), bf16)
+
     xhat, unused = norm_parts(x_ref[...].astype(f32))
     gain = tab_ref[3:4]
     a2 = (xhat * gain + tab_ref[4:5]).astype(bf16)
     z = dot(a2, w1_ref[...]) + tab_ref[5:6]
     cdf = 0.5 * (1.0 + lax.erf(z * root_half))
     hidden = (z * cdf).astype(bf16)
-    part = dot(hidden, w2_ref[...]) + dot(c_ref[...], wo_ref[...])
+    context = c_ref[...]
+    part = dot(hidden, w2_ref[...]) + dot(context, wo_ref[...])
     part_ref[...] = part.astype(part_ref.dtype)
     dy = dy_ref[...]
     slope = cdf + z * jnp.exp(-0.5 * z * z) * inv_root_two_pi
     dz = (dot(dy, w2_ref[...], ((1,), (1,))) * slope).astype(bf16)
+
     da2 = dot(dz, w1_ref[...], ((1,), (1,)))
     u_ref[...] = (da2 * gain).astype(u_ref.dtype)
-
-    @pl.when(i == 0)
-    def _():
-        dw1_scr[...] = jnp.zeros_like(dw1_scr)
-        dw2_scr[...] = jnp.zeros_like(dw2_scr)
-        vec_ref[...] = jnp.zeros_like(vec_ref)
-
-    dw1_scr[...] += dot(a2, dz, ((0,), (0,)))
-    dw2_scr[...] += dot(hidden, dy, ((0,), (0,)))
-    vec_ref[2:3] += jnp.sum(da2 * xhat, axis=0, keepdims=True)
-    vec_ref[3:4] += jnp.sum(da2, axis=0, keepdims=True)
-    vec_ref[4:5] += jnp.sum(dz.astype(f32), axis=0, keepdims=True)
-    vec_ref[6:7] += jnp.sum(dy.astype(f32), axis=0, keepdims=True)
-
-    @pl.when(i == pl.num_programs(0) - 1)
-    def _():
-        dw1_ref[...] = dw1_scr[...].astype(bf16)
-        dw2_ref[...] = dw2_scr[...].astype(bf16)
-        vec_ref[7:8, 0:1] = squares_of(dw1_scr[...]) + squares_of(dw2_scr[...])
-
-
-def attn_bwd_kernel(
-    np_, r_in, r_ff, x_ref, dy_ref, cf_ref, c_ref, u_in_ref, q_ref, k_ref, v_ref, tab_ref, w_ref,
-    wo_ref, cos_ref, sin_ref, vec_in_ref, hot_ref, qkv_at, part, xg, dyg, dw1, dw2,
-    block_out, input_grad, t1, tq, t2, to, pieces,
-    wo_scr, dk_scr, dv_scr, dq_scr, dc_scr, dqkv_scr, dw_scr, dwo_scr, vec_ref, u_scr, dw, dwo,
-    from_sib, from_far, to_far, mine, done, xq, ls_o, ss_o, rs_o,
-    from_sib2, from_far2, to_far2, done2, dyq, ls_u, ss_u, rs_u,
-    ls_s, ss_s, rs_s, ls_w, ss_w, rs_w, sums_all, ls_g, ss_g, rs_g,
-    b1, bq, b2, bo, s1, sq, s2, so, msg, m_all, p_out, ls, ss_m, rs_m, ss, rs,
-):
-    step = pl.program_id(0)
-    blocks = pl.num_programs(0)
-    i = blocks - 1 - step
-    nh = k_ref.shape[0]
-    rows = x_ref.shape[0]
-    wide = 3 * nh * HEAD_DIM
     lane = lax.broadcasted_iota(jnp.int32, (rows, PAD), 1)
-    first = lane < ROT // 2
-    here = pl.ds(pl.multiple_of(i * rows, rows), rows)
-    red = Reduce(
-        part, block_out, [(xg, xq)], (from_sib, from_far, to_far, mine, done), ls_o, ss_o, rs_o
-    )
-    red_u = ReduceQuarters(
-        u_scr, input_grad, (from_sib2, from_far2, to_far2, done2), ls_u, ss_u, rs_u
-    )
-    swap = Swap(np_, [(dw1, b1), (dw2, b2)], None, ls_s, ss_s, rs_s)
-    load_dy = pltpu.make_async_copy(dyg.at[red.q_here], dyq, ls.at[4])
-
-    def back(total, r):
-        return norm_back(total, xq[r], dyq[r])
-
-    @pl.when(step == 0)
-    def _():
-        meet(np_)
-        red.start()
-        load_dy.start()
-        swap.start()
-
-    @pl.when(step == 2)
-    def _():
-        red.add_far(lambda total, r: xq[r].astype(f32) + tab_ref[2:3] + total)
-
-    @pl.when(step == 0)
-    def _():
-        dk_scr[...] = jnp.zeros_like(dk_scr)
-        dv_scr[...] = jnp.zeros_like(dv_scr)
-        dw_scr[...] = jnp.zeros_like(dw_scr)
-        dwo_scr[...] = jnp.zeros_like(dwo_scr)
-        vec_ref[...] = vec_in_ref[...]
-        for h in range(nh):
-            wo_scr[h * PAD : h * PAD + HEAD_DIM] = wo_ref[h * HEAD_DIM : (h + 1) * HEAD_DIM]
-            wo_scr[h * PAD + HEAD_DIM : (h + 1) * PAD] = jnp.zeros((PAD - HEAD_DIM, D), bf16)
-
-    dy = dy_ref[...]
     dc_all = dot(dy, wo_scr[...], ((1,), (1,))).astype(bf16)
     for h in range(nh):
         dc = dc_all[:, h * PAD : (h + 1) * PAD].astype(f32)
@@ -262,45 +207,117 @@
         dc = jnp.where(lane == HEAD_DIM, hi, dc)
         dc = jnp.where(lane == HEAD_DIM + 1, mid, dc)
         dc = jnp.where(lane == HEAD_DIM + 2, low, dc)
-        dc_scr[h] = dc.astype(bf16)
+        dc_ref[h] = dc.astype(bf16)
+    dw1_scr[...] += dot(a2, dz, ((0,), (0,)))
+    dw2_scr[...] += dot(hidden, dy, ((0,), (0,)))
+    dwo_scr[...] += dot(context, dy, ((0,), (0,)))
+    vec_ref[2:3] += jnp.sum(da2 * xhat, axis=0, keepdims=True)
+    vec_ref[3:4] += jnp.sum(da2, axis=0, keepdims=True)
+    vec_ref[4:5] += jnp.sum(dz.astype(f32), axis=0, keepdims=True)
+    vec_ref[6:7] += jnp.sum(dy.astype(f32), axis=0, keepdims=True)
+
+    @pl.when(i == pl.num_programs(0) - 1)
+    def _():
+        dw1_ref[...] = dw1_scr[...].astype(bf16)
+        dw2_ref[...] = dw2_scr[...].astype(bf16)
+        dwo_ref[...] = dwo_scr[...].astype(bf16)
+        vec_ref[7:8, 0:1] = (
+            squares_of(dw1_scr[...]) + squares_of(dw2_scr[...]) + squares_of(dwo_scr[...])
+        )
+
+
+def attn_bwd_kernel(
+    np_, r_in, r_ff, x_ref, u_in_ref, q_ref, k_ref, v_ref, dc_ref, tab_ref, w_ref,
+    cos_ref, sin_ref, vec_in_ref, hot_ref, qkv_at, part, xg, dyg, dw1, dw2, dwo,
+    block_out, input_grad, t1, tq, t2, to, pieces,
+    dk_scr, dv_scr, dq_scr, dqkv_scr, dw_scr, vec_ref, u_scr, dw,
+    from_sib, from_far, to_far, mine, done, xq, ls_o, ss_o, rs_o,
+    from_sib2, from_far2, to_far2, done2, dyq, ls_u, ss_u, rs_u,
+    ls_s, ss_s, rs_s, ls_w, ss_w, rs_w, sums_all, ls_g, ss_g, rs_g,
+    b1, bq, b2, bo, s1, sq, s2, so, msg, m_all, p_out, ls, ss_m, rs_m, ss, rs,
+):
+    step = pl.program_id(0)
+    blocks = pl.num_programs(0)
+    g, y = place()[4:6]
+    b = far_first(step)
+    nh = k_ref.shape[0]
+    rows = x_ref.shape[0]
+    wide = 3 * nh * HEAD_DIM
+    lane = lax.broadcasted_iota(jnp.int32, (rows, PAD), 1)
+    first = lane < ROT // 2
+
+    def block_rows(n):
+        return pl.ds(pl.multiple_of(n * rows, rows), rows)
+
+    here = block_rows(b)
+    red = Reduce(
+        part, block_out, [(xg, xq)], (from_sib, from_far, to_far, mine, done), ls_o, ss_o, rs_o
+    )
+    red_u = ReduceQuarters(
+        u_scr, input_grad, (from_sib2, from_far2, to_far2, done2), ls_u, ss_u, rs_u
+    )
+    swap = Swap(np_, [(dw1, b1), (dw2, b2)], (dwo, bo), ls_s, ss_s, rs_s)
+
+    load_dy = pltpu.make_async_copy(dyg.at[red.q_here], dyq, ls.at[4])
+
+    def back(total, r):
+        return norm_back(total, xq[r], dyq[r])
 
     @pl.when(step == 0)
     def _():
-        red.add_near()
+        meet(np_)
+        red.start()
+        load_dy.start()
+        swap.start()
+        dk_scr[...] = jnp.zeros_like(dk_scr)
+        dv_scr[...] = jnp.zeros_like(dv_scr)
+        dq_scr[...] = jnp.zeros_like(dq_scr)
+        dw_scr[...] = jnp.zeros_like(dw_scr)
+        vec_ref[...] = vec_in_ref[...]
 
     causal = lax.broadcasted_iota(jnp.int32, (rows, rows), 0) <= lax.broadcasted_iota(
         jnp.int32, (rows, rows), 1
     )
 
-    def block(j, diagonal):
-        there = pl.ds(pl.multiple_of(j * rows, rows), rows)
+    def block(n, m, diagonal):
+        asks, keys = block_rows(n), block_rows(m)
         for h in range(nh):
-            k = k_ref[h, there]
-            q = q_ref[h]
-            dc = dc_scr[h]
+            k = k_ref[h, keys]
+            q = q_ref[h, asks]
+            dc = dc_ref[h, asks]
             pt = jnp.exp(dot(k, q, ((1,), (1,))))
             if diagonal:
                 pt = jnp.where(causal, pt, 0.0)
-            dpt = dot(v_ref[h, there], dc, ((1,), (1,)))
+            dpt = dot(v_ref[h, keys], dc, ((1,), (1,)))
             dst = (pt * dpt).astype(bf16)
-            dv_scr[h, there] += dot(pt.astype(bf16), dc)
-            dk_scr[h, there] += dot(dst, q)
-            dq = dot(dst, k, ((0,), (0,)))
-            if diagonal:
-                dq_scr[h] = dq
-            else:
-                dq_scr[h] += dq
-
-    block(i, True)
-
-    def off(j, carry):
-        block(j, False)
+            dv_scr[h, keys] += dot(pt.astype(bf16), dc)
+            dk_scr[h, keys] += dot(dst, q)
+            dq_scr[h, asks] += dot(dst, k, ((0,), (0,)))
+
+    block(b, b, True)
+
+    @pl.when(step == 0)
+    def _():
+        red.add_near()
+
+    def off(n, carry):
+        block(jnp.where(g == 0, b, b + 1 + n), jnp.where(g == 0, n, b), False)
         return carry
 
-    lax.fori_loop(0, i, off, 0)
+    lax.fori_loop(0, blocks - 1 - step, off, 0)
+
+    @pl.when(step == 1)
+    def _():
+        red.add_far(lambda total, r: xq[r].astype(f32) + tab_ref[2:3] + total)
+        load_dy.wait()
+
+    @pl.when(step == 3)
+    def _():
+        red_u.pull(mirror(2, g), back)
+
     cosine, sine = cos_ref[...], -sin_ref[...]
     for h in range(nh):
-        dq = turn(dq_scr[h], cosine, sine, first) * HEAD_DIM**-0.5
+        dq = turn(dq_scr[h, here], cosine, sine, first) * HEAD_DIM**-0.5
         dk = turn(dk_scr[h, here], cosine, sine, first)
         for at, piece in ((h, dq), (nh + h, dk), (2 * nh + h, dv_scr[h, here])):
             dqkv_scr[:, at * HEAD_DIM : (at + 1) * HEAD_DIM] = piece[:, :HEAD_DIM].astype(bf16)
@@ -309,29 +326,34 @@
     gain = tab_ref[0:1]
     a1 = (xhat * gain + tab_ref[1:2]).astype(bf16)
     da1 = dot(dqkv, w_ref[...], ((1,), (1,)))
-    u_scr[i] = (u_in_ref[...] + da1 * gain).astype(bf16)
-    red_u.ready(i)
+    u_scr[b] = (u_in_ref[...] + da1 * gain).astype(bf16)
+
+    @pl.when(step < blocks - 1)
+    def _():
+        red_u.ready(b)
+
     dw_scr[...] += dot(a1, dqkv, ((0,), (0,)))
-    dwo_scr[...] += dot(c_ref[...], dy, ((0,), (0,)))
     vec_ref[0:1] += jnp.sum(da1 * xhat, axis=0, keepdims=True)
     vec_ref[1:2] += jnp.sum(da1, axis=0, keepdims=True)
     vec_ref[5:6, :wide] += jnp.sum(dqkv.astype(f32), axis=0, keepdims=True)
-    red_u.push(i)
+
+    @pl.when(step < blocks - 1)
+    def _():
+        red_u.push(b)
+
+    @pl.when(step == 2)
+    def _():
+        red_u.pull(mirror(3, g), back)
 
     @pl.when(step == blocks - 1)
     def _():
-        vec_ref[7:8, 0:1] += squares_of(dw_scr[...]) + squares_of(dwo_scr[...])
+        vec_ref[7:8, 0:1] += squares_of(dw_scr[...])
         share = D // np_
         for n in range(np_):
             dw[n] = dw_scr[n * share : (n + 1) * share].astype(bf16)
-        per = np_ // 4
-        share_o = dwo_scr.shape[0] // per
-        for n in range(per):
-            dwo[n] = dwo_scr[n * share_o : (n + 1) * share_o].astype(bf16)
-        load_dy.wait()
         finish_all(
             np_, r_in, r_ff, wide // 3, red, red_u, swap, back,
-            dw, dwo, vec_ref, hot_ref, qkv_at, t1, tq, t2, to, pieces,
+            dw, vec_ref, hot_ref, qkv_at, t1, tq, t2, to, pieces,
             ls_w, ss_w, rs_w, sums_all, ls_g, ss_g, rs_g,
             b1, bq, b2, bo, s1, sq, s2, so, msg, m_all, p_out, ls, ss_m, rs_m, ss, rs,
         )
@@ -371,12 +393,12 @@
             sds((nh, t, PAD), bf16), sds((nh, t, PAD), bf16), sds((nh, t, PAD), bf16),
             sds((t, nh * PAD), f32), sds((t, nh * HEAD_DIM), bf16),
             sds((4,) + dy.shape, bf16),
-            sds((np_, 2) + w2.shape, bf16), sds((np_ // 4, 2, 4) + wo.shape, bf16),
+            sds((np_,) + w2.shape, bf16), sds(wo.shape, bf16),
         ),
         in_specs=[
             whole((1, PAD)), pl.BlockSpec((rows, D), lambda i: (i, 0)),
             whole((8, D)), whole(w.shape), whole(wb.shape), lanes, lanes,
-            any_, any_, any_,
+            pl.BlockSpec(memory_space=pltpu.VMEM), any_, any_,
         ],
         out_specs=(
             pl.BlockSpec((nh, rows, PAD), lambda i: (0, i, 0)),
@@ -392,91 +414,131 @@
             pltpu.VMEM((nh, rows, PAD), f32),
             pltpu.VMEM((nh, rows, PAD), f32),
             pltpu.VMEM((nh, rows, PAD), f32),
-        ] + spread_sems() + weight_sems(np_, 2),
+        ] + spread_sems() + swap_sems(np_, 2),
         compiler_params=params(2),
         name="attn_fwd",
     )(length, x, tab, w, wb, cosine, sine, dy, w2, wo)
 
 
-def mlp(x, dy, c, tab, wo, w1, w2, rows):
+def far_first(i):
+    return mirror(3 - i, place()[4])
+
+
+def mlp(x, dy, c, cf, tab, wo, w1, w2, rows):
     t = x.shape[0]
     ff = w1.shape[1]
-    row = pl.BlockSpec((rows, D), lambda i: (i, 0))
+    nh = wo.shape[0] // HEAD_DIM
+    at = lambda cols: pl.BlockSpec((rows, cols), lambda i: (i, 0))
+    vm = pltpu.VMEM
     return pl.pallas_call(
         mlp_kernel,
         grid=(t // rows,),
         out_shape=(
-            sds((t, D), bf16), sds((t, D), f32), sds((D, ff), bf16), sds((ff, D), bf16),
-            sds((8, D), f32),
+            sds((t, D), bf16), sds((t, D), f32), sds((nh, t, PAD), bf16), sds((D, ff), bf16),
+            sds((ff, D), bf16), sds(wo.shape, bf16), sds((8, D), f32),
         ),
         in_specs=[
-            row, row, pl.BlockSpec((rows, c.shape[1]), lambda i: (i, 0)),
+            at(D), at(D), at(c.shape[1]), at(cf.shape[1]),
             whole((8, D)), whole(wo.shape), whole(w1.shape), whole(w2.shape),
         ],
-        out_specs=(row, row, whole((D, ff)), whole((ff, D)), whole((8, D))),
-        scratch_shapes=[pltpu.VMEM((D, ff), f32), pltpu.VMEM((ff, D), f32)],
+        out_specs=(
+            at(D), at(D), pl.BlockSpec((nh, rows, PAD), lambda i: (0, i, 0)),
+            whole((D, ff)), whole((ff, D)), whole(wo.shape), whole((8, D)),
+        ),
+        scratch_shapes=[
+            vm((D, ff), f32), vm((ff, D), f32), vm(wo.shape, f32), vm((nh * PAD, D), bf16),
+        ],
         compiler_params=params(),
         name="mlp",
-    )(x, dy, c, tab, wo, w1, w2)
+    )(x, dy, c, cf, tab, wo, w1, w2)
 
 
 def attn_bwd(
-    np_, r_in, r_ff, x, dy, cf, c, u_in, q, k, v, tab, w, wo, cosine, sine, vec,
-    part, xg, dyg, dw1, dw2, rows,
+    np_, r_in, r_ff, x, u_in, q, k, v, dc, tab, w, cosine, sine, vec,
+    part, xg, dyg, dw1, dw2, dwo,
 ):
     t = x.shape[0]
     nh = q.shape[0]
-    n = t // rows
     wide = w.shape[1]
-    part_w = wide // 3
     quarter = part.shape[1]
     ff = dw1.shape[2]
-    per = np_ // 4
-    row = pl.BlockSpec((rows, D), lambda i: (n - 1 - i, 0))
-    lanes = pl.BlockSpec((rows, PAD), lambda i: (n - 1 - i, 0))
+    at = lambda cols: pl.BlockSpec((quarter, cols), lambda i: (far_first(i), 0))
     any_ = pl.BlockSpec(memory_space=pl.ANY)
     dma = pltpu.SemaphoreType.DMA
     vm = pltpu.VMEM
-    hot, qkv_at = one_hot_tables(np_, r_in, r_ff, part_w)
+    hot, qkv_at = one_hot_tables(np_, r_in, r_ff, wide // 3)
     per_owner = lambda cols: vm((2, 4, r_in, cols), bf16)
     block = vm((quarter, D), bf16)
     return pl.pallas_call(
         functools.partial(attn_bwd_kernel, np_, r_in, r_ff),
-        grid=(n,),
+        grid=(4,),
         out_shape=(
             sds((quarter, D), bf16), sds((quarter, D), bf16), sds((8, r_in, ff), bf16),
             sds((8, r_in, wide), bf16), sds((2, r_ff, D), bf16), sds((2, r_in, D), bf16),
             sds((8, PAD), f32),
         ),
         in_specs=[
-            row, row, pl.BlockSpec((rows, nh * PAD), lambda i: (n - 1 - i, 0)),
-            pl.BlockSpec((rows, nh * HEAD_DIM), lambda i: (n - 1 - i, 0)), row,
-            pl.BlockSpec((nh, rows, PAD), lambda i: (0, n - 1 - i, 0)),
-            whole(k.shape), whole(v.shape), whole((8, D)), whole(w.shape),
-            whole(wo.shape), lanes, lanes, whole((8, D)), whole(hot.shape), whole(qkv_at.shape),
-            any_, any_, any_, any_, any_,
-        ],
+            at(D), at(D), whole(q.shape), whole(k.shape), whole(v.shape), whole(dc.shape),
+            whole((8, D)), whole(w.shape), at(PAD), at(PAD), whole((8, D)), whole(hot.shape),
+            whole(qkv_at.shape),
+        ] + [any_] * 6,
         out_specs=(any_,) * 7,
         scratch_shapes=[
-            vm((nh * PAD, D), bf16), vm((nh, t, PAD), f32), vm((nh, t, PAD), f32),
-            vm((nh, rows, PAD), f32), vm((nh, rows, PAD), bf16), vm((rows, wide), bf16),
-            vm((D, wide), f32), vm((nh * HEAD_DIM, D), f32), vm((8, D), f32),
+            vm((nh, t, PAD), f32), vm((nh, t, PAD), f32), vm((nh, t, PAD), f32),
+            vm((quarter, wide), bf16), vm((D, wide), f32), vm((8, D), f32),
             vm((4, quarter, D), bf16), vm((np_, D // np_, wide), bf16),
-            vm((per, part_w // per, D), bf16),
         ] + reduce_scratch(quarter, 1) + [
             vm((2, quarter, D), bf16), block, block, block, block,
             dma((5,)), dma((4, PIECES)), dma((4, PIECES)),
-        ] + swap_sems(np_, 2) + swap_sems(np_, 2) + [
+        ] + swap_sems(np_, 3) + swap_sems(np_, 1) + [
             vm((4, 8, D), f32), dma, dma((3,)), dma((3,)),
             vm(dw1.shape, bf16), vm((np_, D // np_, wide), bf16), vm(dw2.shape, bf16),
-            vm((np_, part_w // per, D), bf16),
+            vm((np_,) + dwo.shape[1:], bf16),
             per_owner(ff), per_owner(wide), vm((2, r_ff, D), bf16), per_owner(D),
             vm((2 * np_, 8, PAD), f32), vm((2 * np_, 8, PAD), f32), vm((8, PAD), f32),
             dma((10,)), dma((2 * np_,)), dma((2 * np_,)), dma((4, 8)), dma((4, 8)),
         ],
         compiler_params=params(3),
         name="attn_bwd",
-    )(x, dy, cf, c, u_in, q, k, v, tab, w, wo, cosine, sine, vec, hot, qkv_at, part, xg, dyg, dw1, dw2)
+    )(
+        x, u_in, q, k, v, dc, tab, w, cosine, sine, vec, hot, qkv_at,
+        part, xg, dyg, dw1, dw2, dwo,
+    )
+
+
+def assemble_kernel(np_, t1, tq, t2, to, fc1, qkv, fc2, out):
+    r_ff = t2.shape[1]
+    part_w = tq.shape[2] // 3
+    for c in range(2):
+        for y in range(2):
+            a, b = (0, 3) if y == 0 else (1, 2)
+            up = t1[4 * c + a].astype(f32) + t1[4 * c + b].astype(f32)
+            for pair in range(np_):
+                for e, z in enumerate((a, b)):
+                    to_at = r_ff * (4 * (2 * pair + c) + z)
+                    at = r_ff * (2 * pair + e)
+                    fc1[:, to_at : to_at + r_ff] = up[:, at : at + r_ff]
+            into = tq[4 * c + a].astype(f32) + tq[4 * c + b].astype(f32)
+            for s in range(3):
+                to_at = s * D + (2 * y + c) * part_w
+                qkv[:, to_at : to_at + part_w] = into[:, s * part_w : (s + 1) * part_w]
+    fc2[...] = t2[0].astype(f32) + t2[1].astype(f32)
+    out[...] = to[0].astype(f32) + to[1].astype(f32)
+
+
+def assemble(np_, t1, tq, t2, to):
+    r_in = t1.shape[1]
+    vmem = pl.BlockSpec(memory_space=pltpu.VMEM)
+    return pl.pallas_call(
+        functools.partial(assemble_kernel, np_),
+        out_shape=(
+            sds((r_in, t1.shape[2] * 4), f32), sds((r_in, tq.shape[2] * 4), f32),
+            sds(t2.shape[1:], f32), sds(to.shape[1:], f32),
+        ),
+        in_specs=[vmem] * 4,
+        out_specs=(vmem,) * 4,
+        name="assemble",
+    )(t1, tq, t2, to)
 
 
 def swap_sems(np_, n):
@@ -501,7 +563,7 @@
 
 MESH = pl.DeviceIdType.MESH
 AX = ("dp", "ctx")
-CHUNKS = 2
+CHUNKS = 4
 
 
 def place():
@@ -655,7 +717,7 @@
 
     def second(self, s, o):
         d, z, c, pair, g, y = self.here
-        out = self.sliced[s][1] if s < len(self.sliced) else self.w2[1]
+        out = self.sliced[s][1]
         return rcopy(
             out.at[pair], out.at[pair], self.ss.at[s, 7 + o - 1], self.rs.at[s, 7 + o - 1],
             (2 * lax.rem(pair + o, self.np_) + c, z),
@@ -667,19 +729,19 @@
         for s in range(n):
             for o in range(8):
                 self.first(s, o).start()
-        if self.w2 is not None:
-            for o in range(2):
-                self.w2_first(o).start()
-        if self.wo is not None:
-            self.wo_first(lambda cp: cp.start())
+
+    def start_rows(self):
+        for o in range(2):
+            self.w2_first(o).start()
+        self.wo_first(lambda cp: cp.start())
 
     def w2_first(self, o):
         d, z, c, pair, g, y = self.here
         src, out = self.w2
         n = len(self.sliced)
         if o == 0:
-            return pltpu.make_async_copy(src, out.at[pair, g], self.ls.at[n])
-        return rcopy(src, out.at[pair, g], self.ss.at[n, 0], self.rs.at[n, 0], (d, 3 - z))
+            return pltpu.make_async_copy(src, out.at[g], self.ls.at[n])
+        return rcopy(src, out.at[g], self.ss.at[n, 0], self.rs.at[n, 0], (d, 3 - z))
 
     def wo_parts(self):
         d, z, c, pair, g, y = self.here
@@ -708,17 +770,6 @@
                 )
                 do(cp)
 
-    def wo_second(self, o):
-        d, z, c, pair, g, y = self.here
-        per = self.np_ // 4
-        out = self.wo[1]
-        n = len(self.sliced) + 1
-        slot = out.at[lax.rem(pair, per)]
-        return rcopy(
-            slot, slot, self.ss.at[n, 8 + o - 1], self.rs.at[n, 8 + o - 1],
-            (2 * lax.rem(pair + o, self.np_) + c, z),
-        )
-
     def between(self, s):
         self.first(s, 0).wait()
         for o in range(1, 8):
@@ -726,17 +777,12 @@
         for o in range(1, self.np_):
             self.second(s, o).start()
 
-    def between_w2(self):
-        n = len(self.sliced)
-        self.w2_first(0).wait()
-        self.w2_first(1).wait_recv()
-        for o in range(1, self.np_):
-            self.second(n, o).start()
-
-    def between_wo(self):
+    def finish_rows(self):
         d, z, c, pair, g, y = self.here
         n = len(self.sliced) + 1
         per, owner, c_to, y_to = self.wo_parts()
+        for o in range(2):
+            self.w2_first(o).wait()
 
         @pl.when(owner == 2 * y + c)
         def _():
@@ -748,13 +794,22 @@
                     def _():
                         slot = self.wo[1].at[0, c2, z2]
                         rcopy(
-                            slot, slot, self.ss.at[n, 0], self.rs.at[n, c2 * 4 + z2], (d + 1 - 2 * c, z)
+                            slot, slot, self.ss.at[n, 0], self.rs.at[n, c2 * 4 + z2],
+                            (d + 1 - 2 * c, z),
                         ).wait_recv()
             pltpu.make_async_copy(
                 self.wo[0], self.wo[1].at[0, c, z], self.ls.at[n]
             ).wait()
-            for o in range(1, self.np_):
-                self.wo_second(o).start()
+
+        for t in range(2):
+            z_to = jnp.where(t == 0, y_to, 3 - y_to)
+
+            @pl.when(jnp.logical_not(jnp.logical_and(c == c_to, z == z_to)))
+            def _():
+                rcopy(
+                    self.wo[0], self.wo[1].at[0, c, z], self.ss.at[n, t], self.rs.at[n, 0],
+                    (d + 1 - 2 * c, z),
+                ).wait_send()
 
     def finish(self, s):
         for o in range(1, 8):
@@ -762,36 +817,59 @@
         for o in range(1, self.np_):
             self.second(s, o).wait()
 
-    def finish_w2(self):
-        n = len(self.sliced)
-        self.w2_first(1).wait_send()
-        for o in range(1, self.np_):
-            self.second(n, o).wait()
-
-    def finish_wo(self):
+
+class Rows:
+    def __init__(self, np_, w2, wo, ls, ss, rs):
+        self.np_, self.w2, self.wo, self.ls, self.ss, self.rs = np_, w2, wo, ls, ss, rs
+        self.here = place()
+
+    def copy_w2(self, o):
         d, z, c, pair, g, y = self.here
-        n = len(self.sliced) + 1
-        per, owner, c_to, y_to = self.wo_parts()
-        for t in range(2):
-            z_to = jnp.where(t == 0, y_to, 3 - y_to)
-
-            @pl.when(jnp.logical_not(jnp.logical_and(c == c_to, z == z_to)))
-            def _():
-                rcopy(
-                    self.wo[0], self.wo[1].at[0, c, z], self.ss.at[n, t], self.rs.at[n, 0], (d + 1 - 2 * c, z)
-                ).wait_send()
-
-        @pl.when(owner == 2 * y + c)
+        src, out = self.w2
+        if o == 0:
+            return pltpu.make_async_copy(src, out.at[pair], self.ls.at[0])
+        to = (2 * lax.rem(pair + o, self.np_) + c, z)
+        return rcopy(src, out.at[pair], self.ss.at[0, o], self.rs.at[0, o], to)
+
+    def copy_wo(self, o):
+        d, z, c, pair, g, y = self.here
+        src, out = self.wo
+        slot = lax.rem(pair, self.np_ // 4)
+        if o == 0:
+            return pltpu.make_async_copy(src.at[slot], out.at[slot], self.ls.at[1])
+        to = (2 * lax.rem(pair + o, self.np_) + c, z)
+        return rcopy(src.at[slot], out.at[slot], self.ss.at[1, o], self.rs.at[1, o], to)
+
+    def holds(self, pair):
+        d, z, c, unused, g, y = self.here
+        return lax.div(pair, self.np_ // 4) == 2 * y + c
+
+    def start(self):
+        @pl.when(self.holds(self.here[3]))
         def _():
             for o in range(1, self.np_):
-                self.wo_second(o).wait_send()
+                self.copy_wo(o).start()
+            self.copy_wo(0).start()
 
         for o in range(1, self.np_):
-            source = lax.div(lax.rem(pair + self.np_ - o, self.np_), per)
-
-            @pl.when(source == 2 * y + c)
+            self.copy_w2(o).start()
+        self.copy_w2(0).start()
+
+    def finish(self):
+        pair = self.here[3]
+        for o in range(self.np_):
+            self.copy_w2(o).wait()
+
+        @pl.when(self.holds(pair))
+        def _():
+            self.copy_wo(0).wait()
+            for o in range(1, self.np_):
+                self.copy_wo(o).wait_send()
+
+        for o in range(1, self.np_):
+            @pl.when(self.holds(lax.rem(pair + self.np_ - o, self.np_)))
             def _():
-                self.wo_second(o).wait_recv()
+                self.copy_wo(o).wait_recv()
 
 
 def decode_tables(np_, r_in, r_ff, part, nh):
@@ -853,27 +931,30 @@
 
 
 def gather_kernel(
-    np_, r_in, r_ff, x, wq, w1, vec_own, by_d, by_q, extra,
-    xg, wqg, w1g, tab, b_pad, length, vec, ls_x, ss_x, rs_x, ls_w, ss_w, rs_w,
+    np_, r_in, r_ff, x, wq, w1, w2, wo, vec_own, by_d, by_q, extra,
+    xg, wqg, w1g, w2p, wop, tab, b_pad, length, vec, ls_x, ss_x, rs_x, ls_w, ss_w, rs_w,
 ):
     d, z, c, pair, g, y = place()
     barrier_all(np_, d, z, c, pair)
     spread = Spread(x, xg, ls_x, ss_x, rs_x)
     weights = Weights(
-        np_, [(vec_own, vec, False), (wq, wqg, True), (w1, w1g, True)], None, None,
+        np_, [(vec_own, vec, False), (wq, wqg, True), (w1, w1g, True)], (w2, w2p), (wo, wop),
         ls_w, ss_w, rs_w,
     )
     weights.start()
     spread.start()
+    weights.start_rows()
     for s in range(3):
         weights.between(s)
     spread.forward(0)
     weights.finish(0)
     decode(np_, r_in, r_ff, vec, by_d, by_q, extra, tab, b_pad, length)
-    spread.forward(1)
+    for j in range(1, CHUNKS):
+        spread.forward(j)
     spread.finish()
     for s in range(1, 3):
         weights.finish(s)
+    weights.finish_rows()
 
 
 def spread_sems():
@@ -884,7 +965,7 @@
     ]
 
 
-def gather(np_, r_in, r_ff, nh, x, wq, w1, vec, collective_id=1):
+def gather(np_, r_in, r_ff, nh, x, wq, w1, w2, wo, vec, collective_id=1):
     any_ = pl.BlockSpec(memory_space=pl.ANY)
     vmem = pl.BlockSpec(memory_space=pltpu.VMEM)
     wide = 3 * nh * PAD
@@ -892,18 +973,19 @@
         functools.partial(gather_kernel, np_, r_in, r_ff),
         out_shape=(
             sds((4,) + x.shape, bf16), sds((np_, 2, 4) + wq.shape[1:], bf16),
-            sds((np_, 2, 4) + w1.shape[1:], bf16),
+            sds((np_, 2, 4) + w1.shape[1:], bf16), sds((2,) + w2.shape, bf16),
+            sds((np_ // 4, 2, 4) + wo.shape, bf16),
             sds((8, D), f32), sds((1, wide), f32), sds((1, PAD), f32),
         ),
-        in_specs=[any_] * 4 + [vmem] * 3,
-        out_specs=(any_,) * 3 + (vmem,) * 3,
+        in_specs=[any_] * 6 + [vmem] * 3,
+        out_specs=(any_,) * 5 + (vmem,) * 3,
         scratch_shapes=[pltpu.VMEM((np_, 2, 4, 16, PAD), bf16)] + spread_sems()
-        + weight_sems(np_, 3),
+        + weight_sems(np_, 5),
         compiler_params=pltpu.CompilerParams(
             collective_id=collective_id, has_side_effects=True, vmem_limit_bytes=VMEM_BYTES
         ),
         name="gather",
-    )(x, wq, w1, vec, *decode_tables(np_, r_in, r_ff, wq.shape[2] // 3, nh))
+    )(x, wq, w1, w2, wo, vec, *decode_tables(np_, r_in, r_ff, wq.shape[2] // 3, nh))
 
 
 PIECES = 4
@@ -1244,16 +1326,16 @@
 
 def finish_all(
     np_, r_in, r_ff, part_w, red_out, red, swap1, back,
-    dw, dwo, sums, hot_ref, qkv_at, t1, tq, t2, to, pieces,
+    dw, sums, hot_ref, qkv_at, t1, tq, t2, to, pieces,
     ls_w, ss_w, rs_w, sums_all, ls_g, ss_g, rs_g,
     b1, bq, b2, bo, s1, sq, s2, so, msg, m_all, p_out, ls, ss_m, rs_m, ss, rs,
 ):
     d, z, c, pair, g, y = place()
     grp = Group(sums, sums_all, ls_g, ss_g, rs_g)
-    swap = Swap(np_, [(dw, bq)], (dwo, bo), ls_w, ss_w, rs_w)
+    swap = Swap(np_, [(dw, bq)], None, ls_w, ss_w, rs_w)
     grp.start()
     swap.start()
-    red.pull(3, back)
+    red.ready(mirror(0, g))
     grp.finish()
     pieces_of(np_, sums_all, sums, hot_ref, qkv_at, r_in, r_ff, part_w, msg)
     me = pair * 2 + g
@@ -1266,8 +1348,8 @@
     own.start()
     for e in range(1, 2 * np_):
         tell(e).start()
-    red.pull(2, back)
-    red.pull(1, back)
+    red.push(mirror(0, g))
+    red.pull(mirror(1, g), back)
     own.wait()
     for e in range(1, 2 * np_):
         tell(e).wait()
@@ -1281,7 +1363,7 @@
     ]
     final = pltpu.make_async_copy(p_out, pieces, ls.at[9])
     final.start()
-    collects = swap.collects(pair)
+    collects = swap1.collects(pair)
     swap1.finish()
 
     def rows_to(s, src, dst, o, slot):
@@ -1331,7 +1413,7 @@
         for o in range(8):
             wo_to(o).start()
 
-    red.pull(0, back)
+    red.pull(mirror(0, g), back)
     for n, (acc, dst) in enumerate(((sq, tq), (s1, t1))):
         for o in range(8):
             rows_to(n, acc, dst, o, c * 4 + z).wait()
@@ -1391,33 +1473,26 @@
             packed = packed + jnp.pad(one, (start, 16 * PAD - start - one.shape[0]))
             start += one.shape[0]
         at += PAD
-    xq, w_qkv, w1, tab, b_pad, length = gather(
-        np_, r_in, r_ff, nh, x_own, w_qkv, w1, packed.reshape(16, PAD)
+    xq, w_qkv, w1, w2, wo, tab, b_pad, length = gather(
+        np_, r_in, r_ff, nh, x_own, w_qkv, w1, fc2_weight, out_weight, packed.reshape(16, PAD)
     )
     x = xq.reshape(t, D)
     w_qkv, w1 = w_qkv.reshape(D, 3 * part), w1.reshape(D, ff)
     cosine, sine = tables(t)
     q, k, v, cf, ctx, dyq, w2, wo = attn_fwd(
-        np_, length, x, tab, w_qkv, b_pad, cosine, sine, dy_own, fc2_weight, out_weight, nh, rows
+        np_, length, x, tab, w_qkv, b_pad, cosine, sine, dy_own, w2, wo, nh, rows
     )
-    dy = dyq.reshape(t, D)
     w2, wo = w2.reshape(ff, D), wo.reshape(part, D)
-    out_part, u_mlp, dw1, dw2, vec = mlp(x, dy, ctx, tab, wo, w1, w2, rows // 2)
+    out_part, u_mlp, dc, dw1, dw2, dwo, vec = mlp(
+        x, dyq.reshape(t, D), ctx, cf, tab, wo, w1, w2, rows
+    )
+    per = np_ // 4
     block_out, input_grad, t1, tq, t2, to, mine = attn_bwd(
-        np_, r_in, r_ff, x, dy, cf, ctx, u_mlp, q, k, v, tab, w_qkv, wo, cosine, sine, vec,
+        np_, r_in, r_ff, x, u_mlp, q, k, v, dc, tab, w_qkv, cosine, sine, vec,
         out_part.reshape(4, local_rows, D), xq, dyq, dw1.reshape(np_, D // np_, ff),
-        dw2.reshape(np_, 2 * r_ff, D), rows,
+        dw2.reshape(np_, 2 * r_ff, D), dwo.reshape(per, part // per, D),
     )
-    t1 = t1.reshape(2, tp, r_in, ff).astype(f32)
-    t1 = jnp.stack([t1[:, 0] + t1[:, 3], t1[:, 1] + t1[:, 2]], axis=1)
-    t1 = t1.reshape(2, 2, r_in, np_, 2, r_ff)
-    t1 = jnp.stack([t1[:, s, :, :, e] for s, e in ((0, 0), (1, 0), (1, 1), (0, 1))], axis=0)
-    g_fc1 = t1.transpose(2, 3, 1, 0, 4).reshape(r_in, ff * tp)
-    tq = tq.reshape(2, tp, r_in, 3, part).astype(f32)
-    tq = jnp.stack([tq[:, 0] + tq[:, 3], tq[:, 1] + tq[:, 2]], axis=0)
-    g_qkv = tq.reshape(tp, r_in, 3, part).transpose(1, 2, 0, 3).reshape(r_in, 3 * D)
-    g_fc2 = jnp.sum(t2.astype(f32), axis=0)
-    g_out = jnp.sum(to.astype(f32), axis=0)
+    g_fc1, g_qkv, g_fc2, g_out = assemble(np_, t1, tq, t2, to)
     cut = [mine[0, s * r_in : (s + 1) * r_in] for s in range(5)]
     return (
         block_out[None], input_grad[None],

time: 259 us -> 238 us (0.919); the launches traced: 259 us -> 234 us
  Pallas kernels: 234 us -> 217 us
  other arithmetic: 7.85 us -> 2.89 us
    pallas_call x1, Pallas kernels: 105 us -> 90.1 us  [attn_bwd(): pl.pallas_call(functools.partial(attn_bwd_kernel, np_, r_in, r_ff), grid=...]
    pallas_call x1, Pallas kernels: 48.7 us -> 40.6 us  [attn_fwd(): pl.pallas_call(functools.partial(attn_fwd_kernel, np_), grid=(t // rows,)...]
    pallas_call x1, Pallas kernels: 52.1 us -> 56.6 us  [gather(): pl.pallas_call(functools.partial(gather_kernel, np_, r_in, r_ff), out_sha...]
    reduce_sum x2 -> x0, other arithmetic: 3.28 us -> none  [the longest x1 1.74 us: local(): g_fc2 = jnp.sum(t2.astype(f32), axis=0)]
where the time goes in v4:
time: 238 us; the launch traced here: 234 us
  Pallas kernels  217 us (91%)
  local copies, waits for them, and re-layouts  13 us (5%)
  other arithmetic  2.89 us (1%)
    pallas_call x1, Pallas kernels, attn_bwd(): pl.pallas_call(functools.partial(attn_bwd_kernel, np_, r_in, r_ff), grid=...  90.1 us
    pallas_call x1, Pallas kernels, gather(): pl.pallas_call(functools.partial(gather_kernel, np_, r_in, r_ff), out_sha...  56.6 us
    pallas_call x1, Pallas kernels, attn_fwd(): pl.pallas_call(functools.partial(attn_fwd_kernel, np_), grid=(t // rows,)...  40.6 us
    pallas_call x1, Pallas kernels, mlp(): pl.pallas_call(mlp_kernel, grid=(t // rows,), out_shape=(sds((t, D), bf16...  27 us

profile of v4, /device:TPU:1, one launch (start us, length us, event | category | flops | bytes accessed | tf_op | source)
XLA Modules:
  0.0 234.0 jit_solution(11161052690301418726)
XLA Ops:
  1.3 1.5 fusion.5.vec_own
  2.8 1.1 reshape.83
  3.9 0.1 copy.44
  4.0 0.8 reshape.84.wq
  4.8 1.1 reshape.85
  5.9 0.1 slice.48
  6.0 0.1 fusion.6
  6.2 0.4 pad_maximum_fusion
  6.6 0.1 copy.41
  6.7 0.2 copy.42
  6.8 0.8 reshape.87.w1
  7.7 1.0 bitcast_select_fusion.dy
  8.7 56.6 %gather.1 = (bf16[4,512,768]{2,1,0:T(8,128)(2,1)}, bf16[4,2,4,24,576]{4,3,2,1,0:T(8,128)(2,1)}, bf16[4,2,4,24,768]{4,3,2,1,0:T(8,128)(2,1)}, bf16[2,96,768]{2,1,...) custom-call(bf16[512,768]{1,0:T(8,128)(2,1)} %bitcast.57, ...), custom_call_target="tpu_custom_call" | custom-call | tf_op jit(solution)/shard_map/gather/pallas_call | solution.py:972
  65.3 40.6 %attn_fwd.1 = (bf16[3,2048,128]{2,1,0:T(8,128)(2,1)}, bf16[3,2048,128]{2,1,0:T(8,128)(2,1)}, bf16[3,2048,128]{2,1,0:T(8,128)(2,1)}, f32[2048,384]{1,0:T(8,128)},...) custom-call(f32[1,128]{1,0:T(1,128)} %get-tuple-element.50.len_ref, ...), custom_call_target="tpu_custom_call" | custom-call | tf_op jit(solution)/shard_map/attn_fwd/pallas_call | solution.py:389
  106.0 27.0 %mlp.1 = (bf16[2048,768]{1,0:T(8,128)(2,1)}, f32[2048,768]{1,0:T(8,128)}, bf16[3,2048,128]{2,1,0:T(8,128)(2,1)}, bf16[768,768]{1,0:T(8,128)(2,1)}, bf16[768,768]...) custom-call(bf16[2048,768]{1,0:T(8,128)(2,1)} %bitcast.47, bf16[2048,768]{1,0:T(8,128)(2,1)} %bitcast.49, ...), custom_call_target="tpu_custom_call" | custom-call | tf_op jit(solution)/shard_map/mlp/pallas_call | solution.py:433
  133.0 90.1 %attn_bwd.1 = (bf16[512,768]{1,0:T(8,128)(2,1)}, bf16[512,768]{1,0:T(8,128)(2,1)}, bf16[8,24,768]{2,1,0:T(8,128)(2,1)}, bf16[8,24,576]{2,1,0:T(8,128)(2,1)}, bf1...) custom-call(bf16[2048,768]{1,0:T(8,128)(2,1)} %bitcast.48, ...), custom_call_target="tpu_custom_call" | custom-call | tf_op jit(solution)/shard_map/attn_bwd/pallas_call | solution.py:472
  223.1 1.3 slice.45
  224.4 1.2 slice_bitcast_fusion
  225.6 1.2 slice_bitcast_fusion.4
  226.8 1.5 slice_bitcast_fusion.1
  228.2 2.3 assemble.1
  230.5 0.5 copy.49
  231.0 2.1 copy.50
  233.1 0.9 copy.51
  (7 shorter events, 0.0 us)
Async XLA Ops:
  3.9 3.8 %copy-start = (bf16[1,512,768]{2,1,0:T(8,128)(2,1)S(1)}, bf16[1,512,768]{2,1,0:T(8,128)(2,1)}, u32[]{:S(2)}) copy-start(bf16[1,512,768]{2,1,0:T(8,128)(2,1)} %param.23) | copy-start | bytes 2359300
  223.1 10.0 %copy-start.1 = (bf16[512,768]{1,0:T(8,128)(2,1)S(1)}, bf16[512,768]{1,0:T(8,128)(2,1)}, u32[]{:S(2)}) copy-start(bf16[512,768]{1,0:T(8,128)(2,1)} %get-tuple-element.73) | copy-start | bytes 2359300
  228.2 5.7 %copy-start.2 = (f32[24]{0:T(128)}, f32[24]{0:T(128)S(1)}, u32[]{:S(2)}) copy-start(f32[24]{0:T(128)S(1)} %get-tuple-element.142) | copy-start | bytes 292

commit v5 on v4

--- a/solution.py
+++ b/solution.py
@@ -506,9 +506,20 @@
     )
 
 
-def assemble_kernel(np_, t1, tq, t2, to, fc1, qkv, fc2, out):
-    r_ff = t2.shape[1]
+def assemble_kernel(
+    np_, out_in, grad_in, t1, tq, t2, to, pieces,
+    out_o, grad_o, g1, b1, qkv, qkv_b, out, out_b, g2, b2, fc1, fc1_b, fc2, fc2_b, norm,
+):
+    r_ff, r_in = t2.shape[1], t1.shape[1]
     part_w = tq.shape[2] // 3
+    out_o[...] = out_in[...]
+    grad_o[...] = grad_in[...]
+    for s, ref in enumerate((g1, b1, g2, b2, out_b)):
+        ref[...] = pieces[0, s * r_in : (s + 1) * r_in]
+    fc2_b[...] = pieces[0, 4 * r_in : 5 * r_in]
+    qkv_b[...] = pieces[1, : 3 * r_in]
+    fc1_b[...] = pieces[2, :r_ff]
+    norm[...] = pieces[4, :1]
     for c in range(2):
         for y in range(2):
             a, b = (0, 3) if y == 0 else (1, 2)
@@ -526,19 +537,23 @@
     out[...] = to[0].astype(f32) + to[1].astype(f32)
 
 
-def assemble(np_, t1, tq, t2, to):
-    r_in = t1.shape[1]
+def assemble(np_, out, grad, t1, tq, t2, to, pieces):
+    r_in, r_ff = t1.shape[1], t2.shape[1]
     vmem = pl.BlockSpec(memory_space=pltpu.VMEM)
+    vec = sds((r_in,), f32)
+    outs = (
+        sds(out.shape, bf16), sds(grad.shape, bf16), vec, vec,
+        sds((r_in, tq.shape[2] * 4), f32), sds((3 * r_in,), f32), sds(to.shape[1:], f32), vec,
+        vec, vec, sds((r_in, t1.shape[2] * 4), f32), sds((r_ff,), f32), sds(t2.shape[1:], f32),
+        vec, sds((1,), f32),
+    )
     return pl.pallas_call(
         functools.partial(assemble_kernel, np_),
-        out_shape=(
-            sds((r_in, t1.shape[2] * 4), f32), sds((r_in, tq.shape[2] * 4), f32),
-            sds(t2.shape[1:], f32), sds(to.shape[1:], f32),
-        ),
-        in_specs=[vmem] * 4,
-        out_specs=(vmem,) * 4,
+        out_shape=outs,
+        in_specs=[vmem] * 7,
+        out_specs=(vmem,) * len(outs),
         name="assemble",
-    )(t1, tq, t2, to)
+    )(out, grad, t1, tq, t2, to, pieces)
 
 
 def swap_sems(np_, n):
@@ -931,10 +946,23 @@
 
 
 def gather_kernel(
-    np_, r_in, r_ff, x, wq, w1, w2, wo, vec_own, by_d, by_q, extra,
-    xg, wqg, w1g, w2p, wop, tab, b_pad, length, vec, ls_x, ss_x, rs_x, ls_w, ss_w, rs_w,
+    np_, r_in, r_ff, len_ref, x, grad, qkv_w, fc1_w, w2, wo, vec_own, by_d, by_q, extra,
+    xg, dy_own, wqg, w1g, w2p, wop, tab, b_pad, length, wq, w1, dy, ls_m, vec, ls_x, ss_x, rs_x, ls_w, ss_w, rs_w,
 ):
     d, z, c, pair, g, y = place()
+    load = pltpu.make_async_copy(grad, dy, ls_m.at[0])
+    load.start()
+    part_w = wq.shape[2] // 3
+    for k in range(4):
+        y2, c2 = k // 2, k % 2
+        for s in range(3):
+            at = s * D + k * part_w
+            wq[k, :, s * part_w : (s + 1) * part_w] = qkv_w[:, at : at + part_w]
+        for n in range(np_):
+            for e, z2 in enumerate((0, 3) if y2 == 0 else (1, 2)):
+                at = r_ff * (4 * (2 * n + c2) + z2)
+                to = r_ff * (2 * n + e)
+                w1[k, :, to : to + r_ff] = fc1_w[:, at : at + r_ff]
     barrier_all(np_, d, z, c, pair)
     spread = Spread(x, xg, ls_x, ss_x, rs_x)
     weights = Weights(
@@ -944,6 +972,11 @@
     weights.start()
     spread.start()
     weights.start_rows()
+    load.wait()
+    pos = z * dy.shape[0] + lax.broadcasted_iota(jnp.int32, (dy.shape[0], 1), 0)
+    dy[...] = jnp.where(pos < len_ref[0], dy[...].astype(f32), 0.0).astype(bf16)
+    store = pltpu.make_async_copy(dy, dy_own, ls_m.at[1])
+    store.start()
     for s in range(3):
         weights.between(s)
     spread.forward(0)
@@ -955,6 +988,7 @@
     for s in range(1, 3):
         weights.finish(s)
     weights.finish_rows()
+    store.wait()
 
 
 def spread_sems():
@@ -965,27 +999,34 @@
     ]
 
 
-def gather(np_, r_in, r_ff, nh, x, wq, w1, w2, wo, vec, collective_id=1):
+def gather(
+    np_, r_in, r_ff, nh, length, x, grad, qkv_w, fc1_w, w2, wo, vec, collective_id=1
+):
     any_ = pl.BlockSpec(memory_space=pl.ANY)
     vmem = pl.BlockSpec(memory_space=pltpu.VMEM)
     wide = 3 * nh * PAD
+    thin, ff = qkv_w.shape[1] // 4, fc1_w.shape[1] // 4
     return pl.pallas_call(
         functools.partial(gather_kernel, np_, r_in, r_ff),
         out_shape=(
-            sds((4,) + x.shape, bf16), sds((np_, 2, 4) + wq.shape[1:], bf16),
-            sds((np_, 2, 4) + w1.shape[1:], bf16), sds((2,) + w2.shape, bf16),
+            sds((4,) + x.shape, bf16), sds(x.shape, bf16), sds((np_, 2, 4, r_in, thin), bf16),
+            sds((np_, 2, 4, r_in, ff), bf16), sds((2,) + w2.shape, bf16),
             sds((np_ // 4, 2, 4) + wo.shape, bf16),
             sds((8, D), f32), sds((1, wide), f32), sds((1, PAD), f32),
         ),
-        in_specs=[any_] * 6 + [vmem] * 3,
-        out_specs=(any_,) * 5 + (vmem,) * 3,
-        scratch_shapes=[pltpu.VMEM((np_, 2, 4, 16, PAD), bf16)] + spread_sems()
-        + weight_sems(np_, 5),
+        in_specs=[pl.BlockSpec(memory_space=pltpu.SMEM), any_, any_, vmem, vmem, any_, any_, any_]
+        + [vmem] * 3,
+        out_specs=(any_,) * 6 + (vmem,) * 3,
+        scratch_shapes=[
+            pltpu.VMEM((4, r_in, thin), bf16), pltpu.VMEM((4, r_in, ff), bf16),
+            pltpu.VMEM(x.shape, bf16), pltpu.SemaphoreType.DMA((2,)),
+            pltpu.VMEM((np_, 2, 4, 16, PAD), bf16),
+        ] + spread_sems() + weight_sems(np_, 5),
         compiler_params=pltpu.CompilerParams(
             collective_id=collective_id, has_side_effects=True, vmem_limit_bytes=VMEM_BYTES
         ),
         name="gather",
-    )(x, wq, w1, w2, wo, vec, *decode_tables(np_, r_in, r_ff, wq.shape[2] // 3, nh))
+    )(length, x, grad, qkv_w, fc1_w, w2, wo, vec, *decode_tables(np_, r_in, r_ff, thin // 3, nh))
 
 
 PIECES = 4
@@ -1444,7 +1485,6 @@
     dp = lax.axis_size("dp")
     np_ = dp // 2
     world = dp * tp
-    d, z, c, pair, g, y = place()
     nh = HEADS // tp
     local_rows = block_in.shape[1]
     t = local_rows * tp
@@ -1454,14 +1494,6 @@
     r_ff = fc2_weight.shape[0]
     ff = r_ff * dp
 
-    x_own = block_in[0]
-    pos = z * local_rows + jnp.arange(local_rows, dtype=jnp.int32)
-    dy_own = jnp.where((pos < lengths[0])[:, None], out_grad[0], jnp.zeros((), bf16))
-
-    w_qkv = jnp.moveaxis(qkv_weight.reshape(r_in, 3, tp, part), 2, 0).reshape(tp, r_in, 3 * part)
-    w1 = fc1_weight.reshape(r_in, np_, 2, tp, r_ff)
-    w1 = jnp.stack([w1[:, :, :, s] for s in (0, 3, 1, 2)], axis=3)
-    w1 = w1.reshape(r_in, np_, 2, 2, 2, r_ff).transpose(3, 2, 0, 1, 4, 5).reshape(tp, r_in, ff)
     length_parts = jnp.stack([lengths[0] // 256, lengths[0] % 256]).astype(bf16)
     packed, at = jnp.zeros((16 * PAD,), bf16), 0
     for row_of in (
@@ -1473,8 +1505,9 @@
             packed = packed + jnp.pad(one, (start, 16 * PAD - start - one.shape[0]))
             start += one.shape[0]
         at += PAD
-    xq, w_qkv, w1, w2, wo, tab, b_pad, length = gather(
-        np_, r_in, r_ff, nh, x_own, w_qkv, w1, fc2_weight, out_weight, packed.reshape(16, PAD)
+    xq, dy_own, w_qkv, w1, w2, wo, tab, b_pad, length = gather(
+        np_, r_in, r_ff, nh, lengths, block_in[0], out_grad[0], qkv_weight, fc1_weight, fc2_weight,
+        out_weight, packed.reshape(16, PAD),
     )
     x = xq.reshape(t, D)
     w_qkv, w1 = w_qkv.reshape(D, 3 * part), w1.reshape(D, ff)
@@ -1492,14 +1525,8 @@
         out_part.reshape(4, local_rows, D), xq, dyq, dw1.reshape(np_, D // np_, ff),
         dw2.reshape(np_, 2 * r_ff, D), dwo.reshape(per, part // per, D),
     )
-    g_fc1, g_qkv, g_fc2, g_out = assemble(np_, t1, tq, t2, to)
-    cut = [mine[0, s * r_in : (s + 1) * r_in] for s in range(5)]
-    return (
-        block_out[None], input_grad[None],
-        cut[0], cut[1], g_qkv, mine[1, : 3 * r_in], g_out, cut[4],
-        cut[2], cut[3], g_fc1, mine[2, :r_ff], g_fc2, cut[4],
-        mine[4, :1],
-    )
+    outs = assemble(np_, block_out, input_grad, t1, tq, t2, to, mine)
+    return (outs[0][None], outs[1][None]) + tuple(outs[2:])
 
 
 def solution(mesh):

time: 238 us -> 225 us (0.945)
  local copies, waits for them, and re-layouts: 13 us -> 0 us
    reshape x5 -> x0, local copies, waits for them, and re-layouts: 3.92 us -> none  [the longest x2 1.14 us: local(): qkv_weight.reshape(r_in, 3, tp, part)]
    squeeze x3 -> x0, local copies, waits for them, and re-layouts: 3.85 us -> none  [the longest x1 1.46 us: local(): cut = [mine[0, s * r_in:(s + 1) * r_in] for s in range(5)]]
    unnamed x9 -> x0, local copies, waits for them, and re-layouts: 3.47 us -> none
where the time goes in v5:
time: 225 us; the launch traced here: 221 us
  Pallas kernels  218 us (97%)
    pallas_call x1, Pallas kernels, attn_bwd(): pl.pallas_call(functools.partial(attn_bwd_kernel, np_, r_in, r_ff), grid=...  90.1 us
    pallas_call x1, Pallas kernels, gather(): pl.pallas_call(functools.partial(gather_kernel, np_, r_in, r_ff), out_sha...  57.1 us
    pallas_call x1, Pallas kernels, attn_fwd(): pl.pallas_call(functools.partial(attn_fwd_kernel, np_), grid=(t // rows,)...  40.5 us
    pallas_call x1, Pallas kernels, mlp(): pl.pallas_call(mlp_kernel, grid=(t // rows,), out_shape=(sds((t, D), bf16...  27 us

profile of v5, /device:TPU:1, one launch (start us, length us, event | category | flops | bytes accessed | tf_op | source)
XLA Modules:
  0.0 221.0 jit_solution(3151624992006338022)
XLA Ops:
  1.3 1.5 fusion.5.vec_own
  2.8 57.1 %gather.1 = (bf16[4,512,768]{2,1,0:T(8,128)(2,1)}, bf16[512,768]{1,0:T(8,128)(2,1)}, bf16[4,2,4,24,576]{4,3,2,1,0:T(8,128)(2,1)}, bf16[4,2,4,24,768]{4,3,2,1,0:T...) custom-call(s32[1]{0:T(128)} %copy.37.len_ref, ...), custom_call_target="tpu_custom_call" | custom-call | tf_op jit(solution)/shard_map/gather/pallas_call | solution.py:1009
  59.9 40.5 %attn_fwd.1 = (bf16[3,2048,128]{2,1,0:T(8,128)(2,1)}, bf16[3,2048,128]{2,1,0:T(8,128)(2,1)}, bf16[3,2048,128]{2,1,0:T(8,128)(2,1)}, f32[2048,384]{1,0:T(8,128)},...) custom-call(f32[1,128]{1,0:T(1,128)} %get-tuple-element.62.len_ref, ...), custom_call_target="tpu_custom_call" | custom-call | tf_op jit(solution)/shard_map/attn_fwd/pallas_call | solution.py:389
  100.5 27.0 %mlp.1 = (bf16[2048,768]{1,0:T(8,128)(2,1)}, f32[2048,768]{1,0:T(8,128)}, bf16[3,2048,128]{2,1,0:T(8,128)(2,1)}, bf16[768,768]{1,0:T(8,128)(2,1)}, bf16[768,768]...) custom-call(bf16[2048,768]{1,0:T(8,128)(2,1)} %bitcast.24, bf16[2048,768]{1,0:T(8,128)(2,1)} %bitcast.26, ...), custom_call_target="tpu_custom_call" | custom-call | tf_op jit(solution)/shard_map/mlp/pallas_call | solution.py:433
  127.5 90.1 %attn_bwd.1 = (bf16[512,768]{1,0:T(8,128)(2,1)}, bf16[512,768]{1,0:T(8,128)(2,1)}, bf16[8,24,768]{2,1,0:T(8,128)(2,1)}, bf16[8,24,576]{2,1,0:T(8,128)(2,1)}, bf1...) custom-call(bf16[2048,768]{1,0:T(8,128)(2,1)} %bitcast.25, ...), custom_call_target="tpu_custom_call" | custom-call | tf_op jit(solution)/shard_map/attn_bwd/pallas_call | solution.py:472
  217.6 3.3 %assemble.1 = (bf16[512,768]{1,0:T(8,128)(2,1)}, bf16[512,768]{1,0:T(8,128)(2,1)}, f32[24]{0:T(128)}, f32[24]{0:T(128)}, f32[24,2304]{1,0:T(8,128)}, /*index=5*/...) custom-call(bf16[512,768]{1,0:T(8,128)(2,1)} %get-tuple-element.85.o, ...), custom_call_target="tpu_custom_call" | custom-call | tf_op jit(solution)/shard_map/assemble/pallas_call | solution.py:550

commit v6 on v5

--- a/solution.py
+++ b/solution.py
@@ -275,6 +275,10 @@
         dw_scr[...] = jnp.zeros_like(dw_scr)
         vec_ref[...] = vec_in_ref[...]
 
+    @pl.when(step == 1)
+    def _():
+        red.add_far(lambda total, r: xq[r].astype(f32) + tab_ref[2:3] + total, (0, 1))
+
     causal = lax.broadcasted_iota(jnp.int32, (rows, rows), 0) <= lax.broadcasted_iota(
         jnp.int32, (rows, rows), 1
     )
@@ -294,11 +298,11 @@
             dk_scr[h, keys] += dot(dst, q)
             dq_scr[h, asks] += dot(dst, k, ((0,), (0,)))
 
+    @pl.when(step == 0)
+    def _():
+        red.add_near()
+
     block(b, b, True)
-
-    @pl.when(step == 0)
-    def _():
-        red.add_near()
 
     def off(n, carry):
         block(jnp.where(g == 0, b, b + 1 + n), jnp.where(g == 0, n, b), False)
@@ -308,8 +312,12 @@
 
     @pl.when(step == 1)
     def _():
-        red.add_far(lambda total, r: xq[r].astype(f32) + tab_ref[2:3] + total)
+        red.add_far(lambda total, r: xq[r].astype(f32) + tab_ref[2:3] + total, (2, 3))
         load_dy.wait()
+
+    @pl.when(step == 2)
+    def _():
+        red_u.pull(mirror(3, g), back)
 
     @pl.when(step == 3)
     def _():
@@ -341,19 +349,12 @@
     def _():
         red_u.push(b)
 
-    @pl.when(step == 2)
-    def _():
-        red_u.pull(mirror(3, g), back)
-
     @pl.when(step == blocks - 1)
     def _():
         vec_ref[7:8, 0:1] += squares_of(dw_scr[...])
-        share = D // np_
-        for n in range(np_):
-            dw[n] = dw_scr[n * share : (n + 1) * share].astype(bf16)
         finish_all(
             np_, r_in, r_ff, wide // 3, red, red_u, swap, back,
-            dw, vec_ref, hot_ref, qkv_at, t1, tq, t2, to, pieces,
+            dw, dw_scr, vec_ref, hot_ref, qkv_at, t1, tq, t2, to, pieces,
             ls_w, ss_w, rs_w, sums_all, ls_g, ss_g, rs_g,
             b1, bq, b2, bo, s1, sq, s2, so, msg, m_all, p_out, ls, ss_m, rs_m, ss, rs,
         )
@@ -977,13 +978,14 @@
     dy[...] = jnp.where(pos < len_ref[0], dy[...].astype(f32), 0.0).astype(bf16)
     store = pltpu.make_async_copy(dy, dy_own, ls_m.at[1])
     store.start()
-    for s in range(3):
+    for s in range(2):
         weights.between(s)
     spread.forward(0)
+    weights.between(2)
     weights.finish(0)
-    decode(np_, r_in, r_ff, vec, by_d, by_q, extra, tab, b_pad, length)
     for j in range(1, CHUNKS):
         spread.forward(j)
+    decode(np_, r_in, r_ff, vec, by_d, by_q, extra, tab, b_pad, length)
     spread.finish()
     for s in range(1, 3):
         weights.finish(s)
@@ -1105,8 +1107,8 @@
         for e in range(len(self.extra)):
             self.load_extra(e).wait()
 
-    def add_far(self, finish):
-        for j in range(PIECES):
+    def add_far(self, finish, pieces=range(PIECES)):
+        for j in pieces:
             r = self.rows_of(j)
             self.to_sib(1, j).wait_recv()
             self.across(j).wait_recv()
@@ -1367,7 +1369,7 @@
 
 def finish_all(
     np_, r_in, r_ff, part_w, red_out, red, swap1, back,
-    dw, sums, hot_ref, qkv_at, t1, tq, t2, to, pieces,
+    dw, dw_sum, sums, hot_ref, qkv_at, t1, tq, t2, to, pieces,
     ls_w, ss_w, rs_w, sums_all, ls_g, ss_g, rs_g,
     b1, bq, b2, bo, s1, sq, s2, so, msg, m_all, p_out, ls, ss_m, rs_m, ss, rs,
 ):
@@ -1375,6 +1377,9 @@
     grp = Group(sums, sums_all, ls_g, ss_g, rs_g)
     swap = Swap(np_, [(dw, bq)], None, ls_w, ss_w, rs_w)
     grp.start()
+    share = D // np_
+    for n in range(np_):
+        dw[n] = dw_sum[n * share : (n + 1) * share].astype(bf16)
     swap.start()
     red.ready(mirror(0, g))
     grp.finish()

time: 225 us -> 222 us (0.987)
  Pallas kernels: 218 us -> 215 us
    pallas_call x1, Pallas kernels: 90.1 us -> 87.1 us  [attn_bwd(): pl.pallas_call(functools.partial(attn_bwd_kernel, np_, r_in, r_ff), grid=...]
where the time goes in v6:
time: 222 us; the launch traced here: 218 us
  Pallas kernels  215 us (97%)
    pallas_call x1, Pallas kernels, attn_bwd(): pl.pallas_call(functools.partial(attn_bwd_kernel, np_, r_in, r_ff), grid=...  87.1 us
    pallas_call x1, Pallas kernels, gather(): pl.pallas_call(functools.partial(gather_kernel, np_, r_in, r_ff), out_sha...  57.1 us
    pallas_call x1, Pallas kernels, attn_fwd(): pl.pallas_call(functools.partial(attn_fwd_kernel, np_), grid=(t // rows,)...  40.5 us
    pallas_call x1, Pallas kernels, mlp(): pl.pallas_call(mlp_kernel, grid=(t // rows,), out_shape=(sds((t, D), bf16...  27 us

profile of v6, /device:TPU:1, one launch (start us, length us, event | category | flops | bytes accessed | tf_op | source)
XLA Modules:
  0.0 217.9 jit_solution(11682497899620399597)
XLA Ops:
  1.3 1.5 fusion.5.vec_own
  2.8 57.1 %gather.1 = (bf16[4,512,768]{2,1,0:T(8,128)(2,1)}, bf16[512,768]{1,0:T(8,128)(2,1)}, bf16[4,2,4,24,576]{4,3,2,1,0:T(8,128)(2,1)}, bf16[4,2,4,24,768]{4,3,2,1,0:T...) custom-call(s32[1]{0:T(128)} %copy.37.len_ref, ...), custom_call_target="tpu_custom_call" | custom-call | tf_op jit(solution)/shard_map/gather/pallas_call | solution.py:1011
  59.9 40.5 %attn_fwd.1 = (bf16[3,2048,128]{2,1,0:T(8,128)(2,1)}, bf16[3,2048,128]{2,1,0:T(8,128)(2,1)}, bf16[3,2048,128]{2,1,0:T(8,128)(2,1)}, f32[2048,384]{1,0:T(8,128)},...) custom-call(f32[1,128]{1,0:T(1,128)} %get-tuple-element.62.len_ref, ...), custom_call_target="tpu_custom_call" | custom-call | tf_op jit(solution)/shard_map/attn_fwd/pallas_call | solution.py:390
  100.5 27.0 %mlp.1 = (bf16[2048,768]{1,0:T(8,128)(2,1)}, f32[2048,768]{1,0:T(8,128)}, bf16[3,2048,128]{2,1,0:T(8,128)(2,1)}, bf16[768,768]{1,0:T(8,128)(2,1)}, bf16[768,768]...) custom-call(bf16[2048,768]{1,0:T(8,128)(2,1)} %bitcast.24, bf16[2048,768]{1,0:T(8,128)(2,1)} %bitcast.26, ...), custom_call_target="tpu_custom_call" | custom-call | tf_op jit(solution)/shard_map/mlp/pallas_call | solution.py:434
  127.5 87.1 %attn_bwd.1 = (bf16[512,768]{1,0:T(8,128)(2,1)}, bf16[512,768]{1,0:T(8,128)(2,1)}, bf16[8,24,768]{2,1,0:T(8,128)(2,1)}, bf16[8,24,576]{2,1,0:T(8,128)(2,1)}, bf1...) custom-call(bf16[2048,768]{1,0:T(8,128)(2,1)} %bitcast.25, ...), custom_call_target="tpu_custom_call" | custom-call | tf_op jit(solution)/shard_map/attn_bwd/pallas_call | solution.py:473
  214.6 3.3 %assemble.1 = (bf16[512,768]{1,0:T(8,128)(2,1)}, bf16[512,768]{1,0:T(8,128)(2,1)}, f32[24]{0:T(128)}, f32[24]{0:T(128)}, f32[24,2304]{1,0:T(8,128)}, /*index=5*/...) custom-call(bf16[512,768]{1,0:T(8,128)(2,1)} %get-tuple-element.85.o, ...), custom_call_target="tpu_custom_call" | custom-call | tf_op jit(solution)/shard_map/assemble/pallas_call | solution.py:551

commit v7 on v6

--- a/solution.py
+++ b/solution.py
@@ -277,7 +277,7 @@
 
     @pl.when(step == 1)
     def _():
-        red.add_far(lambda total, r: xq[r].astype(f32) + tab_ref[2:3] + total, (0, 1))
+        red.add_far(lambda total, r: xq[r].astype(f32) + tab_ref[2:3] + total, (0, 1, 2, 3))
 
     causal = lax.broadcasted_iota(jnp.int32, (rows, rows), 0) <= lax.broadcasted_iota(
         jnp.int32, (rows, rows), 1
@@ -312,7 +312,7 @@
 
     @pl.when(step == 1)
     def _():
-        red.add_far(lambda total, r: xq[r].astype(f32) + tab_ref[2:3] + total, (2, 3))
+        red.add_far(lambda total, r: xq[r].astype(f32) + tab_ref[2:3] + total, (4, 5, 6, 7))
         load_dy.wait()
 
     @pl.when(step == 2)
@@ -1031,7 +1031,7 @@
     )(length, x, grad, qkv_w, fc1_w, w2, wo, vec, *decode_tables(np_, r_in, r_ff, thin // 3, nh))
 
 
-PIECES = 4
+PIECES = 8
 
 
 class Reduce:

time: 222 us -> 222 us (level)
  no operation moved by 1% of the time
where the time goes in v7:
time: 222 us; the launch traced here: 218 us
  Pallas kernels  215 us (97%)
    pallas_call x1, Pallas kernels, attn_bwd(): pl.pallas_call(functools.partial(attn_bwd_kernel, np_, r_in, r_ff), grid=...  87.4 us
    pallas_call x1, Pallas kernels, gather(): pl.pallas_call(functools.partial(gather_kernel, np_, r_in, r_ff), out_sha...  57.1 us
    pallas_call x1, Pallas kernels, attn_fwd(): pl.pallas_call(functools.partial(attn_fwd_kernel, np_), grid=(t // rows,)...  40.5 us
    pallas_call x1, Pallas kernels, mlp(): pl.pallas_call(mlp_kernel, grid=(t // rows,), out_shape=(sds((t, D), bf16...  27 us

profile of v7, /device:TPU:1, one launch (start us, length us, event | category | flops | bytes accessed | tf_op | source)
XLA Modules:
  0.0 218.3 jit_solution(9365507656456009396)
XLA Ops:
  1.3 1.5 fusion.5.vec_own
  2.8 57.1 %gather.1 = (bf16[4,512,768]{2,1,0:T(8,128)(2,1)}, bf16[512,768]{1,0:T(8,128)(2,1)}, bf16[4,2,4,24,576]{4,3,2,1,0:T(8,128)(2,1)}, bf16[4,2,4,24,768]{4,3,2,1,0:T...) custom-call(s32[1]{0:T(128)} %copy.37.len_ref, ...), custom_call_target="tpu_custom_call" | custom-call | tf_op jit(solution)/shard_map/gather/pallas_call | solution.py:1011
  59.9 40.5 %attn_fwd.1 = (bf16[3,2048,128]{2,1,0:T(8,128)(2,1)}, bf16[3,2048,128]{2,1,0:T(8,128)(2,1)}, bf16[3,2048,128]{2,1,0:T(8,128)(2,1)}, f32[2048,384]{1,0:T(8,128)},...) custom-call(f32[1,128]{1,0:T(1,128)} %get-tuple-element.62.len_ref, ...), custom_call_target="tpu_custom_call" | custom-call | tf_op jit(solution)/shard_map/attn_fwd/pallas_call | solution.py:390
  100.5 27.0 %mlp.1 = (bf16[2048,768]{1,0:T(8,128)(2,1)}, f32[2048,768]{1,0:T(8,128)}, bf16[3,2048,128]{2,1,0:T(8,128)(2,1)}, bf16[768,768]{1,0:T(8,128)(2,1)}, bf16[768,768]...) custom-call(bf16[2048,768]{1,0:T(8,128)(2,1)} %bitcast.24, bf16[2048,768]{1,0:T(8,128)(2,1)} %bitcast.26, ...), custom_call_target="tpu_custom_call" | custom-call | tf_op jit(solution)/shard_map/mlp/pallas_call | solution.py:434
  127.5 87.4 %attn_bwd.1 = (bf16[512,768]{1,0:T(8,128)(2,1)}, bf16[512,768]{1,0:T(8,128)(2,1)}, bf16[8,24,768]{2,1,0:T(8,128)(2,1)}, bf16[8,24,576]{2,1,0:T(8,128)(2,1)}, bf1...) custom-call(bf16[2048,768]{1,0:T(8,128)(2,1)} %bitcast.25, ...), custom_call_target="tpu_custom_call" | custom-call | tf_op jit(solution)/shard_map/attn_bwd/pallas_call | solution.py:473
  214.9 3.3 %assemble.1 = (bf16[512,768]{1,0:T(8,128)(2,1)}, bf16[512,768]{1,0:T(8,128)(2,1)}, f32[24]{0:T(128)}, f32[24]{0:T(128)}, f32[24,2304]{1,0:T(8,128)}, /*index=5*/...) custom-call(bf16[512,768]{1,0:T(8,128)(2,1)} %get-tuple-element.85.o, ...), custom_call_target="tpu_custom_call" | custom-call | tf_op jit(solution)/shard_map/assemble/pallas_call | solution.py:551
